TPU v7x, 32 devices: a whole 2x2x4 slice. The times are simulated.
32 devices in a mesh: grp: 2 (over y), wide: 8 (over z, x), narrow: 2 (over core).
Axes of the slice: x: 2, y: 2, z: 4, core: 2. Of those that a mesh axis runs over, the one named last changes fastest.
Arguments:
- tile_hidden: bfloat16 [32, 64, 1024], P(('grp', 'wide')), parts along dimension 0, may hold values from -6 to 6
- cached_rows: bfloat16 [2048, 2048], P(('grp', 'wide'), 'narrow'), parts along dimension 0, may hold values from -5 to 5
- tile_image: int32 [32], P(('grp', 'wide')), parts along dimension 0, may hold values from 0 to 4095, as said below
- cache_ids: int32 [128], P('grp'), parts along dimension 0, may hold values from 0 to 4095, as said below
- adapter_weight: bfloat16 [1024, 2048], P('wide', 'narrow'), may hold values from -0.1875 to 0.1875
- routes: int32 [2048, 6], P(('grp', 'wide')), parts along dimension 0, may hold values from 0 to 63, all different within a row; in each aligned block of 128 rows (0 to 127, 128 to 255, ...) at most 16 rows name the same one
- route_gates: float32 [2048, 6], P(('grp', 'wide')), parts along dimension 0, may hold values from 0.03 to 0.4
- gate_up: bfloat16 [128, 2048, 2, 512], P('wide', 'narrow'), may hold values from -0.125 to 0.125
- expert_down: bfloat16 [128, 512, 2048], P('wide', None, 'narrow'), may hold values from -0.1875 to 0.1875
Outputs:
- expert_mix: bfloat16 [2048, 2048], P(('grp', 'wide'), 'narrow'), parts along dimension 0
There are 2 independent parts, one for each index of `grp`. A program takes and returns all parts, laid end to end along the dimension named above; an argument that names none is the same for every part. Nothing has to cross between parts.
Inputs may be any that keep to these rules, and one draw needn't show every extreme that they name: `tile_image`: slot s belongs to chip s // 2. A slot misses the cache when its image id is not in cache_ids. Chips w and w + 4 together have at most 2 missed slots, and in every draw some chip misses all 2 of its slots. `cache_ids`: the ids are distinct. `routes`: within the rows of one chip (128 tokens), no expert is named by more than 16 rows, and in every draw some expert is named by exactly 16 rows of some chip.
All inputs are finite; a program needn't handle non-finite values.
Results may differ from a plain program's by a relative error of at most 0.018.
Values may be sent and summed in bfloat16 or wider, within the bound.
No kernel may reach another device: no remote copies, remote signals or barrier semaphores. Data moves between devices by JAX's collectives and lax.ppermute only.
A program may use at most 192 MiB of HBM per device.

v0:
```python
import jax
import jax.numpy as jnp
from jax import lax
from jax.sharding import PartitionSpec as P

EXPERTS = 64
TOP = 6
CAP = 16


def encode_tiles(active, adapter_weight):
    tile_count, tile_rows, adapt_width = active.shape
    flattened = active.reshape(tile_count * tile_rows, adapt_width)
    whole_weight = lax.all_gather(adapter_weight, "wide", axis=0, tiled=True)
    product = jnp.dot(flattened, whole_weight, preferred_element_type=jnp.float32)
    return product.astype(jnp.bfloat16).reshape(tile_count, tile_rows, adapter_weight.shape[1])


def activate(tiles):
    return jax.nn.gelu(tiles.astype(jnp.float32), approximate=False).astype(jnp.bfloat16)


def round_keep(values):
    return lax.optimization_barrier(values.astype(jnp.bfloat16)).astype(jnp.float32)


def on_device(
    tile_hidden,
    cached_rows,
    tile_image,
    cache_ids,
    adapter_weight,
    routes,
    route_gates,
    gate_up,
    expert_down,
):
    slot_count, tile_rows, adapt_width = tile_hidden.shape
    half_width = cached_rows.shape[1]
    cache_hit = jnp.any(tile_image[:, None] == cache_ids[None, :], axis=1)
    encoded = encode_tiles(activate(tile_hidden), adapter_weight)
    token_count = slot_count * tile_rows
    hit_rows = jnp.repeat(cache_hit, tile_rows)
    tokens_in = jnp.where(hit_rows[:, None], cached_rows, encoded.reshape(token_count, half_width))
    expert_flat = routes.reshape(-1)
    pair_count = expert_flat.shape[0]
    onehot = (expert_flat[:, None] == jnp.arange(EXPERTS, dtype=jnp.int32)[None, :]).astype(
        jnp.int32
    )
    earlier = jnp.cumsum(onehot, axis=0) - onehot
    slot_index = jnp.sum(earlier * onehot, axis=1)
    target = expert_flat * CAP + slot_index
    owner_table = (
        jnp.full((EXPERTS * CAP,), token_count, jnp.int32)
        .at[target]
        .set(jnp.arange(pair_count, dtype=jnp.int32) // TOP)
    )
    padded_tokens = jnp.concatenate([tokens_in, jnp.zeros((1, half_width), jnp.bfloat16)])
    expert_rows = padded_tokens[owner_table].reshape(EXPERTS, CAP, half_width)
    local_halves = gate_up.shape[0]
    outgoing = jnp.broadcast_to(expert_rows[:, None], (EXPERTS, 2, CAP, half_width)).reshape(
        2 * EXPERTS, CAP, half_width
    )
    arrived = lax.all_to_all(outgoing, "wide", split_axis=0, concat_axis=1, tiled=True)
    inner_width = gate_up.shape[3]
    preact_local = jnp.einsum(
        "lrd,ldf->lrf",
        arrived,
        gate_up.reshape(local_halves, half_width, 2 * inner_width),
        preferred_element_type=jnp.float32,
    )
    rounded = round_keep(preact_local)
    summed = lax.psum(rounded.astype(jnp.bfloat16), "narrow").astype(jnp.float32)
    hidden = (jax.nn.silu(summed[:, :, :inner_width]) * summed[:, :, inner_width:]).astype(
        jnp.bfloat16
    )
    partial_out = jnp.einsum(
        "lrf,lfd->lrd", hidden, expert_down, preferred_element_type=jnp.float32
    ).astype(jnp.bfloat16)
    returned = lax.all_to_all(partial_out, "wide", split_axis=1, concat_axis=0, tiled=True)
    both_halves = returned.reshape(EXPERTS, 2, CAP, half_width).astype(jnp.float32)
    summed_rows = round_keep(both_halves[:, 0] + both_halves[:, 1]).reshape(
        EXPERTS * CAP, half_width
    )
    picked = summed_rows[target].reshape(token_count, TOP, half_width)
    mixed = jnp.sum(picked * route_gates[:, :, None], axis=1)
    return mixed.astype(jnp.bfloat16)


def solution(mesh):
    return jax.shard_map(
        on_device,
        mesh=mesh,
        in_specs=(
            P(("grp", "wide"), None, None),
            P(("grp", "wide"), "narrow"),
            P(("grp", "wide")),
            P("grp"),
            P("wide", "narrow"),
            P(("grp", "wide"), None),
            P(("grp", "wide"), None),
            P("wide", "narrow", None, None),
            P("wide", None, "narrow"),
        ),
        out_specs=P(("grp", "wide"), "narrow"),
        check_vma=False,
    )
```

profile of v0, /device:TPU:0, one launch (start us, length us, event | category | flops | bytes accessed | tf_op | source)
XLA Modules:
  0.0 372.0 jit_solution(16675624103529468104)
XLA Ops:
  6.5 0.0 all-gather.2.cloned.1.call-start
  6.5 0.7 all-gather.2.cloned.1.call-update
  7.3 0.8 copy.35
  8.1 0.1 eq.45
  8.2 0.1 eq.41
  8.4 1.8 reduce-window.6
  10.2 0.3 slice_reduce_fusion
  10.5 0.7 broadcast_multiply_fusion
  11.2 0.1 copy.34
  11.3 0.1 mul.56
  11.4 0.9 compare_reduce_fusion
  12.3 0.1 broadcast_in_dim.33
  12.3 0.1 broadcast_in_dim.34
  12.4 0.1 fusion.39
  12.6 3.4 scatter_custom_fusion
  16.0 2.1 fusion.7
  18.1 43.4 %all-gather.2.cloned.1.call-done = bf16[1024,1024]{1,0:T(8,128)(2,1)} async-done(((bf16[128,1024]{1,0:T(8,128)(2,1)}), bf16[1024,1024]{1,0:T(8,128)(2,1)}) %all-gather.2.cloned.1.call-update) | async-done | bytes 2097168 | tf_op jit(solution)/shard_map/all_gather | solution.py:14
  61.5 2.0 fusion.5
  63.6 4.1 %gather_fusion = bf16[1024,1024]{1,0:T(8,128)(2,1)S(1)} fusion(bf16[129,1024]{1,0:T(8,128)(2,1)S(1)} %concatenate.3, s32[1024]{0:T(1024)S(1)} %fusion.43), kind=kCustom, calls=%fused_computation | custom fusion | bytes 4198400 | tf_op jit(solution)/shard_map/gather | solution.py:59
  67.7 2.5 broadcast_in_dim.39
  70.2 4.6 %all-to-all-start = ((bf16[128,16,1024]{2,1,0:T(8,128)(2,1)}), bf16[128,16,1024]{2,1,0:T(8,128)(2,1)}, u32[]{:S(2)}, u32[]{:S(2)}) async-start(bf16[128,16,1024]{2,1,0:T(8,128)(2,1)} %bitcast.45), calls=%async_computation | async-start | bytes 8388608 | tf_op jit(solution)/shard_map/all_to_all | solution.py:64
  74.8 0.2 all-reduce.3.cloned.1.call-start
  75.0 53.6 %reshape.80 = bf16[16,1024,1024]{2,1,0:T(8,128)(2,1)} reshape(bf16[16,1024,2,512]{3,2,1,0:T(2,128)(2,1)} %param.16) | data formatting | bytes 67108864 | tf_op jit(solution)/shard_map/reshape | solution.py:69
  128.6 38.5 %all-to-all-done = bf16[128,16,1024]{2,1,0:T(8,128)(2,1)} async-done(((bf16[128,16,1024]{2,1,0:T(8,128)(2,1)}), bf16[128,16,1024]{2,1,0:T(8,128)(2,1)}, u32[]{:S(2)}, u32[]{:S(2)}) %all-to-all-start) | async-done | bytes 4194336 | tf_op jit(solution)/shard_map/all_to_all | solution.py:64
  167.1 5.0 %copy.38 = bf16[16,8,16,1024]{3,2,1,0:T(8,128)(2,1)} copy(bf16[16,8,16,1024]{3,2,0,1:T(8,128)(2,1)} %bitcast.5) | data formatting | bytes 8388608 | tf_op jit(solution)/shard_map/all_to_all | solution.py:64
  172.1 16.4 %convolution_convert_fusion.1 = bf16[16,128,1024]{2,1,0:T(8,128)(2,1)} fusion(bf16[16,128,1024]{2,1,0:T(8,128)(2,1)} %bitcast.43, bf16[16,1024,1024]{2,1,0:T(8,128)(2,1)} %reshape.80), kind=kOutput, calls=%fused_computation.10 | convolution fusion | flops 4297064448 | bytes 41943040 | tf_op jit(solution)/shard_map/lrd,ldf->lrf/dot_general | solution.py:66
  188.4 0.0 all-reduce.3.cloned.1.call-update
  188.5 27.6 %all-reduce.3.cloned.1.call-done = bf16[16,128,1024]{2,1,0:T(8,128)(2,1)} async-done(((bf16[16,128,1024]{2,1,0:T(8,128)(2,1)}), bf16[16,128,1024]{2,1,0:T(8,128)(2,1)}) %all-reduce.3.cloned.1.call-update) | async-done | bytes 4194320 | tf_op jit(solution)/shard_map/psum | solution.py:73
  216.1 6.5 %convert_element_type.58 = f32[16,128,1024]{2,1,0:T(8,128)} convert(bf16[16,128,1024]{2,1,0:T(8,128)(2,1)} %all-reduce.3.cloned.1.call-done) | non-fusion elementwise | flops 2097152 | bytes 12582912 | tf_op jit(solution)/shard_map/convert_element_type | solution.py:73
  222.5 13.4 %convolution_convert_fusion = bf16[16,128,1024]{2,1,0:T(8,128)(2,1)} fusion(bf16[16,512,1024]{2,1,0:T(8,128)(2,1)} %param.17, f32[16,128,1024]{2,1,0:T(8,128)} %convert_element_type.58), kind=kOutput, calls=%fused_computation.9 | convolution fusion | flops 2155872256 | bytes 29360128 | tf_op jit(solution)/shard_map/lrf,lfd->lrd/dot_general | solution.py:77
  236.0 6.4 %copy.39 = bf16[16,128,1024]{2,0,1:T(8,128)(2,1)} copy(bf16[16,128,1024]{2,1,0:T(8,128)(2,1)} %convolution_convert_fusion) | data formatting | bytes 8388608 | tf_op jit(solution)/shard_map/convert_element_type | solution.py:79
  242.4 0.0 copy-start
  242.4 5.9 %all-to-all-start.1 = ((bf16[16,128,1024]{2,0,1:T(8,128)(2,1)}), bf16[16,128,1024]{2,0,1:T(8,128)(2,1)}, u32[]{:S(2)}, u32[]{:S(2)}) async-start(bf16[16,128,1024]{2,0,1:T(8,128)(2,1)} %copy.39), calls=%async_computation.1 | async-start | bytes 8388608 | tf_op jit(solution)/shard_map/all_to_all | solution.py:80
  248.3 0.0 copy-done
  248.3 0.1 copy.42
  248.4 93.6 %all-to-all-done.1 = bf16[16,128,1024]{2,0,1:T(8,128)(2,1)} async-done(((bf16[16,128,1024]{2,0,1:T(8,128)(2,1)}), bf16[16,128,1024]{2,0,1:T(8,128)(2,1)}, u32[]{:S(2)}, u32[]{:S(2)}) %all-to-all-start.1) | async-done | bytes 4194336 | tf_op jit(solution)/shard_map/all_to_all | solution.py:80
  342.1 4.5 %copy.40 = bf16[16,128,1024]{2,1,0:T(8,128)(2,1)S(1)} copy(bf16[16,128,1024]{2,0,1:T(8,128)(2,1)} %all-to-all-done.1) | data formatting | bytes 8388608 | tf_op jit(solution)/shard_map/all_to_all | solution.py:80
  346.6 1.1 convert_bitcast_fusion
  347.6 1.7 copy.41
  349.3 0.7 fusion.3
  350.0 2.5 bitcast_convert_fusion
  352.6 6.1 %gather_fusion.1 = f32[768,1024]{1,0:T(8,128)S(1)} fusion(f32[1024,1024]{1,0:T(8,128)} %bitcast_convert_fusion, s32[1024]{0:T(1024)S(1)} %pad_clamp_fusion), kind=kCustom, calls=%fused_computation.1 | custom fusion | bytes 6294528 | tf_op jit(solution)/shard_map/gather | solution.py:85
  358.7 2.1 reshape.83
  360.9 4.3 %multiply_reduce_fusion = bf16[128,1024]{1,0:T(8,128)(2,1)} fusion(f32[128,6,1024]{2,1,0:T(8,128)} %reshape.83, f32[128,6]{1,0:T(8,128)S(1)} %copy.42), kind=kLoop, calls=%fused_computation.8 | loop fusion | flops 1441792 | bytes 3410944 | tf_op jit(solution)/shard_map/reduce_sum | solution.py:86
  (7 shorter events, 0.1 us)
Async XLA Ops:
  6.5 55.0 %all-gather.2.cloned.1.call-start = ((), (), s32[]{:S(2)}) async-start(), calls=%async_computation.2 | async-start | bytes 2359296 | tf_op jit(solution)/shard_map/all_gather | solution.py:14
  70.2 96.9 %all-to-all-start = ((bf16[128,16,1024]{2,1,0:T(8,128)(2,1)}), bf16[128,16,1024]{2,1,0:T(8,128)(2,1)}, u32[]{:S(2)}, u32[]{:S(2)}) async-start(bf16[128,16,1024]{2,1,0:T(8,128)(2,1)} %bitcast.45), calls=%async_computation | async-start | bytes 8388608 | tf_op jit(solution)/shard_map/all_to_all | solution.py:64
  74.8 141.3 %all-reduce.3.cloned.1.call-start = ((), (), s32[]{:S(2)}) async-start(), calls=%async_computation.3 | async-start | bytes 8388608 | tf_op jit(solution)/shard_map/psum | solution.py:73
  242.4 5.9 %copy-start = (f32[128,6]{0,1:T(8,128)S(1)}, f32[128,6]{0,1:T(8,128)}, u32[]{:S(2)}) copy-start(f32[128,6]{0,1:T(8,128)} %param.15) | copy-start | bytes 9220
  242.4 99.7 %all-to-all-start.1 = ((bf16[16,128,1024]{2,0,1:T(8,128)(2,1)}), bf16[16,128,1024]{2,0,1:T(8,128)(2,1)}, u32[]{:S(2)}, u32[]{:S(2)}) async-start(bf16[16,128,1024]{2,0,1:T(8,128)(2,1)} %copy.39), calls=%async_computation.1 | async-start | bytes 8388608 | tf_op jit(solution)/shard_map/all_to_all | solution.py:80
Sparse Core Ops, SparseCore 0:
  9.5 51.9 all-gather.1
  188.6 27.4 all-reduce.2
where the time goes:
time: 374 us; the launch traced here: 372 us
  waiting for transfers between devices  204 us (55%)
  local copies, waits for them, and re-layouts  91.3 us (24%)
  matrix products  31.8 us (9%)
  other arithmetic  20.7 us (6%)
  between operations  13.5 us (4%)
  starting transfers between devices  10.7 us (3%)
    all_to_all x1, waiting for transfers between devices, on_device(): lax.all_to_all(partial_out, 'wide', split_axis=1, concat_axis=0, tiled=True)  93.6 us
    reshape x1, local copies, waits for them, and re-layouts, on_device(): gate_up.reshape(local_halves, half_width, 2 * inner_width)  53.6 us
    all_gather x1, waiting for transfers between devices, encode_tiles(): whole_weight = lax.all_gather(adapter_weight, 'wide', axis=0, tiled=True)  43.4 us
    all_to_all x1, waiting for transfers between devices, on_device(): lax.all_to_all(outgoing, 'wide', split_axis=0, concat_axis=1, tiled=True)  38.5 us
    psum x1, waiting for transfers between devices, on_device(): lax.psum(rounded.astype(jnp.bfloat16), 'narrow').astype(jnp.float32)  27.6 us
    dot_general x1, matrix products, on_device(): jnp.einsum('lrd,ldf->lrf', arrived, gate_up.reshape(local_halves, half_wi...  16.4 us
    dot_general x1, matrix products, on_device(): jnp.einsum('lrf,lfd->lrd', hidden, expert_down, preferred_element_type=jn...  13.4 us
  transfers between devices with their start and end apart: 4, of which 4 were waited for; matrix products, arithmetic and copies ran while one was open for 17% of the time, Pallas kernels for 0%

commit v1 on v0

v1 whole, which is shorter than its diff:
```python
import functools

import jax
import jax.numpy as jnp
from jax import lax
from jax.experimental import pallas as pl
from jax.experimental.pallas import tpu as pltpu
from jax.sharding import PartitionSpec as P

EXPERTS = 64
TOP = 6
CAP = 16
F32 = jnp.float32
BF16 = jnp.bfloat16
RING = (0, 2, 4, 6, 7, 5, 3, 1)
NR = 8
VMEM_LIMIT = 48 << 20
ANY = pl.BlockSpec(memory_space=pl.ANY)
VM = pl.BlockSpec(memory_space=pltpu.VMEM)
SM = pl.BlockSpec(memory_space=pltpu.SMEM)


def activate(tiles):
    return jax.nn.gelu(tiles.astype(F32), approximate=False).astype(BF16)


def round_keep(values):
    return lax.optimization_barrier(values.astype(BF16)).astype(F32)


def on_device_plain(
    tile_hidden, cached_rows, tile_image, cache_ids, adapter_weight, routes, route_gates, gate_up, expert_down
):
    slot_count, tile_rows, adapt_width = tile_hidden.shape
    half_width = cached_rows.shape[1]
    cache_hit = jnp.any(tile_image[:, None] == cache_ids[None, :], axis=1)
    whole_weight = lax.all_gather(adapter_weight, "wide", axis=0, tiled=True)
    active = activate(tile_hidden).reshape(slot_count * tile_rows, adapt_width)
    encoded = jnp.dot(active, whole_weight, preferred_element_type=F32).astype(BF16)
    token_count = slot_count * tile_rows
    hit_rows = jnp.repeat(cache_hit, tile_rows)
    tokens_in = jnp.where(hit_rows[:, None], cached_rows, encoded)
    expert_flat = routes.reshape(-1)
    pair_count = expert_flat.shape[0]
    onehot = (expert_flat[:, None] == jnp.arange(EXPERTS, dtype=jnp.int32)[None, :]).astype(jnp.int32)
    earlier = jnp.cumsum(onehot, axis=0) - onehot
    slot_index = jnp.sum(earlier * onehot, axis=1)
    target = expert_flat * CAP + slot_index
    owner_table = (
        jnp.full((EXPERTS * CAP,), token_count, jnp.int32)
        .at[target]
        .set(jnp.arange(pair_count, dtype=jnp.int32) // TOP)
    )
    padded_tokens = jnp.concatenate([tokens_in, jnp.zeros((1, half_width), BF16)])
    expert_rows = padded_tokens[owner_table].reshape(EXPERTS, CAP, half_width)
    local_halves = gate_up.shape[0]
    outgoing = jnp.broadcast_to(expert_rows[:, None], (EXPERTS, 2, CAP, half_width)).reshape(
        2 * EXPERTS, CAP, half_width
    )
    arrived = lax.all_to_all(outgoing, "wide", split_axis=0, concat_axis=1, tiled=True)
    inner_width = gate_up.shape[3]
    preact_local = jnp.einsum(
        "lrd,ldf->lrf",
        arrived,
        gate_up.reshape(local_halves, half_width, 2 * inner_width),
        preferred_element_type=F32,
    )
    rounded = round_keep(preact_local)
    summed = lax.psum(rounded.astype(BF16), "narrow").astype(F32)
    hidden = (jax.nn.silu(summed[:, :, :inner_width]) * summed[:, :, inner_width:]).astype(BF16)
    partial_out = jnp.einsum("lrf,lfd->lrd", hidden, expert_down, preferred_element_type=F32).astype(BF16)
    returned = lax.all_to_all(partial_out, "wide", split_axis=1, concat_axis=0, tiled=True)
    both_halves = returned.reshape(EXPERTS, 2, CAP, half_width).astype(F32)
    summed_rows = round_keep(both_halves[:, 0] + both_halves[:, 1]).reshape(EXPERTS * CAP, half_width)
    picked = summed_rows[target].reshape(token_count, TOP, half_width)
    mixed = jnp.sum(picked * route_gates[:, :, None], axis=1)
    return mixed.astype(BF16)


def ring_pairs(shift):
    return [(RING[i], RING[(i + shift) % NR]) for i in range(NR)]


def from_prev(value):
    return lax.ppermute(value, "wide", ring_pairs(1))


def from_next(value):
    return lax.ppermute(value, "wide", ring_pairs(-1))


def swap(value, axis):
    return lax.ppermute(value, axis, [(0, 1), (1, 0)])


def ring_gather(own, antipode_by_prev):
    got = [None] * NR
    got[0] = own
    for q in (1, 2, 3):
        got[q] = from_prev(got[q - 1])
        got[NR - q] = from_next(got[(NR - q + 1) % NR])
    got[4] = from_prev(got[3]) if antipode_by_prev else from_next(got[5])
    return got


def add(left, right):
    return (left.astype(F32) + right.astype(F32)).astype(BF16)


def ring_scatter(parts, antipode_by_next):
    if antipode_by_next:
        low = add(from_next(parts[4]), parts[3])
        high = parts[5]
    else:
        low = parts[3]
        high = add(from_prev(parts[4]), parts[5])
    for q in (2, 1, 0):
        low = from_next(low)
        high = from_prev(high)
        if q:
            low = add(low, parts[q])
            high = add(high, parts[NR - q])
    return (parts[0].astype(F32) + low.astype(F32) + high.astype(F32)).astype(BF16)


def prologue_kernel(
    experts,
    slots,
    tile_rows,
    *refs,
):
    n_tok = NR * slots
    meta, info = refs[0], refs[1]
    token_in = refs[2 : 2 + n_tok]
    weight_in = refs[2 + n_tok : 2 + n_tok + 2 * NR]
    rows_out, mix_out = refs[2 + n_tok + 2 * NR : 4 + n_tok + 2 * NR]
    tokens, weight, packed, token_sem, weight_sem = refs[4 + n_tok + 2 * NR :]
    part = weight_in[0].shape[0]
    copies = []
    for i, ref in enumerate(token_in):
        copies.append(pltpu.make_async_copy(ref, tokens.at[i], token_sem.at[i]))
    for i, ref in enumerate(weight_in):
        at = pl.multiple_of(meta[16 + i] * part, part)
        copies.append(pltpu.make_async_copy(ref, weight.at[pl.ds(at, part)], weight_sem.at[i]))
    for copy in copies:
        copy.start()

    first = meta[0].astype(F32)
    toks = slots * tile_rows
    before = lax.broadcasted_iota(jnp.int32, (toks, toks), 0) < lax.broadcasted_iota(jnp.int32, (toks, toks), 1)
    before = before.astype(F32).astype(BF16)
    ids = lax.broadcasted_iota(jnp.int32, (experts, toks), 0).astype(F32) + first
    place = lax.broadcasted_iota(jnp.int32, (experts, CAP, toks), 1).astype(F32)
    picks = []
    for q in range(NR):
        named = jnp.zeros((experts, toks), F32)
        gate = jnp.zeros((experts, toks), F32)
        for k in range(TOP):
            same = jnp.broadcast_to(info[q, k : k + 1, :], (experts, toks)) == ids
            named = jnp.where(same, 1.0, named)
            gate = jnp.where(same, jnp.broadcast_to(info[q, 8 + k : 9 + k, :], (experts, toks)), gate)
        rank = jnp.dot(named.astype(BF16), before, preferred_element_type=F32)
        rank = jnp.where(named > 0.0, rank, -1.0)
        chosen = jnp.broadcast_to(rank[:, None, :], (experts, CAP, toks)) == place
        pick = jnp.where(chosen, 1.0, 0.0).reshape(experts * CAP, toks)
        picks.append(pick.astype(BF16))
        gated = jnp.where(chosen, jnp.broadcast_to(gate[:, None, :], (experts, CAP, toks)), 0.0)
        gated = gated.reshape(experts * CAP, toks)
        coarse = gated.astype(BF16)
        mix_out[q, 0] = coarse
        mix_out[q, 1] = (gated - coarse.astype(F32)).astype(BF16)

    for copy in copies:
        copy.wait()

    missed = meta[1]
    most = packed.shape[0]
    for i in range(most):

        @pl.when(i < missed)
        def _(i=i):
            packed[i] = tokens[meta[2 + i]]

    for i in range(0, most, 2):

        @pl.when(i < missed)
        def _(i=i):
            rows = packed[i : i + 2].reshape(2 * tile_rows, packed.shape[2])
            coded = jnp.dot(rows, weight[...], preferred_element_type=F32).astype(BF16)
            tokens[meta[2 + i]] = coded[:tile_rows]

            @pl.when(i + 1 < missed)
            def _():
                tokens[meta[3 + i]] = coded[tile_rows:]

    for q in range(NR):
        source = tokens[q * slots : (q + 1) * slots].reshape(toks, tokens.shape[2])
        rows = jnp.dot(picks[q], source, preferred_element_type=F32).astype(BF16)
        rows_out[:, q * CAP : (q + 1) * CAP, :] = rows.reshape(experts, CAP, tokens.shape[2])


def first_kernel(base, count, rows, gate_up, out, wbuf, spread, sem):
    halves = 2 * count
    copies = [
        pltpu.make_async_copy(gate_up.at[2 * base + h], wbuf.at[h], sem.at[h]) for h in range(halves)
    ]
    for copy in copies:
        copy.start()
    width = rows.shape[2]
    most = rows.shape[1]
    inner = gate_up.shape[3]
    src = lax.broadcasted_iota(jnp.int32, (128, 256), 0)
    dst = lax.broadcasted_iota(jnp.int32, (128, 256), 1)
    even = (dst == 2 * src).astype(F32).astype(BF16)
    odd = (dst == 2 * src + 1).astype(F32).astype(BF16)
    for e in range(count):
        for c in range(width // 128):
            piece = rows[base + e, :, 128 * c : 128 * c + 128]
            spread[e, :most, 256 * c : 256 * c + 256] = jnp.dot(piece, even, preferred_element_type=F32).astype(BF16)
            spread[e, most:, 256 * c : 256 * c + 256] = jnp.dot(piece, odd, preferred_element_type=F32).astype(BF16)
    for h in range(halves):
        copies[h].wait()
        acc = jnp.dot(
            spread[h // 2], wbuf[h].reshape(2 * width, inner), preferred_element_type=F32
        )
        out[h, :, :inner] = acc[:most].astype(BF16)
        out[h, :, inner:] = acc[most:].astype(BF16)


def second_kernel(chunk, width, n_chunks, make_hidden, *refs):
    if make_hidden:
        own = refs[:n_chunks]
        other = refs[n_chunks : 2 * n_chunks]
        mix, down = refs[2 * n_chunks : 2 * n_chunks + 2]
        hidden = refs[2 * n_chunks + 2]
        outs = refs[2 * n_chunks + 3 : 2 * n_chunks + 3 + NR]
        wbuf, pairs, sem = refs[2 * n_chunks + 3 + NR :]
    else:
        hidden, mix, down = refs[:3]
        outs = refs[3 : 3 + NR]
        wbuf, pairs, sem = refs[3 + NR :]
    halves, _, inner = hidden.shape
    copies = [
        pltpu.make_async_copy(
            down.at[pl.ds(2 * e, 2), :, pl.ds(chunk * width, width)], wbuf.at[pl.ds(2 * e, 2)], sem.at[e]
        )
        for e in range(halves // 2)
    ]
    for copy in copies:
        copy.start()
    if make_hidden:
        per = halves // n_chunks
        for h in range(halves):
            pre = own[h // per][h % per].astype(F32) + other[h // per][h % per].astype(F32)
            gate, up = pre[:, :inner], pre[:, inner:]
            hidden[h] = (gate / (1.0 + jnp.exp(-gate)) * up).astype(BF16)
    for e in range(halves // 2):
        copies[e].wait()
        acc = jnp.dot(hidden[2 * e], wbuf[2 * e], preferred_element_type=F32)
        acc += jnp.dot(hidden[2 * e + 1], wbuf[2 * e + 1], preferred_element_type=F32)
        pairs[e] = acc.astype(BF16)
    dims = (((0,), (0,)), ((), ()))
    for q in range(NR):
        rows = pairs[:, q * CAP : (q + 1) * CAP, :].reshape(halves // 2 * CAP, width)
        total = lax.dot_general(mix[q, 0], rows, dims, preferred_element_type=F32)
        total += lax.dot_general(mix[q, 1], rows, dims, preferred_element_type=F32)
        outs[q][...] = total.astype(BF16)


def on_device_ring(
    tile_hidden, cached_rows, tile_image, cache_ids, adapter_weight, routes, route_gates, gate_up, expert_down
):
    slots, tile_rows, adapt_width = tile_hidden.shape
    toks = slots * tile_rows
    half_width = cached_rows.shape[1]
    halves, _, _, inner = gate_up.shape
    experts = halves // 2
    shard = adapter_weight.shape[0]
    part = shard // 2
    params = pltpu.CompilerParams(vmem_limit_bytes=VMEM_LIMIT)

    wide_id = lax.axis_index("wide")
    grp_id = lax.axis_index("grp")
    where_in_ring = [RING.index(w) for w in range(NR)]
    pos = jnp.asarray(where_in_ring, jnp.int32)[wide_id]
    sources = jnp.asarray(RING, jnp.int32)[(pos - jnp.arange(NR, dtype=jnp.int32)) % NR]

    weight_own = lax.dynamic_slice_in_dim(adapter_weight, grp_id * part, part, axis=0)
    weight_ring = ring_gather(weight_own, True)
    weight_other = [swap(value, "grp") for value in weight_ring]

    cache_hit = jnp.any(tile_image[:, None] == cache_ids[None, :], axis=1)
    sent = jnp.where(cache_hit[:, None, None], cached_rows.reshape(slots, tile_rows, half_width), activate(tile_hidden))
    info_own = jnp.concatenate(
        [
            routes.T.astype(F32),
            jnp.broadcast_to(jnp.where(cache_hit, 0.0, 1.0).astype(F32)[:, None], (slots, tile_rows)).reshape(1, toks),
            jnp.zeros((1, toks), F32),
            route_gates.T,
            jnp.zeros((2, toks), F32),
        ]
    )
    info = jnp.stack([info_own] + [lax.ppermute(info_own, "wide", ring_pairs(q)) for q in range(1, NR)])
    tokens = [ring_gather(sent[s], s % 2 == 0) for s in range(slots)]

    missed = info[:, 6, :].reshape(NR * slots, tile_rows)[:, 0] > 0.5
    rank = jnp.where(missed, jnp.cumsum(missed.astype(jnp.int32)) - 1, -1)
    most = NR * slots // 2
    at = jnp.arange(NR * slots, dtype=jnp.int32)
    missed_at = jnp.sum(
        jnp.where(rank[None, :] == jnp.arange(most, dtype=jnp.int32)[:, None], at[None, :], 0), axis=1
    )
    meta = jnp.concatenate(
        [
            (wide_id * experts).reshape(1).astype(jnp.int32),
            jnp.sum(missed.astype(jnp.int32)).reshape(1),
            missed_at.astype(jnp.int32),
            jnp.zeros((16 - 2 - most,), jnp.int32),
            sources * 2 + grp_id,
            sources * 2 + (1 - grp_id),
        ]
    )

    rows, mix = pl.pallas_call(
        functools.partial(prologue_kernel, experts, slots, tile_rows),
        in_specs=[SM, VM] + [ANY] * (NR * slots + 2 * NR),
        out_specs=[VM, VM],
        out_shape=[
            jax.ShapeDtypeStruct((experts, NR * CAP, half_width), BF16),
            jax.ShapeDtypeStruct((NR, 2, experts * CAP, toks), BF16),
        ],
        scratch_shapes=[
            pltpu.VMEM((NR * slots, tile_rows, half_width), BF16),
            pltpu.VMEM((NR * shard, half_width), BF16),
            pltpu.VMEM((most, tile_rows, half_width), BF16),
            pltpu.SemaphoreType.DMA((NR * slots,)),
            pltpu.SemaphoreType.DMA((2 * NR,)),
        ],
        compiler_params=params,
    )(meta, info, *[tokens[s][q] for q in range(NR) for s in range(slots)], *weight_ring, *weight_other)

    n_first = 4
    count = experts // n_first
    own, other = [], []
    for c in range(n_first):
        pre = pl.pallas_call(
            functools.partial(first_kernel, c * count, count),
            in_specs=[VM, ANY],
            out_specs=VM,
            out_shape=jax.ShapeDtypeStruct((2 * count, NR * CAP, 2 * inner), BF16),
            scratch_shapes=[
                pltpu.VMEM((2 * count, half_width, 2, inner), BF16),
                pltpu.VMEM((count, 2 * NR * CAP, 2 * half_width), BF16),
                pltpu.SemaphoreType.DMA((2 * count,)),
            ],
            compiler_params=params,
            cost_estimate=pl.CostEstimate(
                flops=4 * NR * CAP * half_width * 4 * count * inner,
                bytes_accessed=2 * count * half_width * 4 * inner,
                transcendentals=0,
            ),
        )(rows, gate_up)
        own.append(pre)
        other.append(swap(pre, "narrow"))

    n_second = 2
    width = half_width // n_second
    mixed = []
    hidden = None
    for c in range(n_second):
        part_shapes = [jax.ShapeDtypeStruct((toks, width), BF16)] * NR
        scratch = [
            pltpu.VMEM((halves, inner, width), BF16),
            pltpu.VMEM((experts, NR * CAP, width), BF16),
            pltpu.SemaphoreType.DMA((experts,)),
        ]
        cost = pl.CostEstimate(
            flops=2 * halves * NR * CAP * inner * width,
            bytes_accessed=2 * halves * inner * width,
            transcendentals=0,
        )
        if hidden is None:
            hidden, *parts = pl.pallas_call(
                functools.partial(second_kernel, c, width, n_first, True),
                in_specs=[VM] * (2 * n_first) + [VM, ANY],
                out_specs=[VM] * (NR + 1),
                out_shape=[jax.ShapeDtypeStruct((halves, NR * CAP, inner), BF16)] + part_shapes,
                scratch_shapes=scratch,
                compiler_params=params,
                cost_estimate=cost,
            )(*own, *other, mix, expert_down)
        else:
            parts = pl.pallas_call(
                functools.partial(second_kernel, c, width, n_first, False),
                in_specs=[VM, VM, ANY],
                out_specs=[VM] * NR,
                out_shape=part_shapes,
                scratch_shapes=scratch,
                compiler_params=params,
                cost_estimate=cost,
            )(hidden, mix, expert_down)
        mixed.append(ring_scatter(parts, c % 2 == 0))
    return jnp.concatenate(mixed, axis=1)


def solution(mesh):
    body = on_device_ring if mesh.shape["wide"] == NR else on_device_plain
    return jax.shard_map(
        body,
        mesh=mesh,
        in_specs=(
            P(("grp", "wide"), None, None),
            P(("grp", "wide"), "narrow"),
            P(("grp", "wide")),
            P("grp"),
            P("wide", "narrow"),
            P(("grp", "wide"), None),
            P(("grp", "wide"), None),
            P("wide", "narrow", None, None),
            P("wide", None, "narrow"),
        ),
        out_specs=P(("grp", "wide"), "narrow"),
        check_vma=False,
    )
```

time: 374 us -> 152 us (0.41)
  waiting for transfers between devices: 204 us -> 27.8 us
  local copies, waits for them, and re-layouts: 91.3 us -> 10.5 us
  starting transfers between devices: 10.7 us -> 61.4 us
  Pallas kernels: 0 us -> 43.3 us
  matrix products: 31.8 us -> 0 us
  between operations: 13.5 us -> 0.26 us
  other arithmetic: 20.7 us -> 8.43 us
    all_to_all x2 -> x0, waiting for transfers between devices: 132 us -> none  [the longest x1 93.6 us: on_device(): lax.all_to_all(partial_out, 'wide', split_axis=1, concat_axis=0, tiled=True)]
    ppermute x0 -> x54, starting transfers between devices: none -> 61.4 us  [the longest x17 25.5 us: from_next(): return lax.ppermute(value, 'wide', ring_pairs(-1))]
    reshape x2 -> x1, local copies, waits for them, and re-layouts: 55.8 us -> 0.08 us  [on_device_ring(): jnp.broadcast_to(jnp.where(cache_hit, 0.0, 1.0).astype(F32)[:, None], (sl...]
    all_gather x1 -> x0, waiting for transfers between devices: 43.4 us -> none  [encode_tiles(): whole_weight = lax.all_gather(adapter_weight, 'wide', axis=0, tiled=True)]
    pallas_call x0 -> x7, Pallas kernels: none -> 43.3 us  [the longest x4 20.4 us: on_device_ring(): pl.pallas_call(functools.partial(first_kernel, c * count, count), in_spec...]
    dot_general x3 -> x0, matrix products: 31.8 us -> none  [the longest x1 16.4 us: on_device(): jnp.einsum('lrd,ldf->lrf', arrived, gate_up.reshape(local_halves, half_wi...]
    ppermute x0 -> x54, waiting for transfers between devices: none -> 27.8 us  [the longest x18 9.53 us: from_prev(): return lax.ppermute(value, 'wide', ring_pairs(1))]
    psum x1 -> x0, waiting for transfers between devices: 27.6 us -> none  [on_device(): lax.psum(rounded.astype(jnp.bfloat16), 'narrow').astype(jnp.float32)]
  transfers between devices with their start and end apart: 4 -> 54, of which waited for: 4 -> 21; matrix products, arithmetic and copies ran while one was open for 17% -> 7% of each run, Pallas kernels for 0% -> 3%
where the time goes in v1:
time: 152 us
  starting transfers between devices  61.4 us (40%)
  Pallas kernels  43.3 us (28%)
  waiting for transfers between devices  27.8 us (18%)
  local copies, waits for them, and re-layouts  10.5 us (7%)
  other arithmetic  8.43 us (6%)
    ppermute x17, starting transfers between devices, from_next(): return lax.ppermute(value, 'wide', ring_pairs(-1))  25.5 us
    pallas_call x4, Pallas kernels, on_device_ring(): pl.pallas_call(functools.partial(first_kernel, c * count, count), in_spec...  20.4 us
    ppermute x7, starting transfers between devices, on_device_ring(): lax.ppermute(info_own, 'wide', ring_pairs(q))  14.2 us
    ppermute x18, starting transfers between devices, from_prev(): return lax.ppermute(value, 'wide', ring_pairs(1))  12.9 us
    pallas_call x1, Pallas kernels, on_device_ring(): pl.pallas_call(functools.partial(prologue_kernel, experts, slots, tile_ro...  10.5 us
    ppermute x18, waiting for transfers between devices, from_prev(): return lax.ppermute(value, 'wide', ring_pairs(1))  9.53 us
    ppermute x12, starting transfers between devices, swap(): return lax.ppermute(value, axis, [(0, 1), (1, 0)])  8.78 us
    pallas_call x1, Pallas kernels, on_device_ring(): pl.pallas_call(functools.partial(second_kernel, c, width, n_first, True),...  7.85 us
  transfers between devices with their start and end apart: 54, of which 21 were waited for; matrix products, arithmetic and copies ran while one was open for 7% of the time, Pallas kernels for 3%

profile of v1, /device:TPU:0, one launch (start us, length us, event | category | flops | bytes accessed | tf_op | source)
XLA Modules:
  0.0 151.6 jit_solution(13704601892984767415)
XLA Ops:
  2.5 2.9 %collective-permute-start.6 = (f32[16,128]{1,0:T(8,128)S(1)}, f32[16,128]{1,0:T(8,128)S(1)}, u32[]{:S(2)}, u32[]{:S(2)}) collective-permute-start(f32[16,128]{1,0:T(8,128)S(1)} %concatenate.9), channel_id=1, source_target_pairs={{0,2},{4,0},{8,4},{12,8},{14,12},{10,14},{6,10},{2,6},{1,3},{5,1},... | collective-permute-start | bytes 24584 | tf_op jit(solution)/shard_map/ppermute | solution.py:303
  5.4 2.6 %collective-permute-start.5 = (f32[16,128]{1,0:T(8,128)S(1)}, f32[16,128]{1,0:T(8,128)S(1)}, u32[]{:S(2)}, u32[]{:S(2)}) collective-permute-start(f32[16,128]{1,0:T(8,128)S(1)} %concatenate.9), channel_id=1, source_target_pairs={{0,6},{4,2},{8,0},{12,4},{14,8},{10,12},{6,14},{2,10},{1,7},{5,3},... | collective-permute-start | bytes 24584 | tf_op jit(solution)/shard_map/ppermute | solution.py:303
  8.0 1.4 collective-permute-start.4
  9.4 2.3 %collective-permute-start.3 = (f32[16,128]{1,0:T(8,128)S(1)}, f32[16,128]{1,0:T(8,128)S(1)}, u32[]{:S(2)}, u32[]{:S(2)}) collective-permute-start(f32[16,128]{1,0:T(8,128)S(1)} %concatenate.9), channel_id=1, source_target_pairs={{0,14},{4,10},{8,6},{12,2},{14,0},{10,4},{6,8},{2,12},{1,15},{5,11... | collective-permute-start | bytes 24584 | tf_op jit(solution)/shard_map/ppermute | solution.py:303
  11.7 1.2 dynamic_slice.6
  13.6 2.2 %fusion.31 = bf16[2,64,1024]{2,1,0:T(8,128)(2,1)S(1)} fusion(bf16[2,64,1024]{2,1,0:T(8,128)(2,1)} %bitcast.29, bf16[2,64,1024]{2,1,0:T(8,128)(2,1)} %param.11, pred[2]{0:T(512)(128)(4,1)S(1)} %compare_reduce_fusion), kind=kLoop, calls=%fused_computation.35 | loop fusion | flops 8781824 | bytes 786434 | tf_op jit(solution)/shard_map/jit(_where)/select_n | solution.py:293
  15.9 1.3 gather_fusion
  17.8 2.0 %collective-permute-start.1 = (f32[16,128]{1,0:T(8,128)S(1)}, f32[16,128]{1,0:T(8,128)S(1)}, u32[]{:S(2)}, u32[]{:S(2)}) collective-permute-start(f32[16,128]{1,0:T(8,128)S(1)} %concatenate.9), channel_id=1, source_target_pairs={{0,8},{4,12},{8,14},{12,10},{14,6},{10,2},{6,0},{2,4},{1,9},{5,13}... | collective-permute-start | bytes 24584 | tf_op jit(solution)/shard_map/ppermute | solution.py:303
  19.8 2.7 %collective-permute-done.1 = f32[16,128]{1,0:T(8,128)S(1)} collective-permute-done((f32[16,128]{1,0:T(8,128)S(1)}, f32[16,128]{1,0:T(8,128)S(1)}, u32[]{:S(2)}, u32[]{:S(2)}) %collective-permute-start.1) | collective-permute-done | bytes 8224 | tf_op jit(solution)/shard_map/ppermute | solution.py:303
  22.5 2.9 %collective-permute-start.2 = (f32[16,128]{1,0:T(8,128)S(1)}, f32[16,128]{1,0:T(8,128)S(1)}, u32[]{:S(2)}, u32[]{:S(2)}) collective-permute-start(f32[16,128]{1,0:T(8,128)S(1)} %concatenate.9), channel_id=1, source_target_pairs={{0,12},{4,14},{8,10},{12,6},{14,2},{10,0},{6,4},{2,8},{1,13},{5,15... | collective-permute-start | bytes 24584 | tf_op jit(solution)/shard_map/ppermute | solution.py:303
  25.4 2.6 %collective-permute-done.2 = f32[16,128]{1,0:T(8,128)S(1)} collective-permute-done((f32[16,128]{1,0:T(8,128)S(1)}, f32[16,128]{1,0:T(8,128)S(1)}, u32[]{:S(2)}, u32[]{:S(2)}) %collective-permute-start.2) | collective-permute-done | bytes 8224 | tf_op jit(solution)/shard_map/ppermute | solution.py:303
  28.0 1.5 %collective-permute-start.28 = (bf16[64,1024]{1,0:T(8,128)(2,1)S(1)}, bf16[64,1024]{1,0:T(8,128)(2,1)S(1)}, u32[]{:S(2)}, u32[]{:S(2)}) collective-permute-start(bf16[64,1024]{1,0:T(8,128)(2,1)S(1)} %constant_dynamic-slice_fusion.refs_18_), channel_id=1, source_target_pairs={{0,16},{16,0},{1,17},{17,1},{2,18},{18,2},{3,19},{19,3},{4,20},{20... | collective-permute-start | bytes 393224 | tf_op jit(solution)/shard_map/ppermute | solution.py:93
  29.5 2.0 %collective-permute-start.25 = (bf16[64,1024]{1,0:T(8,128)(2,1)S(1)}, bf16[64,1024]{1,0:T(8,128)(2,1)S(1)}, u32[]{:S(2)}, u32[]{:S(2)}) collective-permute-start(bf16[64,1024]{1,0:T(8,128)(2,1)S(1)} %constant_dynamic-slice_fusion.refs_18_), channel_id=1, source_target_pairs={{0,2},{4,0},{8,4},{12,8},{14,12},{10,14},{6,10},{2,6},{1,3},{5,1},... | collective-permute-start | bytes 393224 | tf_op jit(solution)/shard_map/ppermute | solution.py:89
  31.5 2.0 %collective-permute-start.14 = (bf16[64,1024]{1,0:T(8,128)(2,1)S(1)}, bf16[64,1024]{1,0:T(8,128)(2,1)S(1)}, u32[]{:S(2)}, u32[]{:S(2)}) collective-permute-start(bf16[64,1024]{1,0:T(8,128)(2,1)S(1)} %get-tuple-element.47.refs_3_), channel_id=1, source_target_pairs={{0,2},{4,0},{8,4},{12,8},{14,12},{10,14},{6,10},{2,6},{1,3},{5,1},... | collective-permute-start | bytes 393224 | tf_op jit(solution)/shard_map/ppermute | solution.py:89
  33.6 2.0 %collective-permute-start.18 = (bf16[64,1024]{1,0:T(8,128)(2,1)S(1)}, bf16[64,1024]{1,0:T(8,128)(2,1)S(1)}, u32[]{:S(2)}, u32[]{:S(2)}) collective-permute-start(bf16[64,1024]{1,0:T(8,128)(2,1)S(1)} %get-tuple-element.48.refs_2_), channel_id=1, source_target_pairs={{0,2},{4,0},{8,4},{12,8},{14,12},{10,14},{6,10},{2,6},{1,3},{5,1},... | collective-permute-start | bytes 393224 | tf_op jit(solution)/shard_map/ppermute | solution.py:89
  37.8 2.3 %collective-permute-start.26 = (bf16[64,1024]{1,0:T(8,128)(2,1)S(1)}, bf16[64,1024]{1,0:T(8,128)(2,1)S(1)}, u32[]{:S(2)}, u32[]{:S(2)}) collective-permute-start(bf16[64,1024]{1,0:T(8,128)(2,1)S(1)} %collective-permute-done.25.refs_25_), channel_id=1, source_target_pairs={{0,2},{4,0},{8,4},{12,8},{14,12},{10,14},{6,10},{2,6},{1,3},{5,1},... | collective-permute-start | bytes 393224 | tf_op jit(solution)/shard_map/ppermute | solution.py:89
  41.2 1.5 collective-permute-done.7.refs_4_
  42.6 2.1 %collective-permute-start.15 = (bf16[64,1024]{1,0:T(8,128)(2,1)S(1)}, bf16[64,1024]{1,0:T(8,128)(2,1)S(1)}, u32[]{:S(2)}, u32[]{:S(2)}) collective-permute-start(bf16[64,1024]{1,0:T(8,128)(2,1)S(1)} %collective-permute-done.14.refs_17_), channel_id=1, source_target_pairs={{0,2},{4,0},{8,4},{12,8},{14,12},{10,14},{6,10},{2,6},{1,3},{5,1},... | collective-permute-start | bytes 393224 | tf_op jit(solution)/shard_map/ppermute | solution.py:89
  44.8 2.0 %collective-permute-start.19 = (bf16[64,1024]{1,0:T(8,128)(2,1)S(1)}, bf16[64,1024]{1,0:T(8,128)(2,1)S(1)}, u32[]{:S(2)}, u32[]{:S(2)}) collective-permute-start(bf16[64,1024]{1,0:T(8,128)(2,1)S(1)} %collective-permute-done.18.refs_16_), channel_id=1, source_target_pairs={{0,2},{4,0},{8,4},{12,8},{14,12},{10,14},{6,10},{2,6},{1,3},{5,1},... | collective-permute-start | bytes 393224 | tf_op jit(solution)/shard_map/ppermute | solution.py:89
  47.2 1.2 collective-permute-start.34
  49.0 2.0 %collective-permute-start.27 = (bf16[64,1024]{1,0:T(8,128)(2,1)S(1)}, bf16[64,1024]{1,0:T(8,128)(2,1)S(1)}, u32[]{:S(2)}, u32[]{:S(2)}) collective-permute-start(bf16[64,1024]{1,0:T(8,128)(2,1)S(1)} %collective-permute-done.26.refs_24_), channel_id=1, source_target_pairs={{0,2},{4,0},{8,4},{12,8},{14,12},{10,14},{6,10},{2,6},{1,3},{5,1},... | collective-permute-start | bytes 393224 | tf_op jit(solution)/shard_map/ppermute | solution.py:89
  60.4 1.5 collective-permute-start.33
  64.5 1.5 select_reduce_fusion
  66.0 1.4 concatenate.10.refs_0_
  67.9 1.1 collective-permute-done.32.refs_30_
  69.8 10.5 %shard_map.109 = (bf16[8,128,1024]{2,1,0:T(8,128)(2,1)}, bf16[8,2,128,128]{3,2,1,0:T(8,128)(2,1)S(1)}) custom-call(s32[32]{0:T(128)S(1)} %concatenate.10.refs_0_, f32[8,16,128]{2,1,0:T(8,128)S(1)} %copy-done.5, bf16[64,1024]{1,0:T(8,128)(2,1)S(1)} %get-tuple-element.48.refs_2_, bf16[64,1024]{1,0:T(8,128)(2,1)S(1)} %get-tuple-element.47.refs_3_, ...), custom_call_target="tpu_custom_call" | custom-call | tf_op jit(solution)/shard_map/pallas_call | solution.py:324
  80.4 1.6 %copy-done.2 = bf16[8,128,1024]{2,1,0:T(8,128)(2,1)S(1)} copy-done((bf16[8,128,1024]{2,1,0:T(8,128)(2,1)S(1)}, bf16[8,128,1024]{2,1,0:T(8,128)(2,1)}, u32[]{:S(2)}) %copy-start.2) | copy-done | bytes 2097176
  81.9 5.1 %shard_map.113.refs_3_ = bf16[4,128,1024]{2,1,0:T(8,128)(2,1)S(1)} custom-call(bf16[8,128,1024]{2,1,0:T(8,128)(2,1)S(1)} %copy-done.2, bf16[16,1024,2,512]{3,2,1,0:T(2,128)(2,1)} %gate_up.7), custom_call_target="tpu_custom_call" | custom-call | flops 2147483648 | bytes 8388608 | tf_op jit(solution)/shard_map/pallas_call | solution.py:346
  87.0 5.1 %shard_map.112.refs_2_ = bf16[4,128,1024]{2,1,0:T(8,128)(2,1)S(1)} custom-call(bf16[8,128,1024]{2,1,0:T(8,128)(2,1)S(1)} %copy-done.2, bf16[16,1024,2,512]{3,2,1,0:T(2,128)(2,1)} %gate_up.7), custom_call_target="tpu_custom_call" | custom-call | flops 2147483648 | bytes 8388608 | tf_op jit(solution)/shard_map/pallas_call | solution.py:346
  92.1 5.1 %shard_map.111.refs_1_ = bf16[4,128,1024]{2,1,0:T(8,128)(2,1)S(1)} custom-call(bf16[8,128,1024]{2,1,0:T(8,128)(2,1)S(1)} %copy-done.2, bf16[16,1024,2,512]{3,2,1,0:T(2,128)(2,1)} %gate_up.7), custom_call_target="tpu_custom_call" | custom-call | flops 2147483648 | bytes 8388608 | tf_op jit(solution)/shard_map/pallas_call | solution.py:346
  97.2 5.1 %shard_map.110.refs_0_ = bf16[4,128,1024]{2,1,0:T(8,128)(2,1)S(1)} custom-call(bf16[8,128,1024]{2,1,0:T(8,128)(2,1)S(1)} %copy-done.2, bf16[16,1024,2,512]{3,2,1,0:T(2,128)(2,1)} %gate_up.7), custom_call_target="tpu_custom_call" | custom-call | flops 2147483648 | bytes 8388608 | tf_op jit(solution)/shard_map/pallas_call | solution.py:346
  103.4 1.6 %collective-permute-done.36.refs_4_ = bf16[4,128,1024]{2,1,0:T(8,128)(2,1)S(1)} collective-permute-done((bf16[4,128,1024]{2,1,0:T(8,128)(2,1)S(1)}, bf16[4,128,1024]{2,1,0:T(8,128)(2,1)S(1)}, u32[]{:S(2)}, u32[]{:S(2)}) %collective-permute-start.36) | collective-permute-done | bytes 1048608 | tf_op jit(solution)/shard_map/ppermute | solution.py:93
  105.1 1.5 collective-permute-done.37.refs_5_
  106.6 1.5 collective-permute-done.38.refs_6_
  108.1 1.5 collective-permute-done.39.refs_7_
  110.5 7.8 %shard_map.114 = (bf16[16,128,512]{2,1,0:T(8,128)(2,1)}, bf16[128,512]{1,0:T(8,128)(2,1)S(1)}, bf16[128,512]{1,0:T(8,128)(2,1)S(1)}, bf16[128,512]{1,0:T(8,128)(...) custom-call(bf16[4,128,1024]{2,1,0:T(8,128)(2,1)S(1)} %shard_map.110, ...), custom_call_target="tpu_custom_call" | custom-call | flops 1073741824 | bytes 8388608 | tf_op jit(solution)/shard_map/pallas_call | solution.py:383
  118.4 1.2 collective-permute-start.40
  120.5 1.6 %copy-done.3 = bf16[16,128,512]{2,1,0:T(8,128)(2,1)S(1)} copy-done((bf16[16,128,512]{2,1,0:T(8,128)(2,1)S(1)}, bf16[16,128,512]{2,1,0:T(8,128)(2,1)}, u32[]{:S(2)}) %copy-start.3) | copy-done | bytes 2097176
  122.1 4.6 %shard_map.115 = (bf16[128,512]{1,0:T(8,128)(2,1)S(1)}, bf16[128,512]{1,0:T(8,128)(2,1)S(1)}, bf16[128,512]{1,0:T(8,128)(2,1)S(1)}, bf16[128,512]{1,0:T(8,128)(2...) custom-call(bf16[16,128,512]{2,1,0:T(8,128)(2,1)S(1)} %copy-done.3, ...), custom_call_target="tpu_custom_call" | custom-call | flops 1073741824 | bytes 8388608 | tf_op jit(solution)/shard_map/pallas_call | solution.py:393
  126.6 1.2 collective-permute-start.47
  128.7 1.2 collective-permute-start.41
  130.9 2.0 %collective-permute-done.47 = bf16[128,512]{1,0:T(8,128)(2,1)S(1)} collective-permute-done((bf16[128,512]{1,0:T(8,128)(2,1)S(1)}, bf16[128,512]{1,0:T(8,128)(2,1)S(1)}, u32[]{:S(2)}, u32[]{:S(2)}) %collective-permute-start.47) | collective-permute-done | bytes 131104 | tf_op jit(solution)/shard_map/ppermute | solution.py:89
  132.9 1.2 collective-permute-start.48
  135.7 1.2 collective-permute-start.42
  139.0 1.1 collective-permute-start.49
  142.1 1.3 collective-permute-start.43
  143.4 2.4 %collective-permute-done.52 = bf16[128,512]{1,0:T(8,128)(2,1)S(1)} collective-permute-done((bf16[128,512]{1,0:T(8,128)(2,1)S(1)}, bf16[128,512]{1,0:T(8,128)(2,1)S(1)}, u32[]{:S(2)}, u32[]{:S(2)}) %collective-permute-start.52) | collective-permute-done | bytes 131104 | tf_op jit(solution)/shard_map/ppermute | solution.py:85
  147.2 3.7 %collective-permute-done.53 = bf16[128,512]{1,0:T(8,128)(2,1)S(1)} collective-permute-done((bf16[128,512]{1,0:T(8,128)(2,1)S(1)}, bf16[128,512]{1,0:T(8,128)(2,1)S(1)}, u32[]{:S(2)}, u32[]{:S(2)}) %collective-permute-start.53) | collective-permute-done | bytes 131104 | tf_op jit(solution)/shard_map/ppermute | solution.py:85
  (132 shorter events, 34.3 us)
Async XLA Ops:
  2.5 27.0 %collective-permute-start.6 = (f32[16,128]{1,0:T(8,128)S(1)}, f32[16,128]{1,0:T(8,128)S(1)}, u32[]{:S(2)}, u32[]{:S(2)}) collective-permute-start(f32[16,128]{1,0:T(8,128)S(1)} %concatenate.9), channel_id=1, source_target_pairs={{0,2},{4,0},{8,4},{12,8},{14,12},{10,14},{6,10},{2,6},{1,3},{5,1},... | collective-permute-start | bytes 24584 | tf_op jit(solution)/shard_map/ppermute | solution.py:303
  5.4 26.0 %collective-permute-start.5 = (f32[16,128]{1,0:T(8,128)S(1)}, f32[16,128]{1,0:T(8,128)S(1)}, u32[]{:S(2)}, u32[]{:S(2)}) collective-permute-start(f32[16,128]{1,0:T(8,128)S(1)} %concatenate.9), channel_id=1, source_target_pairs={{0,6},{4,2},{8,0},{12,4},{14,8},{10,12},{6,14},{2,10},{1,7},{5,3},... | collective-permute-start | bytes 24584 | tf_op jit(solution)/shard_map/ppermute | solution.py:303
  8.0 25.5 %collective-permute-start.4 = (f32[16,128]{1,0:T(8,128)S(1)}, f32[16,128]{1,0:T(8,128)S(1)}, u32[]{:S(2)}, u32[]{:S(2)}) collective-permute-start(f32[16,128]{1,0:T(8,128)S(1)} %concatenate.9), channel_id=1, source_target_pairs={{0,10},{4,6},{8,2},{12,0},{14,4},{10,8},{6,12},{2,14},{1,11},{5,7}... | collective-permute-start | bytes 24584 | tf_op jit(solution)/shard_map/ppermute | solution.py:303
  9.4 22.1 %collective-permute-start.3 = (f32[16,128]{1,0:T(8,128)S(1)}, f32[16,128]{1,0:T(8,128)S(1)}, u32[]{:S(2)}, u32[]{:S(2)}) collective-permute-start(f32[16,128]{1,0:T(8,128)S(1)} %concatenate.9), channel_id=1, source_target_pairs={{0,14},{4,10},{8,6},{12,2},{14,0},{10,4},{6,8},{2,12},{1,15},{5,11... | collective-permute-start | bytes 24584 | tf_op jit(solution)/shard_map/ppermute | solution.py:303
  11.7 6.1 %collective-permute-start = (f32[16,128]{1,0:T(8,128)S(1)}, f32[16,128]{1,0:T(8,128)S(1)}, u32[]{:S(2)}, u32[]{:S(2)}) collective-permute-start(f32[16,128]{1,0:T(8,128)S(1)} %concatenate.9), channel_id=1, source_target_pairs={{0,4},{4,8},{8,12},{12,14},{14,10},{10,6},{6,2},{2,0},{1,5},{5,9},... | collective-permute-start | bytes 24584 | tf_op jit(solution)/shard_map/ppermute | solution.py:303
  22.5 5.4 %collective-permute-start.2 = (f32[16,128]{1,0:T(8,128)S(1)}, f32[16,128]{1,0:T(8,128)S(1)}, u32[]{:S(2)}, u32[]{:S(2)}) collective-permute-start(f32[16,128]{1,0:T(8,128)S(1)} %concatenate.9), channel_id=1, source_target_pairs={{0,12},{4,14},{8,10},{12,6},{14,2},{10,0},{6,4},{2,8},{1,13},{5,15... | collective-permute-start | bytes 24584 | tf_op jit(solution)/shard_map/ppermute | solution.py:303
  28.0 5.6 %collective-permute-start.28 = (bf16[64,1024]{1,0:T(8,128)(2,1)S(1)}, bf16[64,1024]{1,0:T(8,128)(2,1)S(1)}, u32[]{:S(2)}, u32[]{:S(2)}) collective-permute-start(bf16[64,1024]{1,0:T(8,128)(2,1)S(1)} %constant_dynamic-slice_fusion.refs_18_), channel_id=1, source_target_pairs={{0,16},{16,0},{1,17},{17,1},{2,18},{18,2},{3,19},{19,3},{4,20},{20... | collective-permute-start | bytes 393224 | tf_op jit(solution)/shard_map/ppermute | solution.py:93
  29.5 6.0 %collective-permute-start.25 = (bf16[64,1024]{1,0:T(8,128)(2,1)S(1)}, bf16[64,1024]{1,0:T(8,128)(2,1)S(1)}, u32[]{:S(2)}, u32[]{:S(2)}) collective-permute-start(bf16[64,1024]{1,0:T(8,128)(2,1)S(1)} %constant_dynamic-slice_fusion.refs_18_), channel_id=1, source_target_pairs={{0,2},{4,0},{8,4},{12,8},{14,12},{10,14},{6,10},{2,6},{1,3},{5,1},... | collective-permute-start | bytes 393224 | tf_op jit(solution)/shard_map/ppermute | solution.py:89
  31.4 5.2 %collective-permute-start.21 = (bf16[64,1024]{1,0:T(8,128)(2,1)S(1)}, bf16[64,1024]{1,0:T(8,128)(2,1)S(1)}, u32[]{:S(2)}, u32[]{:S(2)}) collective-permute-start(bf16[64,1024]{1,0:T(8,128)(2,1)S(1)} %constant_dynamic-slice_fusion.refs_18_), channel_id=1, source_target_pairs={{0,4},{4,8},{8,12},{12,14},{14,10},{10,6},{6,2},{2,0},{1,5},{5,9},... | collective-permute-start | bytes 393224 | tf_op jit(solution)/shard_map/ppermute | solution.py:85
  31.5 6.3 %collective-permute-start.14 = (bf16[64,1024]{1,0:T(8,128)(2,1)S(1)}, bf16[64,1024]{1,0:T(8,128)(2,1)S(1)}, u32[]{:S(2)}, u32[]{:S(2)}) collective-permute-start(bf16[64,1024]{1,0:T(8,128)(2,1)S(1)} %get-tuple-element.47.refs_3_), channel_id=1, source_target_pairs={{0,2},{4,0},{8,4},{12,8},{14,12},{10,14},{6,10},{2,6},{1,3},{5,1},... | collective-permute-start | bytes 393224 | tf_op jit(solution)/shard_map/ppermute | solution.py:89
  33.5 6.7 %collective-permute-start.8 = (bf16[64,1024]{1,0:T(8,128)(2,1)S(1)}, bf16[64,1024]{1,0:T(8,128)(2,1)S(1)}, u32[]{:S(2)}, u32[]{:S(2)}) collective-permute-start(bf16[64,1024]{1,0:T(8,128)(2,1)S(1)} %get-tuple-element.47.refs_3_), channel_id=1, source_target_pairs={{0,4},{4,8},{8,12},{12,14},{14,10},{10,6},{6,2},{2,0},{1,5},{5,9},... | collective-permute-start | bytes 393224 | tf_op jit(solution)/shard_map/ppermute | solution.py:85
  33.6 7.6 %collective-permute-start.18 = (bf16[64,1024]{1,0:T(8,128)(2,1)S(1)}, bf16[64,1024]{1,0:T(8,128)(2,1)S(1)}, u32[]{:S(2)}, u32[]{:S(2)}) collective-permute-start(bf16[64,1024]{1,0:T(8,128)(2,1)S(1)} %get-tuple-element.48.refs_2_), channel_id=1, source_target_pairs={{0,2},{4,0},{8,4},{12,8},{14,12},{10,14},{6,10},{2,6},{1,3},{5,1},... | collective-permute-start | bytes 393224 | tf_op jit(solution)/shard_map/ppermute | solution.py:89
  35.5 7.1 %collective-permute-start.7 = (bf16[64,1024]{1,0:T(8,128)(2,1)S(1)}, bf16[64,1024]{1,0:T(8,128)(2,1)S(1)}, u32[]{:S(2)}, u32[]{:S(2)}) collective-permute-start(bf16[64,1024]{1,0:T(8,128)(2,1)S(1)} %get-tuple-element.48.refs_2_), channel_id=1, source_target_pairs={{0,4},{4,8},{8,12},{12,14},{14,10},{10,6},{6,2},{2,0},{1,5},{5,9},... | collective-permute-start | bytes 393224 | tf_op jit(solution)/shard_map/ppermute | solution.py:85
  36.6 8.1 %collective-permute-start.35 = (bf16[64,1024]{1,0:T(8,128)(2,1)S(1)}, bf16[64,1024]{1,0:T(8,128)(2,1)S(1)}, u32[]{:S(2)}, u32[]{:S(2)}) collective-permute-start(bf16[64,1024]{1,0:T(8,128)(2,1)S(1)} %collective-permute-done.25.refs_25_), channel_id=1, source_target_pairs={{0,16},{16,0},{1,17},{17,1},{2,18},{18,2},{3,19},{19,3},{4,20},{20... | collective-permute-start | bytes 393224 | tf_op jit(solution)/shard_map/ppermute | solution.py:93
  37.8 6.9 %collective-permute-start.26 = (bf16[64,1024]{1,0:T(8,128)(2,1)S(1)}, bf16[64,1024]{1,0:T(8,128)(2,1)S(1)}, u32[]{:S(2)}, u32[]{:S(2)}) collective-permute-start(bf16[64,1024]{1,0:T(8,128)(2,1)S(1)} %collective-permute-done.25.refs_25_), channel_id=1, source_target_pairs={{0,2},{4,0},{8,4},{12,8},{14,12},{10,14},{6,10},{2,6},{1,3},{5,1},... | collective-permute-start | bytes 393224 | tf_op jit(solution)/shard_map/ppermute | solution.py:89
  40.2 6.6 %collective-permute-start.29 = (bf16[64,1024]{1,0:T(8,128)(2,1)S(1)}, bf16[64,1024]{1,0:T(8,128)(2,1)S(1)}, u32[]{:S(2)}, u32[]{:S(2)}) collective-permute-start(bf16[64,1024]{1,0:T(8,128)(2,1)S(1)} %collective-permute-done.21.refs_19_), channel_id=1, source_target_pairs={{0,16},{16,0},{1,17},{17,1},{2,18},{18,2},{3,19},{19,3},{4,20},{20... | collective-permute-start | bytes 393224 | tf_op jit(solution)/shard_map/ppermute | solution.py:93
  41.2 6.1 %collective-permute-start.22 = (bf16[64,1024]{1,0:T(8,128)(2,1)S(1)}, bf16[64,1024]{1,0:T(8,128)(2,1)S(1)}, u32[]{:S(2)}, u32[]{:S(2)}) collective-permute-start(bf16[64,1024]{1,0:T(8,128)(2,1)S(1)} %collective-permute-done.21.refs_19_), channel_id=1, source_target_pairs={{0,4},{4,8},{8,12},{12,14},{14,10},{10,6},{6,2},{2,0},{1,5},{5,9},... | collective-permute-start | bytes 393224 | tf_op jit(solution)/shard_map/ppermute | solution.py:85
  42.6 6.4 %collective-permute-start.15 = (bf16[64,1024]{1,0:T(8,128)(2,1)S(1)}, bf16[64,1024]{1,0:T(8,128)(2,1)S(1)}, u32[]{:S(2)}, u32[]{:S(2)}) collective-permute-start(bf16[64,1024]{1,0:T(8,128)(2,1)S(1)} %collective-permute-done.14.refs_17_), channel_id=1, source_target_pairs={{0,2},{4,0},{8,4},{12,8},{14,12},{10,14},{6,10},{2,6},{1,3},{5,1},... | collective-permute-start | bytes 393224 | tf_op jit(solution)/shard_map/ppermute | solution.py:89
  44.8 6.3 %collective-permute-start.10 = (bf16[64,1024]{1,0:T(8,128)(2,1)S(1)}, bf16[64,1024]{1,0:T(8,128)(2,1)S(1)}, u32[]{:S(2)}, u32[]{:S(2)}) collective-permute-start(bf16[64,1024]{1,0:T(8,128)(2,1)S(1)} %collective-permute-done.8.refs_5_), channel_id=1, source_target_pairs={{0,4},{4,8},{8,12},{12,14},{14,10},{10,6},{6,2},{2,0},{1,5},{5,9},... | collective-permute-start | bytes 393224 | tf_op jit(solution)/shard_map/ppermute | solution.py:85
  44.8 7.0 %collective-permute-start.19 = (bf16[64,1024]{1,0:T(8,128)(2,1)S(1)}, bf16[64,1024]{1,0:T(8,128)(2,1)S(1)}, u32[]{:S(2)}, u32[]{:S(2)}) collective-permute-start(bf16[64,1024]{1,0:T(8,128)(2,1)S(1)} %collective-permute-done.18.refs_16_), channel_id=1, source_target_pairs={{0,2},{4,0},{8,4},{12,8},{14,12},{10,14},{6,10},{2,6},{1,3},{5,1},... | collective-permute-start | bytes 393224 | tf_op jit(solution)/shard_map/ppermute | solution.py:89
  46.8 7.1 %collective-permute-start.9 = (bf16[64,1024]{1,0:T(8,128)(2,1)S(1)}, bf16[64,1024]{1,0:T(8,128)(2,1)S(1)}, u32[]{:S(2)}, u32[]{:S(2)}) collective-permute-start(bf16[64,1024]{1,0:T(8,128)(2,1)S(1)} %collective-permute-done.7.refs_4_), channel_id=1, source_target_pairs={{0,4},{4,8},{8,12},{12,14},{14,10},{10,6},{6,2},{2,0},{1,5},{5,9},... | collective-permute-start | bytes 393224 | tf_op jit(solution)/shard_map/ppermute | solution.py:85
  47.2 7.6 %collective-permute-start.34 = (bf16[64,1024]{1,0:T(8,128)(2,1)S(1)}, bf16[64,1024]{1,0:T(8,128)(2,1)S(1)}, u32[]{:S(2)}, u32[]{:S(2)}) collective-permute-start(bf16[64,1024]{1,0:T(8,128)(2,1)S(1)} %collective-permute-done.26.refs_24_), channel_id=1, source_target_pairs={{0,16},{16,0},{1,17},{17,1},{2,18},{18,2},{3,19},{19,3},{4,20},{20... | collective-permute-start | bytes 393224 | tf_op jit(solution)/shard_map/ppermute | solution.py:93
  49.0 6.9 %collective-permute-start.27 = (bf16[64,1024]{1,0:T(8,128)(2,1)S(1)}, bf16[64,1024]{1,0:T(8,128)(2,1)S(1)}, u32[]{:S(2)}, u32[]{:S(2)}) collective-permute-start(bf16[64,1024]{1,0:T(8,128)(2,1)S(1)} %collective-permute-done.26.refs_24_), channel_id=1, source_target_pairs={{0,2},{4,0},{8,4},{12,8},{14,12},{10,14},{6,10},{2,6},{1,3},{5,1},... | collective-permute-start | bytes 393224 | tf_op jit(solution)/shard_map/ppermute | solution.py:89
  51.1 5.8 %collective-permute-start.30 = (bf16[64,1024]{1,0:T(8,128)(2,1)S(1)}, bf16[64,1024]{1,0:T(8,128)(2,1)S(1)}, u32[]{:S(2)}, u32[]{:S(2)}) collective-permute-start(bf16[64,1024]{1,0:T(8,128)(2,1)S(1)} %collective-permute-done.22.refs_20_), channel_id=1, source_target_pairs={{0,16},{16,0},{1,17},{17,1},{2,18},{18,2},{3,19},{19,3},{4,20},{20... | collective-permute-start | bytes 393224 | tf_op jit(solution)/shard_map/ppermute | solution.py:93
  51.8 6.3 %collective-permute-start.23 = (bf16[64,1024]{1,0:T(8,128)(2,1)S(1)}, bf16[64,1024]{1,0:T(8,128)(2,1)S(1)}, u32[]{:S(2)}, u32[]{:S(2)}) collective-permute-start(bf16[64,1024]{1,0:T(8,128)(2,1)S(1)} %collective-permute-done.22.refs_20_), channel_id=1, source_target_pairs={{0,4},{4,8},{8,12},{12,14},{14,10},{10,6},{6,2},{2,0},{1,5},{5,9},... | collective-permute-start | bytes 393224 | tf_op jit(solution)/shard_map/ppermute | solution.py:85
  53.9 5.9 %collective-permute-start.16 = (bf16[64,1024]{1,0:T(8,128)(2,1)S(1)}, bf16[64,1024]{1,0:T(8,128)(2,1)S(1)}, u32[]{:S(2)}, u32[]{:S(2)}) collective-permute-start(bf16[64,1024]{1,0:T(8,128)(2,1)S(1)} %collective-permute-done.15.refs_15_), channel_id=1, source_target_pairs={{0,2},{4,0},{8,4},{12,8},{14,12},{10,14},{6,10},{2,6},{1,3},{5,1},... | collective-permute-start | bytes 393224 | tf_op jit(solution)/shard_map/ppermute | solution.py:89
  54.9 5.5 %collective-permute-start.12 = (bf16[64,1024]{1,0:T(8,128)(2,1)S(1)}, bf16[64,1024]{1,0:T(8,128)(2,1)S(1)}, u32[]{:S(2)}, u32[]{:S(2)}) collective-permute-start(bf16[64,1024]{1,0:T(8,128)(2,1)S(1)} %collective-permute-done.10.refs_7_), channel_id=1, source_target_pairs={{0,4},{4,8},{8,12},{12,14},{14,10},{10,6},{6,2},{2,0},{1,5},{5,9},... | collective-permute-start | bytes 393224 | tf_op jit(solution)/shard_map/ppermute | solution.py:85
  55.9 6.0 %collective-permute-start.20 = (bf16[64,1024]{1,0:T(8,128)(2,1)S(1)}, bf16[64,1024]{1,0:T(8,128)(2,1)S(1)}, u32[]{:S(2)}, u32[]{:S(2)}) collective-permute-start(bf16[64,1024]{1,0:T(8,128)(2,1)S(1)} %collective-permute-done.19.refs_14_), channel_id=1, source_target_pairs={{0,2},{4,0},{8,4},{12,8},{14,12},{10,14},{6,10},{2,6},{1,3},{5,1},... | collective-permute-start | bytes 393224 | tf_op jit(solution)/shard_map/ppermute | solution.py:89
  56.9 5.9 %collective-permute-start.11 = (bf16[64,1024]{1,0:T(8,128)(2,1)S(1)}, bf16[64,1024]{1,0:T(8,128)(2,1)S(1)}, u32[]{:S(2)}, u32[]{:S(2)}) collective-permute-start(bf16[64,1024]{1,0:T(8,128)(2,1)S(1)} %collective-permute-done.9.refs_6_), channel_id=1, source_target_pairs={{0,4},{4,8},{8,12},{12,14},{14,10},{10,6},{6,2},{2,0},{1,5},{5,9},... | collective-permute-start | bytes 393224 | tf_op jit(solution)/shard_map/ppermute | solution.py:85
  58.1 5.9 %collective-permute-start.24 = (bf16[64,1024]{1,0:T(8,128)(2,1)S(1)}, bf16[64,1024]{1,0:T(8,128)(2,1)S(1)}, u32[]{:S(2)}, u32[]{:S(2)}) collective-permute-start(bf16[64,1024]{1,0:T(8,128)(2,1)S(1)} %collective-permute-done.23.refs_21_), channel_id=1, source_target_pairs={{0,4},{4,8},{8,12},{12,14},{14,10},{10,6},{6,2},{2,0},{1,5},{5,9},... | collective-permute-start | bytes 393224 | tf_op jit(solution)/shard_map/ppermute | solution.py:85
  59.8 7.6 %collective-permute-start.31 = (bf16[64,1024]{1,0:T(8,128)(2,1)S(1)}, bf16[64,1024]{1,0:T(8,128)(2,1)}, u32[]{:S(2)}, u32[]{:S(2)}) collective-permute-start(bf16[64,1024]{1,0:T(8,128)(2,1)S(1)} %collective-permute-done.23.refs_21_), channel_id=1, source_target_pairs={{0,16},{16,0},{1,17},{17,1},{2,18},{18,2},{3,19},{19,3},{4,20},{20... | collective-permute-start | bytes 393224 | tf_op jit(solution)/shard_map/ppermute | solution.py:93
  60.4 7.0 %collective-permute-start.33 = (bf16[64,1024]{1,0:T(8,128)(2,1)S(1)}, bf16[64,1024]{1,0:T(8,128)(2,1)}, u32[]{:S(2)}, u32[]{:S(2)}) collective-permute-start(bf16[64,1024]{1,0:T(8,128)(2,1)S(1)} %collective-permute-done.27.refs_23_), channel_id=1, source_target_pairs={{0,16},{16,0},{1,17},{17,1},{2,18},{18,2},{3,19},{19,3},{4,20},{20... | collective-permute-start | bytes 393224 | tf_op jit(solution)/shard_map/ppermute | solution.py:93
  61.9 5.5 %collective-permute-start.17 = (bf16[64,1024]{1,0:T(8,128)(2,1)S(1)}, bf16[64,1024]{1,0:T(8,128)(2,1)}, u32[]{:S(2)}, u32[]{:S(2)}) collective-permute-start(bf16[64,1024]{1,0:T(8,128)(2,1)S(1)} %collective-permute-done.16.refs_13_), channel_id=1, source_target_pairs={{0,2},{4,0},{8,4},{12,8},{14,12},{10,14},{6,10},{2,6},{1,3},{5,1},... | collective-permute-start | bytes 393224 | tf_op jit(solution)/shard_map/ppermute | solution.py:89
  62.8 5.1 %collective-permute-start.13 = (bf16[64,1024]{1,0:T(8,128)(2,1)S(1)}, bf16[64,1024]{1,0:T(8,128)(2,1)}, u32[]{:S(2)}, u32[]{:S(2)}) collective-permute-start(bf16[64,1024]{1,0:T(8,128)(2,1)S(1)} %collective-permute-done.11.refs_8_), channel_id=1, source_target_pairs={{0,4},{4,8},{8,12},{12,14},{14,10},{10,6},{6,2},{2,0},{1,5},{5,9},... | collective-permute-start | bytes 393224 | tf_op jit(solution)/shard_map/ppermute | solution.py:85
  102.9 5.1 %collective-permute-start.38 = (bf16[4,128,1024]{2,1,0:T(8,128)(2,1)S(1)}, bf16[4,128,1024]{2,1,0:T(8,128)(2,1)S(1)}, u32[]{:S(2)}, u32[]{:S(2)}) collective-permute-start(bf16[4,128,1024]{2,1,0:T(8,128)(2,1)S(1)} %shard_map.112.refs_2_), channel_id=1, source_target_pairs={{0,1},{1,0},{2,3},{3,2},{4,5},{5,4},{6,7},{7,6},{8,9},{9,8},{10,11... | collective-permute-start | bytes 3145736 | tf_op jit(solution)/shard_map/ppermute | solution.py:93
  103.0 6.6 %collective-permute-start.39 = (bf16[4,128,1024]{2,1,0:T(8,128)(2,1)S(1)}, bf16[4,128,1024]{2,1,0:T(8,128)(2,1)S(1)}, u32[]{:S(2)}, u32[]{:S(2)}) collective-permute-start(bf16[4,128,1024]{2,1,0:T(8,128)(2,1)S(1)} %shard_map.113.refs_3_), channel_id=1, source_target_pairs={{0,1},{1,0},{2,3},{3,2},{4,5},{5,4},{6,7},{7,6},{8,9},{9,8},{10,11... | collective-permute-start | bytes 3145736 | tf_op jit(solution)/shard_map/ppermute | solution.py:93
  118.4 10.3 %collective-permute-start.40 = (bf16[128,512]{1,0:T(8,128)(2,1)S(1)}, bf16[128,512]{1,0:T(8,128)(2,1)S(1)}, u32[]{:S(2)}, u32[]{:S(2)}) collective-permute-start(bf16[128,512]{1,0:T(8,128)(2,1)S(1)} %get-tuple-element.27), channel_id=1, source_target_pairs={{0,2},{4,0},{8,4},{12,8},{14,12},{10,14},{6,10},{2,6},{1,3},{5,1},... | collective-permute-start | bytes 393224 | tf_op jit(solution)/shard_map/ppermute | solution.py:89
  119.6 10.4 %collective-permute-start.44 = (bf16[128,512]{1,0:T(8,128)(2,1)S(1)}, bf16[128,512]{1,0:T(8,128)(2,1)S(1)}, u32[]{:S(2)}, u32[]{:S(2)}) collective-permute-start(bf16[128,512]{1,0:T(8,128)(2,1)S(1)} %get-tuple-element.31), channel_id=1, source_target_pairs={{0,4},{4,8},{8,12},{12,14},{14,10},{10,6},{6,2},{2,0},{1,5},{5,9},... | collective-permute-start | bytes 393224 | tf_op jit(solution)/shard_map/ppermute | solution.py:85
  126.6 6.3 %collective-permute-start.47 = (bf16[128,512]{1,0:T(8,128)(2,1)S(1)}, bf16[128,512]{1,0:T(8,128)(2,1)S(1)}, u32[]{:S(2)}, u32[]{:S(2)}) collective-permute-start(bf16[128,512]{1,0:T(8,128)(2,1)S(1)} %get-tuple-element.36), channel_id=1, source_target_pairs={{0,2},{4,0},{8,4},{12,8},{14,12},{10,14},{6,10},{2,6},{1,3},{5,1},... | collective-permute-start | bytes 393224 | tf_op jit(solution)/shard_map/ppermute | solution.py:89
  127.8 6.4 %collective-permute-start.50 = (bf16[128,512]{1,0:T(8,128)(2,1)S(1)}, bf16[128,512]{1,0:T(8,128)(2,1)S(1)}, u32[]{:S(2)}, u32[]{:S(2)}) collective-permute-start(bf16[128,512]{1,0:T(8,128)(2,1)S(1)} %get-tuple-element.39), channel_id=1, source_target_pairs={{0,4},{4,8},{8,12},{12,14},{14,10},{10,6},{6,2},{2,0},{1,5},{5,9},... | collective-permute-start | bytes 393224 | tf_op jit(solution)/shard_map/ppermute | solution.py:85
  128.7 7.0 %collective-permute-start.41 = (bf16[128,512]{1,0:T(8,128)(2,1)S(1)}, bf16[128,512]{1,0:T(8,128)(2,1)S(1)}, u32[]{:S(2)}, u32[]{:S(2)}) collective-permute-start(bf16[128,512]{1,0:T(8,128)(2,1)S(1)} %add_convert_fusion.11), channel_id=1, source_target_pairs={{0,2},{4,0},{8,4},{12,8},{14,12},{10,14},{6,10},{2,6},{1,3},{5,1},... | collective-permute-start | bytes 393224 | tf_op jit(solution)/shard_map/ppermute | solution.py:89
  130.0 7.0 %collective-permute-start.45 = (bf16[128,512]{1,0:T(8,128)(2,1)S(1)}, bf16[128,512]{1,0:T(8,128)(2,1)S(1)}, u32[]{:S(2)}, u32[]{:S(2)}) collective-permute-start(bf16[128,512]{1,0:T(8,128)(2,1)S(1)} %add_convert_fusion.8), channel_id=1, source_target_pairs={{0,4},{4,8},{8,12},{12,14},{14,10},{10,6},{6,2},{2,0},{1,5},{5,9},... | collective-permute-start | bytes 393224 | tf_op jit(solution)/shard_map/ppermute | solution.py:85
  132.9 6.0 %collective-permute-start.48 = (bf16[128,512]{1,0:T(8,128)(2,1)S(1)}, bf16[128,512]{1,0:T(8,128)(2,1)S(1)}, u32[]{:S(2)}, u32[]{:S(2)}) collective-permute-start(bf16[128,512]{1,0:T(8,128)(2,1)S(1)} %add_convert_fusion.5), channel_id=1, source_target_pairs={{0,2},{4,0},{8,4},{12,8},{14,12},{10,14},{6,10},{2,6},{1,3},{5,1},... | collective-permute-start | bytes 393224 | tf_op jit(solution)/shard_map/ppermute | solution.py:89
  134.2 5.9 %collective-permute-start.51 = (bf16[128,512]{1,0:T(8,128)(2,1)S(1)}, bf16[128,512]{1,0:T(8,128)(2,1)S(1)}, u32[]{:S(2)}, u32[]{:S(2)}) collective-permute-start(bf16[128,512]{1,0:T(8,128)(2,1)S(1)} %add_convert_fusion.3), channel_id=1, source_target_pairs={{0,4},{4,8},{8,12},{12,14},{14,10},{10,6},{6,2},{2,0},{1,5},{5,9},... | collective-permute-start | bytes 393224 | tf_op jit(solution)/shard_map/ppermute | solution.py:85
  135.7 6.3 %collective-permute-start.42 = (bf16[128,512]{1,0:T(8,128)(2,1)S(1)}, bf16[128,512]{1,0:T(8,128)(2,1)S(1)}, u32[]{:S(2)}, u32[]{:S(2)}) collective-permute-start(bf16[128,512]{1,0:T(8,128)(2,1)S(1)} %add_convert_fusion.10), channel_id=1, source_target_pairs={{0,2},{4,0},{8,4},{12,8},{14,12},{10,14},{6,10},{2,6},{1,3},{5,1},... | collective-permute-start | bytes 393224 | tf_op jit(solution)/shard_map/ppermute | solution.py:89
  137.0 9.9 %collective-permute-start.46 = (bf16[128,512]{1,0:T(8,128)(2,1)S(1)}, bf16[128,512]{1,0:T(8,128)(2,1)S(1)}, u32[]{:S(2)}, u32[]{:S(2)}) collective-permute-start(bf16[128,512]{1,0:T(8,128)(2,1)S(1)} %add_convert_fusion.7), channel_id=1, source_target_pairs={{0,4},{4,8},{8,12},{12,14},{14,10},{10,6},{6,2},{2,0},{1,5},{5,9},... | collective-permute-start | bytes 393224 | tf_op jit(solution)/shard_map/ppermute | solution.py:85
  139.0 8.2 %collective-permute-start.49 = (bf16[128,512]{1,0:T(8,128)(2,1)S(1)}, bf16[128,512]{1,0:T(8,128)(2,1)S(1)}, u32[]{:S(2)}, u32[]{:S(2)}) collective-permute-start(bf16[128,512]{1,0:T(8,128)(2,1)S(1)} %add_convert_fusion.4), channel_id=1, source_target_pairs={{0,2},{4,0},{8,4},{12,8},{14,12},{10,14},{6,10},{2,6},{1,3},{5,1},... | collective-permute-start | bytes 393224 | tf_op jit(solution)/shard_map/ppermute | solution.py:89
  140.1 5.7 %collective-permute-start.52 = (bf16[128,512]{1,0:T(8,128)(2,1)S(1)}, bf16[128,512]{1,0:T(8,128)(2,1)S(1)}, u32[]{:S(2)}, u32[]{:S(2)}) collective-permute-start(bf16[128,512]{1,0:T(8,128)(2,1)S(1)} %add_convert_fusion.2), channel_id=1, source_target_pairs={{0,4},{4,8},{8,12},{12,14},{14,10},{10,6},{6,2},{2,0},{1,5},{5,9},... | collective-permute-start | bytes 393224 | tf_op jit(solution)/shard_map/ppermute | solution.py:85
  (16 other events, 100.2 us)

commit v2 on v0

v2 whole, which is shorter than its diff:
```python
import functools
import math

import jax
import jax.numpy as jnp
from jax import lax
from jax.experimental import pallas as pl
from jax.experimental.pallas import tpu as pltpu
from jax.sharding import PartitionSpec as P

EXPERTS = 64
TOP = 6
CAP = 16
F32 = jnp.float32
BF16 = jnp.bfloat16
RING = (0, 2, 4, 6, 7, 5, 3, 1)
NR = 8
VMEM_LIMIT = 46 << 20
VMEM_SMALL = 14 << 20
FETCH_LIMITS = (40, 33, 24, 16)
ANY = pl.BlockSpec(memory_space=pl.ANY)
VM = pl.BlockSpec(memory_space=pltpu.VMEM)


def activate(tiles):
    return jax.nn.gelu(tiles.astype(F32), approximate=False).astype(BF16)


def round_keep(values):
    return lax.optimization_barrier(values.astype(BF16)).astype(F32)


def on_device_plain(
    tile_hidden, cached_rows, tile_image, cache_ids, adapter_weight, routes, route_gates, gate_up, expert_down
):
    slot_count, tile_rows, adapt_width = tile_hidden.shape
    half_width = cached_rows.shape[1]
    cache_hit = jnp.any(tile_image[:, None] == cache_ids[None, :], axis=1)
    whole_weight = lax.all_gather(adapter_weight, "wide", axis=0, tiled=True)
    active = activate(tile_hidden).reshape(slot_count * tile_rows, adapt_width)
    encoded = jnp.dot(active, whole_weight, preferred_element_type=F32).astype(BF16)
    token_count = slot_count * tile_rows
    hit_rows = jnp.repeat(cache_hit, tile_rows)
    tokens_in = jnp.where(hit_rows[:, None], cached_rows, encoded)
    expert_flat = routes.reshape(-1)
    pair_count = expert_flat.shape[0]
    onehot = (expert_flat[:, None] == jnp.arange(EXPERTS, dtype=jnp.int32)[None, :]).astype(jnp.int32)
    earlier = jnp.cumsum(onehot, axis=0) - onehot
    slot_index = jnp.sum(earlier * onehot, axis=1)
    target = expert_flat * CAP + slot_index
    owner_table = (
        jnp.full((EXPERTS * CAP,), token_count, jnp.int32)
        .at[target]
        .set(jnp.arange(pair_count, dtype=jnp.int32) // TOP)
    )
    padded_tokens = jnp.concatenate([tokens_in, jnp.zeros((1, half_width), BF16)])
    expert_rows = padded_tokens[owner_table].reshape(EXPERTS, CAP, half_width)
    local_halves = gate_up.shape[0]
    outgoing = jnp.broadcast_to(expert_rows[:, None], (EXPERTS, 2, CAP, half_width)).reshape(
        2 * EXPERTS, CAP, half_width
    )
    arrived = lax.all_to_all(outgoing, "wide", split_axis=0, concat_axis=1, tiled=True)
    inner_width = gate_up.shape[3]
    preact_local = jnp.einsum(
        "lrd,ldf->lrf",
        arrived,
        gate_up.reshape(local_halves, half_width, 2 * inner_width),
        preferred_element_type=F32,
    )
    rounded = round_keep(preact_local)
    summed = lax.psum(rounded.astype(BF16), "narrow").astype(F32)
    hidden = (jax.nn.silu(summed[:, :, :inner_width]) * summed[:, :, inner_width:]).astype(BF16)
    partial_out = jnp.einsum("lrf,lfd->lrd", hidden, expert_down, preferred_element_type=F32).astype(BF16)
    returned = lax.all_to_all(partial_out, "wide", split_axis=1, concat_axis=0, tiled=True)
    both_halves = returned.reshape(EXPERTS, 2, CAP, half_width).astype(F32)
    summed_rows = round_keep(both_halves[:, 0] + both_halves[:, 1]).reshape(EXPERTS * CAP, half_width)
    picked = summed_rows[target].reshape(token_count, TOP, half_width)
    mixed = jnp.sum(picked * route_gates[:, :, None], axis=1)
    return mixed.astype(BF16)


def ring_pairs(shift):
    return [(RING[i], RING[(i + shift) % NR]) for i in range(NR)]


def from_prev(value):
    return lax.ppermute(value, "wide", ring_pairs(1))


def from_next(value):
    return lax.ppermute(value, "wide", ring_pairs(-1))


def swap(value, axis):
    return lax.ppermute(value, axis, [(0, 1), (1, 0)])


def tie(*values):
    return lax.optimization_barrier(values)


def ring_gather_two(first, make_second, fetches):
    one, two = [first] * NR, [None] * NR
    fetched = []
    far = NR // 2
    for q in range(1, far + 1):
        up, down = one[q - 1], one[(NR - q + 1) % NR]
        if q > 2:
            up, down, two[q - 2], two[NR - q + 2] = tie(up, down, two[q - 2], two[NR - q + 2])
        if q < far:
            one[q], one[NR - q] = from_prev(up), from_next(down)
        else:
            one[q] = from_next(down)
        if q == 1:
            two[0], one[1], one[NR - 1] = make_second(one[1], one[NR - 1])
        up, down = two[q - 1], two[(NR - q + 1) % NR]
        if q > 1:
            up, down, one[q], one[NR - q], *fetched = tie(up, down, one[q], one[NR - q], *fetched)
        if q < far:
            two[q], two[NR - q] = from_prev(up), from_next(down)
            if fetches:
                fetched.append(fetches.pop(0)())
        else:
            two[q] = from_prev(up)
            fetched += [make() for make in fetches]
    return one, two, fetched


def add(left, right):
    return (left.astype(F32) + right.astype(F32)).astype(BF16)


def ring_scatter(parts, antipode_by_next):
    if antipode_by_next:
        low = add(from_next(parts[4]), parts[3])
        high = parts[5]
    else:
        low = parts[3]
        high = add(from_prev(parts[4]), parts[5])
    for q in (2, 1, 0):
        low = from_next(low)
        high = from_prev(high)
        if q:
            low = add(low, parts[q])
            high = add(high, parts[NR - q])
    return (parts[0].astype(F32) + low.astype(F32) + high.astype(F32)).astype(BF16)


def ring_source(q):
    wide_id = lax.axis_index("wide")
    level = wide_id // 2
    pos = jnp.where(wide_id % 2 == 1, NR - 1 - level, level)
    pos = (pos + NR - q) % NR
    return jnp.where(pos < NR // 2, 2 * pos, 2 * (NR - 1 - pos) + 1)


def prologue_kernel(experts, slots, tile_rows, *refs):
    toks = slots * tile_rows
    sent_in, weight_in, gate_up = refs[:NR], refs[NR : 2 * NR], refs[2 * NR : -11]
    rows_out, mix_out, pre_out, sent, weight, packed, rows_here, missed_at, sent_sem, weight_sem = refs[-10:]
    near = rows_here.shape[0]
    shard = weight_in[0].shape[0]
    width = packed.shape[2]
    sent_copies = [pltpu.make_async_copy(ref, sent.at[q], sent_sem.at[q]) for q, ref in enumerate(sent_in)]
    copies = []
    for q, ref in enumerate(weight_in):
        at = pl.multiple_of(ring_source(q) * shard, shard)
        copies.append(pltpu.make_async_copy(ref, weight.at[pl.ds(at, shard)], weight_sem.at[q]))
    for copy in sent_copies + copies:
        copy.start()

    first = (lax.axis_index("wide") * experts).astype(F32)
    before = lax.broadcasted_iota(jnp.int32, (toks, toks), 0) < lax.broadcasted_iota(jnp.int32, (toks, toks), 1)
    before = before.astype(F32).astype(BF16)
    ids = lax.broadcasted_iota(jnp.int32, (experts, toks), 0).astype(F32) + first
    place = lax.broadcasted_iota(jnp.int32, (experts, CAP, toks), 1).astype(F32)
    picks = []
    missed = jnp.int32(0)
    for q in range(NR):
        sent_copies[q].wait()
        info = sent[q, toks:].astype(F32)
        for s in range(slots):
            flag = info[TOP + s, 0] > 0.5
            missed_at[missed] = q * slots + s
            missed = missed + flag.astype(jnp.int32)
        named = jnp.zeros((experts, toks), F32)
        gate = jnp.zeros((experts, toks), F32)
        for k in range(TOP):
            same = jnp.broadcast_to(info[k : k + 1, :toks], (experts, toks)) == ids
            named = jnp.where(same, 1.0, named)
            value = info[k : k + 1, toks : 2 * toks] + info[k : k + 1, 2 * toks : 3 * toks]
            value = value + info[k : k + 1, 3 * toks : 4 * toks]
            gate = jnp.where(same, jnp.broadcast_to(value, (experts, toks)), gate)
        rank = jnp.dot(named.astype(BF16), before, preferred_element_type=F32)
        rank = jnp.where(named > 0.0, rank, -1.0)
        chosen = jnp.broadcast_to(rank[:, None, :], (experts, CAP, toks)) == place
        pick = jnp.where(chosen, 1.0, 0.0).reshape(experts * CAP, toks)
        picks.append(pick.astype(BF16))
        gated = jnp.where(chosen, jnp.broadcast_to(gate[:, None, :], (experts, CAP, toks)), 0.0)
        gated = gated.reshape(experts * CAP, toks)
        coarse = gated.astype(BF16)
        mix_out[q, 0] = coarse
        mix_out[q, 1] = (gated - coarse.astype(F32)).astype(BF16)

    most = packed.shape[0]

    def tile_of(i):
        n = missed_at[i]
        return sent.at[n // slots, pl.ds(pl.multiple_of((n % slots) * tile_rows, tile_rows), tile_rows)]

    for i in range(most):

        @pl.when(i < missed)
        def _(i=i):
            packed[i] = tile_of(i)[...]

    for copy in copies:
        copy.wait()

    group = 4
    for i in range(0, most, group):

        @pl.when(i < missed)
        def _(i=i):
            rows = packed[i : i + group].reshape(group * tile_rows, width)
            coded = jnp.dot(rows, weight[...], preferred_element_type=F32).astype(BF16)
            for j in range(group):

                @pl.when(i + j < missed)
                def _(j=j):
                    tile_of(i + j)[...] = coded[j * tile_rows : (j + 1) * tile_rows]

    for q in range(NR):
        rows = jnp.dot(picks[q], sent[q, :toks], preferred_element_type=F32).astype(BF16)
        rows = rows.reshape(experts, CAP, width)
        rows_here[:, q * CAP : (q + 1) * CAP, :] = rows[:near]
        rows_out[:, q * CAP : (q + 1) * CAP, :] = rows[near:]
    first_matmuls(rows_here, gate_up, pre_out)


def first_matmuls(rows, weights, out):
    per = weights[0].shape[0]
    for h in range(out.shape[0]):
        out[h] = jnp.dot(rows[h // 2], weights[h // per][h % per], preferred_element_type=F32).astype(BF16)


def fetch_kernel(base, gate_up, out, buf, sem):
    halves, width, _ = out.shape
    inner = gate_up.shape[3]
    copies = [pltpu.make_async_copy(gate_up.at[base + h], buf.at[h], sem.at[h]) for h in range(halves)]
    for copy in copies:
        copy.start()
    rows = 128
    dst = lax.broadcasted_iota(jnp.int32, (2 * rows, 2 * rows), 0)
    src = lax.broadcasted_iota(jnp.int32, (2 * rows, 2 * rows), 1)
    parting = (src == jnp.where(dst < rows, 2 * dst, 2 * (dst - rows) + 1)).astype(F32).astype(BF16)
    for h in range(halves):
        copies[h].wait()
        for k in range(0, width, rows):
            mixed = buf[h, k : k + rows].reshape(2 * rows, inner)
            parted = jnp.dot(parting, mixed, preferred_element_type=F32).astype(BF16)
            out[h, k : k + rows, :inner] = parted[:rows]
            out[h, k : k + rows, inner:] = parted[rows:]


def first_kernel(rows, *refs):
    first_matmuls(rows, refs[:-1], refs[-1])


def gated_hidden(own, other):
    pre = own.astype(F32) + other.astype(F32)
    inner = pre.shape[1] // 2
    gate, up = pre[:, :inner], pre[:, inner:]
    return (gate / (1.0 + jnp.exp(-gate)) * up).astype(BF16)


def second_near_kernel(own, other, down, pairs, wbuf, sem):
    experts = pairs.shape[0]
    copies = [
        pltpu.make_async_copy(down.at[pl.ds(2 * e, 2)], wbuf.at[pl.ds(2 * e, 2)], sem.at[e]) for e in range(experts)
    ]
    for copy in copies:
        copy.start()
    for e in range(experts):
        hidden = [gated_hidden(own[h], other[h]) for h in (2 * e, 2 * e + 1)]
        copies[e].wait()
        acc = jnp.dot(hidden[0], wbuf[2 * e], preferred_element_type=F32)
        acc += jnp.dot(hidden[1], wbuf[2 * e + 1], preferred_element_type=F32)
        pairs[e] = acc.astype(BF16)


def second_far_kernel(base, chunk, width, *refs):
    if len(refs) == 5 + NR + 4:
        own, other, near_pairs, mix, down, hidden = refs[:6]
        outs = refs[6 : 6 + NR]
    else:
        hidden, near_pairs, mix, down = refs[:4]
        outs = refs[4 : 4 + NR]
        own = None
    pairs, wbuf, sem = refs[-3:]
    experts = pairs.shape[0]
    at = chunk * width
    copies = [
        pltpu.make_async_copy(
            down.at[pl.ds(base + 2 * e, 2), :, pl.ds(at, width)], wbuf.at[pl.ds(2 * e, 2)], sem.at[e]
        )
        for e in range(experts)
    ]
    for copy in copies:
        copy.start()
    if own is not None:
        for h in range(2 * experts):
            hidden[h] = gated_hidden(own[h], other[h])
    for e in range(experts):
        copies[e].wait()
        acc = jnp.dot(hidden[2 * e], wbuf[2 * e], preferred_element_type=F32)
        acc += jnp.dot(hidden[2 * e + 1], wbuf[2 * e + 1], preferred_element_type=F32)
        pairs[e] = acc.astype(BF16)
    dims = (((0,), (0,)), ((), ()))
    near = near_pairs.shape[0]
    for q in range(NR):
        span = slice(q * CAP, (q + 1) * CAP)
        rows = jnp.concatenate([near_pairs[:, span, at : at + width], pairs[:, span, :]], axis=0)
        rows = rows.reshape((near + experts) * CAP, width)
        total = lax.dot_general(mix[q, 0], rows, dims, preferred_element_type=F32)
        total += lax.dot_general(mix[q, 1], rows, dims, preferred_element_type=F32)
        outs[q][...] = total.astype(BF16)


def split3(values):
    high = values.astype(BF16)
    rest = values - high.astype(F32)
    middle = rest.astype(BF16)
    return high, middle, (rest - middle.astype(F32)).astype(BF16)


def on_device_ring(
    tile_hidden, cached_rows, tile_image, cache_ids, adapter_weight, routes, route_gates, gate_up, expert_down
):
    slots, tile_rows, adapt_width = tile_hidden.shape
    toks = slots * tile_rows
    half_width = cached_rows.shape[1]
    halves, _, _, inner = gate_up.shape
    experts = halves // 2
    shard = adapter_weight.shape[0]
    params = pltpu.CompilerParams(vmem_limit_bytes=VMEM_LIMIT)

    def message(*passing):
        hidden, *passing = tie(tile_hidden, *passing)
        cache_hit = jnp.any(tile_image[:, None] == cache_ids[None, :], axis=1)
        tokens_own = jnp.where(
            cache_hit[:, None, None], cached_rows.reshape(slots, tile_rows, half_width), activate(hidden)
        ).reshape(toks, half_width)
        flags = jnp.broadcast_to(jnp.where(cache_hit, 0.0, 1.0).astype(BF16)[:, None], (slots, toks))
        info_own = jnp.concatenate([routes.T.astype(BF16), flags, jnp.zeros((16 - TOP - slots, toks), BF16)])
        gates = [jnp.pad(piece, ((0, 16 - TOP), (0, 0))) for piece in split3(route_gates.T)]
        info_own = jnp.concatenate([info_own] + gates, axis=1)
        info_own = jnp.pad(info_own, ((0, 0), (0, half_width - 4 * toks)))
        return jnp.concatenate([tokens_own, info_own]), *passing

    def fetch(base, count, limit):
        shape = (count, half_width, 2 * inner)
        return pl.pallas_call(
            functools.partial(fetch_kernel, base),
            in_specs=[ANY],
            out_specs=VM,
            out_shape=jax.ShapeDtypeStruct(shape, BF16),
            scratch_shapes=[
                pltpu.VMEM((count, half_width, 2, inner), BF16),
                pltpu.SemaphoreType.DMA((count,)),
            ],
            compiler_params=pltpu.CompilerParams(vmem_limit_bytes=limit << 20),
            cost_estimate=pl.CostEstimate(
                flops=512 * count * half_width * 2 * inner, bytes_accessed=8 * count * half_width * inner, transcendentals=0
            ),
        )(gate_up)

    near = experts // 2
    far = experts - near
    count = halves // len(FETCH_LIMITS)
    fetches = [functools.partial(fetch, i * count, count, limit) for i, limit in enumerate(FETCH_LIMITS)]
    weight_ring, sent, fetched = ring_gather_two(adapter_weight, message, fetches)
    fetched_near, fetched_far = fetched[: len(fetched) // 2], fetched[len(fetched) // 2 :]
    most = NR * CAP
    pre_shape = jax.ShapeDtypeStruct((2 * near, most, 2 * inner), BF16)
    rows, mix, own_near = pl.pallas_call(
        functools.partial(prologue_kernel, experts, slots, tile_rows),
        in_specs=[ANY] * (2 * NR) + [VM] * len(fetched_near) + [ANY],
        out_specs=[VM, VM, VM],
        out_shape=[
            jax.ShapeDtypeStruct((far, most, half_width), BF16),
            jax.ShapeDtypeStruct((NR, 2, experts * CAP, toks), BF16),
            pre_shape,
        ],
        scratch_shapes=[
            pltpu.VMEM((NR, toks + 16, half_width), BF16),
            pltpu.VMEM((NR * shard, half_width), BF16),
            pltpu.VMEM((NR * slots // 2, tile_rows, half_width), BF16),
            pltpu.VMEM((near, most, half_width), BF16),
            pltpu.SMEM((NR * slots,), jnp.int32),
            pltpu.SemaphoreType.DMA((NR,)),
            pltpu.SemaphoreType.DMA((NR,)),
        ],
        compiler_params=pltpu.CompilerParams(vmem_limit_bytes=VMEM_SMALL),
    )(*sent, *weight_ring, *fetched_near, fetched_far[-1])
    other_near = swap(own_near, "narrow")

    own_far = pl.pallas_call(
        first_kernel,
        in_specs=[VM] * (1 + len(fetched_far)),
        out_specs=VM,
        out_shape=jax.ShapeDtypeStruct((2 * far, most, 2 * inner), BF16),
        compiler_params=pltpu.CompilerParams(vmem_limit_bytes=VMEM_SMALL),
        cost_estimate=pl.CostEstimate(
            flops=16 * most * half_width * far * inner, bytes_accessed=8 * far * half_width * inner, transcendentals=0
        ),
    )(rows, *fetched_far)
    own_far, other_near = tie(own_far, other_near)
    other_far = swap(own_far, "narrow")

    near_pairs = pl.pallas_call(
        second_near_kernel,
        in_specs=[VM, VM, ANY],
        out_specs=VM,
        out_shape=jax.ShapeDtypeStruct((near, most, half_width), BF16),
        scratch_shapes=[pltpu.VMEM((2 * near, inner, half_width), BF16), pltpu.SemaphoreType.DMA((near,))],
        compiler_params=params,
        cost_estimate=pl.CostEstimate(
            flops=4 * near * most * inner * half_width,
            bytes_accessed=4 * near * inner * half_width,
            transcendentals=2 * near * most * inner,
        ),
    )(own_near, other_near, expert_down)
    near_pairs, other_far = tie(near_pairs, other_far)

    n_second = 2
    width = half_width // n_second
    mixed = []
    hidden = None
    for c in range(n_second):
        start = hidden is None
        out = pl.pallas_call(
            functools.partial(second_far_kernel, 2 * near, c, width),
            in_specs=[VM] * (4 if start else 3) + [ANY],
            out_specs=[VM] * (start + NR),
            out_shape=[jax.ShapeDtypeStruct((2 * far, most, inner), BF16)] * start
            + [jax.ShapeDtypeStruct((toks, width), BF16)] * NR,
            scratch_shapes=[
                pltpu.VMEM((far, most, width), BF16),
                pltpu.VMEM((2 * far, inner, width), BF16),
                pltpu.SemaphoreType.DMA((far,)),
            ],
            compiler_params=params,
            cost_estimate=pl.CostEstimate(
                flops=4 * far * most * inner * width, bytes_accessed=4 * far * inner * width, transcendentals=0
            ),
        )(*((own_far, other_far) if start else (hidden,)), near_pairs, mix, expert_down)
        if start:
            hidden, *out = out
        mixed.append(ring_scatter(out, c % 2 == 0))
    return jnp.concatenate(mixed, axis=1)


def solution(mesh):
    body = on_device_ring if mesh.shape["wide"] == NR else on_device_plain
    return jax.shard_map(
        body,
        mesh=mesh,
        in_specs=(
            P(("grp", "wide"), None, None),
            P(("grp", "wide"), "narrow"),
            P(("grp", "wide")),
            P("grp"),
            P("wide", "narrow"),
            P(("grp", "wide"), None),
            P(("grp", "wide"), None),
            P("wide", "narrow", None, None),
            P("wide", None, "narrow"),
        ),
        out_specs=P(("grp", "wide"), "narrow"),
        check_vma=False,
    )
```

time: 374 us -> 112 us (0.30)
  waiting for transfers between devices: 204 us -> 30 us
  local copies, waits for them, and re-layouts: 91.3 us -> 5.76 us
  Pallas kernels: 0 us -> 38.4 us
  matrix products: 31.8 us -> 0 us
  starting transfers between devices: 10.7 us -> 30.7 us
  other arithmetic: 20.7 us -> 6.33 us
  between operations: 13.5 us -> 0.32 us
    all_to_all x2 -> x0, waiting for transfers between devices: 132 us -> none  [the longest x1 93.6 us: on_device(): lax.all_to_all(partial_out, 'wide', split_axis=1, concat_axis=0, tiled=True)]
    reshape x2 -> x0, local copies, waits for them, and re-layouts: 55.8 us -> none  [the longest x1 53.6 us: on_device(): gate_up.reshape(local_halves, half_width, 2 * inner_width)]
    all_gather x1 -> x0, waiting for transfers between devices: 43.4 us -> none  [encode_tiles(): whole_weight = lax.all_gather(adapter_weight, 'wide', axis=0, tiled=True)]
    pallas_call x0 -> x9, Pallas kernels: none -> 38.4 us  [the longest x4 18.8 us: fetch(): pl.pallas_call(functools.partial(fetch_kernel, base), in_specs=[ANY], out...]
    dot_general x3 -> x0, matrix products: 31.8 us -> none  [the longest x1 16.4 us: on_device(): jnp.einsum('lrd,ldf->lrf', arrived, gate_up.reshape(local_halves, half_wi...]
    ppermute x0 -> x30, starting transfers between devices: none -> 30.7 us  [the longest x14 22.5 us: from_prev(): return lax.ppermute(value, 'wide', ring_pairs(1))]
    ppermute x0 -> x30, waiting for transfers between devices: none -> 30 us  [the longest x14 18 us: from_prev(): return lax.ppermute(value, 'wide', ring_pairs(1))]
    psum x1 -> x0, waiting for transfers between devices: 27.6 us -> none  [on_device(): lax.psum(rounded.astype(jnp.bfloat16), 'narrow').astype(jnp.float32)]
  transfers between devices with their start and end apart: 4 -> 30, of which waited for: 4 -> 14; matrix products, arithmetic and copies ran while one was open for 17% -> 3% of each run, Pallas kernels for 0% -> 26%
where the time goes in v2:
time: 112 us
  Pallas kernels  38.4 us (34%)
  starting transfers between devices  30.7 us (27%)
  waiting for transfers between devices  30 us (27%)
  other arithmetic  6.33 us (6%)
  local copies, waits for them, and re-layouts  5.76 us (5%)
    ppermute x14, starting transfers between devices, from_prev(): return lax.ppermute(value, 'wide', ring_pairs(1))  22.5 us
    pallas_call x4, Pallas kernels, fetch(): pl.pallas_call(functools.partial(fetch_kernel, base), in_specs=[ANY], out...  18.8 us
    ppermute x14, waiting for transfers between devices, from_prev(): return lax.ppermute(value, 'wide', ring_pairs(1))  18 us
    ppermute x14, waiting for transfers between devices, from_next(): return lax.ppermute(value, 'wide', ring_pairs(-1))  12 us
    ppermute x14, starting transfers between devices, from_next(): return lax.ppermute(value, 'wide', ring_pairs(-1))  8.12 us
    pallas_call x1, Pallas kernels, on_device_ring(): pl.pallas_call(functools.partial(prologue_kernel, experts, slots, tile_ro...  6.69 us
    pallas_call x2, Pallas kernels, on_device_ring(): pl.pallas_call(functools.partial(second_far_kernel, 2 * near, c, width),...  6.33 us
    unnamed x22, local copies, waits for them, and re-layouts  5.68 us
  transfers between devices with their start and end apart: 30, of which 14 were waited for; matrix products, arithmetic and copies ran while one was open for 3% of the time, Pallas kernels for 26%

profile of v2, /device:TPU:0, one launch (start us, length us, event | category | flops | bytes accessed | tf_op | source)
XLA Modules:
  0.0 111.6 jit_solution(7196769396804825638)
XLA Ops:
  0.0 3.0 %collective-permute-start = (bf16[128,1024]{1,0:T(8,128)(2,1)}, bf16[128,1024]{1,0:T(8,128)(2,1)S(1)}, u32[]{:S(2)}, u32[]{:S(2)}) collective-permute-start(bf16[128,1024]{1,0:T(8,128)(2,1)} %refs_8_.1), channel_id=1, source_target_pairs={{0,4},{4,8},{8,12},{12,14},{14,10},{10,6},{6,2},{2,0},{1,5},{5,9},... | collective-permute-start | bytes 786440 | tf_op jit(solution)/shard_map/ppermute | solution.py:87
  3.0 0.7 bitcast_convert_fusion
  3.7 0.7 fusion.42
  4.4 0.7 convert_bitcast_fusion
  5.1 0.9 compare_reduce_fusion
  6.1 3.4 %collective-permute-done.refs_9_ = bf16[128,1024]{1,0:T(8,128)(2,1)S(1)} collective-permute-done((bf16[128,1024]{1,0:T(8,128)(2,1)}, bf16[128,1024]{1,0:T(8,128)(2,1)S(1)}, u32[]{:S(2)}, u32[]{:S(2)}) %collective-permute-start) | collective-permute-done | bytes 262176 | tf_op jit(solution)/shard_map/ppermute | solution.py:87
  9.5 1.5 %collective-permute-done.1.refs_15_ = bf16[128,1024]{1,0:T(8,128)(2,1)S(1)} collective-permute-done((bf16[128,1024]{1,0:T(8,128)(2,1)}, bf16[128,1024]{1,0:T(8,128)(2,1)S(1)}, u32[]{:S(2)}, u32[]{:S(2)}) %collective-permute-start.1) | collective-permute-done | bytes 262176 | tf_op jit(solution)/shard_map/ppermute | solution.py:91
  11.0 2.2 %fusion.33 = bf16[2,64,1024]{2,1,0:T(8,128)(2,1)S(1)} fusion(bf16[2,64,1024]{2,1,0:T(8,128)(2,1)} %bitcast.18, bf16[2,64,1024]{2,1,0:T(8,128)(2,1)} %param.9, pred[2]{0:T(512)(128)(4,1)S(1)} %compare_reduce_fusion), kind=kLoop, calls=%fused_computation.37 | loop fusion | flops 8781824 | bytes 786434 | tf_op jit(solution)/shard_map/jit(_where)/select_n | solution.py:351
  13.6 1.7 %collective-permute-start.2 = (bf16[144,1024]{1,0:T(8,128)(2,1)S(1)}, bf16[144,1024]{1,0:T(8,128)(2,1)S(1)}, u32[]{:S(2)}, u32[]{:S(2)}) collective-permute-start(bf16[144,1024]{1,0:T(8,128)(2,1)S(1)} %fusion.32.refs_0_), channel_id=1, source_target_pairs={{0,4},{4,8},{8,12},{12,14},{14,10},{10,6},{6,2},{2,0},{1,5},{5,9},... | collective-permute-start | bytes 884744 | tf_op jit(solution)/shard_map/ppermute | solution.py:87
  15.3 1.6 %collective-permute-start.4 = (bf16[128,1024]{1,0:T(8,128)(2,1)S(1)}, bf16[128,1024]{1,0:T(8,128)(2,1)S(1)}, u32[]{:S(2)}, u32[]{:S(2)}) collective-permute-start(bf16[128,1024]{1,0:T(8,128)(2,1)S(1)} %collective-permute-done.refs_9_), channel_id=1, source_target_pairs={{0,4},{4,8},{8,12},{12,14},{14,10},{10,6},{6,2},{2,0},{1,5},{5,9},... | collective-permute-start | bytes 786440 | tf_op jit(solution)/shard_map/ppermute | solution.py:87
  17.3 4.5 %shard_map.91.refs_16_ = bf16[4,1024,1024]{2,1,0:T(8,128)(2,1)S(1)} custom-call(bf16[16,1024,2,512]{3,2,1,0:T(2,128)(2,1)} %gate_up.7), custom_call_target="tpu_custom_call" | custom-call | flops 2147483648 | bytes 16777216 | tf_op jit(solution)/shard_map/pallas_call | solution.py:363
  21.9 4.9 %collective-permute-done.4.refs_10_ = bf16[128,1024]{1,0:T(8,128)(2,1)S(1)} collective-permute-done((bf16[128,1024]{1,0:T(8,128)(2,1)S(1)}, bf16[128,1024]{1,0:T(8,128)(2,1)S(1)}, u32[]{:S(2)}, u32[]{:S(2)}) %collective-permute-start.4) | collective-permute-done | bytes 262176 | tf_op jit(solution)/shard_map/ppermute | solution.py:87
  26.8 1.4 %collective-permute-start.6 = (bf16[144,1024]{1,0:T(8,128)(2,1)S(1)}, bf16[144,1024]{1,0:T(8,128)(2,1)S(1)}, u32[]{:S(2)}, u32[]{:S(2)}) collective-permute-start(bf16[144,1024]{1,0:T(8,128)(2,1)S(1)} %collective-permute-done.2.refs_1_), channel_id=1, source_target_pairs={{0,4},{4,8},{8,12},{12,14},{14,10},{10,6},{6,2},{2,0},{1,5},{5,9},... | collective-permute-start | bytes 884744 | tf_op jit(solution)/shard_map/ppermute | solution.py:87
  28.9 1.4 %collective-permute-start.8 = (bf16[128,1024]{1,0:T(8,128)(2,1)S(1)}, bf16[128,1024]{1,0:T(8,128)(2,1)S(1)}, u32[]{:S(2)}, u32[]{:S(2)}) collective-permute-start(bf16[128,1024]{1,0:T(8,128)(2,1)S(1)} %collective-permute-done.4.refs_10_), channel_id=1, source_target_pairs={{0,4},{4,8},{8,12},{12,14},{14,10},{10,6},{6,2},{2,0},{1,5},{5,9},... | collective-permute-start | bytes 786440 | tf_op jit(solution)/shard_map/ppermute | solution.py:87
  30.9 4.5 %shard_map.92.refs_17_ = bf16[4,1024,1024]{2,1,0:T(8,128)(2,1)S(1)} custom-call(bf16[16,1024,2,512]{3,2,1,0:T(2,128)(2,1)} %gate_up.7), custom_call_target="tpu_custom_call" | custom-call | flops 2147483648 | bytes 16777216 | tf_op jit(solution)/shard_map/pallas_call | solution.py:363
  35.5 3.8 %collective-permute-done.8.refs_11_ = bf16[128,1024]{1,0:T(8,128)(2,1)S(1)} collective-permute-done((bf16[128,1024]{1,0:T(8,128)(2,1)S(1)}, bf16[128,1024]{1,0:T(8,128)(2,1)S(1)}, u32[]{:S(2)}, u32[]{:S(2)}) %collective-permute-start.8) | collective-permute-done | bytes 262176 | tf_op jit(solution)/shard_map/ppermute | solution.py:87
  39.3 0.8 collective-permute-done.9.refs_13_
  40.1 1.6 %collective-permute-start.10 = (bf16[144,1024]{1,0:T(8,128)(2,1)S(1)}, bf16[144,1024]{1,0:T(8,128)(2,1)S(1)}, u32[]{:S(2)}, u32[]{:S(2)}) collective-permute-start(bf16[144,1024]{1,0:T(8,128)(2,1)S(1)} %collective-permute-done.6.refs_2_), channel_id=1, source_target_pairs={{0,4},{4,8},{8,12},{12,14},{14,10},{10,6},{6,2},{2,0},{1,5},{5,9},... | collective-permute-start | bytes 884744 | tf_op jit(solution)/shard_map/ppermute | solution.py:87
  42.1 0.9 collective-permute-start.12
  43.1 4.5 %shard_map.93.refs_0_ = bf16[4,1024,1024]{2,1,0:T(8,128)(2,1)S(1)} custom-call(bf16[16,1024,2,512]{3,2,1,0:T(2,128)(2,1)} %gate_up.7), custom_call_target="tpu_custom_call" | custom-call | flops 2147483648 | bytes 16777216 | tf_op jit(solution)/shard_map/pallas_call | solution.py:363
  47.7 4.6 %collective-permute-done.12.refs_12_ = bf16[128,1024]{1,0:T(8,128)(2,1)S(1)} collective-permute-done((bf16[128,1024]{1,0:T(8,128)(2,1)S(1)}, bf16[128,1024]{1,0:T(8,128)(2,1)S(1)}, u32[]{:S(2)}, u32[]{:S(2)}) %collective-permute-start.12) | collective-permute-done | bytes 262176 | tf_op jit(solution)/shard_map/ppermute | solution.py:91
  52.3 1.6 %collective-permute-start.13 = (bf16[144,1024]{1,0:T(8,128)(2,1)S(1)}, bf16[144,1024]{1,0:T(8,128)(2,1)S(1)}, u32[]{:S(2)}, u32[]{:S(2)}) collective-permute-start(bf16[144,1024]{1,0:T(8,128)(2,1)S(1)} %collective-permute-done.10.refs_3_), channel_id=1, source_target_pairs={{0,4},{4,8},{8,12},{12,14},{14,10},{10,6},{6,2},{2,0},{1,5},{5,9},... | collective-permute-start | bytes 884744 | tf_op jit(solution)/shard_map/ppermute | solution.py:87
  53.9 5.2 %shard_map.94.refs_18_.refs_1_ = bf16[4,1024,1024]{2,1,0:T(8,128)(2,1)S(1)} custom-call(bf16[16,1024,2,512]{3,2,1,0:T(2,128)(2,1)} %gate_up.7), custom_call_target="tpu_custom_call" | custom-call | flops 2147483648 | bytes 16777216 | tf_op jit(solution)/shard_map/pallas_call | solution.py:363
  59.2 6.7 %shard_map.95 = (bf16[4,128,1024]{2,1,0:T(8,128)(2,1)S(1)}, bf16[8,2,128,128]{3,2,1,0:T(8,128)(2,1)S(1)}, bf16[8,128,1024]{2,1,0:T(8,128)(2,1)S(1)}) custom-call(bf16[144,1024]{1,0:T(8,128)(2,1)S(1)} %fusion.32.refs_0_, bf16[144,1024]{1,0:T(8,128)(2,1)S(1)} %collective-permute-done.2.refs_1_, bf16[144,1024]{1,0:T(8,128)(2,1)S(1)} %collective-permute-done.6.refs_2_, ...), custom_call_target="tpu_custom_call" | custom-call | tf_op jit(solution)/shard_map/pallas_call | solution.py:386
  66.0 4.1 %copy-done.3 = bf16[4,1024,1024]{2,1,0:T(8,128)(2,1)S(1)} copy-done((bf16[4,1024,1024]{2,1,0:T(8,128)(2,1)S(1)}, bf16[4,1024,1024]{2,1,0:T(8,128)(2,1)}, u32[]{:S(2)}) %copy-start.3) | copy-done | bytes 8388632
  70.1 2.4 %shard_map.96.refs_0_ = bf16[8,128,1024]{2,1,0:T(8,128)(2,1)S(1)} custom-call(bf16[4,128,1024]{2,1,0:T(8,128)(2,1)S(1)} %get-tuple-element.80.rows, bf16[4,1024,1024]{2,1,0:T(8,128)(2,1)S(1)} %copy-done.3, bf16[4,1024,1024]{2,1,0:T(8,128)(2,1)S(1)} %shard_map.94.refs_18_.refs_1_), custom_call_target="tpu_custom_call" | custom-call | flops 4294967296 | bytes 16777216 | tf_op jit(solution)/shard_map/pallas_call | solution.py:408
  72.6 1.6 %copy-done.5 = bf16[8,128,1024]{2,1,0:T(8,128)(2,1)S(1)} copy-done((bf16[8,128,1024]{2,1,0:T(8,128)(2,1)S(1)}, bf16[8,128,1024]{2,1,0:T(8,128)(2,1)}, u32[]{:S(2)}) %copy-start.5) | copy-done | bytes 2097176
  74.2 4.2 %shard_map.97.refs_2_.refs_1_ = bf16[4,128,1024]{2,1,0:T(8,128)(2,1)S(1)} custom-call(bf16[8,128,1024]{2,1,0:T(8,128)(2,1)S(1)} %copy-done.5, bf16[8,128,1024]{2,1,0:T(8,128)(2,1)S(1)} %collective-permute-done.14.other, bf16[16,512,1024]{2,1,0:T(8,128)(2,1)} %refs_3_.1), custom_call_target="tpu_custom_call" | custom-call | flops 1073741824 | bytes 8388608 | tf_op jit(solution)/shard_map/pallas_call | solution.py:421
  78.4 3.2 %shard_map.98 = (bf16[8,128,512]{2,1,0:T(8,128)(2,1)S(1)}, bf16[128,512]{1,0:T(8,128)(2,1)S(1)}, bf16[128,512]{1,0:T(8,128)(2,1)S(1)}, bf16[128,512]{1,0:T(8,128...) custom-call(bf16[8,128,1024]{2,1,0:T(8,128)(2,1)S(1)} %shard_map.96., ...), custom_call_target="tpu_custom_call" | custom-call | flops 536870912 | bytes 4194304 | tf_op jit(solution)/shard_map/pallas_call | solution.py:442
  82.3 1.4 %collective-permute-start.20 = (bf16[128,512]{1,0:T(8,128)(2,1)S(1)}, bf16[128,512]{1,0:T(8,128)(2,1)S(1)}, u32[]{:S(2)}, u32[]{:S(2)}) collective-permute-start(bf16[128,512]{1,0:T(8,128)(2,1)S(1)} %get-tuple-element.93), channel_id=1, source_target_pairs={{0,4},{4,8},{8,12},{12,14},{14,10},{10,6},{6,2},{2,0},{1,5},{5,9},... | collective-permute-start | bytes 393224 | tf_op jit(solution)/shard_map/ppermute | solution.py:87
  83.7 3.2 %shard_map.99 = (bf16[128,512]{1,0:T(8,128)(2,1)S(1)}, bf16[128,512]{1,0:T(8,128)(2,1)S(1)}, bf16[128,512]{1,0:T(8,128)(2,1)S(1)}, bf16[128,512]{1,0:T(8,128)(2,...) custom-call(bf16[8,128,512]{2,1,0:T(8,128)(2,1)S(1)} %get-tuple-elem, ...), custom_call_target="tpu_custom_call" | custom-call | flops 536870912 | bytes 4194304 | tf_op jit(solution)/shard_map/pallas_call | solution.py:442
  86.8 0.7 collective-permute-start.23
  87.5 1.4 %collective-permute-start.26 = (bf16[128,512]{1,0:T(8,128)(2,1)S(1)}, bf16[128,512]{1,0:T(8,128)(2,1)S(1)}, u32[]{:S(2)}, u32[]{:S(2)}) collective-permute-start(bf16[128,512]{1,0:T(8,128)(2,1)S(1)} %get-tuple-element.101), channel_id=1, source_target_pairs={{0,4},{4,8},{8,12},{12,14},{14,10},{10,6},{6,2},{2,0},{1,5},{5,9},... | collective-permute-start | bytes 393224 | tf_op jit(solution)/shard_map/ppermute | solution.py:87
  89.0 0.7 collective-permute-start.17
  89.7 1.5 %collective-permute-start.21 = (bf16[128,512]{1,0:T(8,128)(2,1)S(1)}, bf16[128,512]{1,0:T(8,128)(2,1)S(1)}, u32[]{:S(2)}, u32[]{:S(2)}) collective-permute-start(bf16[128,512]{1,0:T(8,128)(2,1)S(1)} %add_convert_fusion.8), channel_id=1, source_target_pairs={{0,4},{4,8},{8,12},{12,14},{14,10},{10,6},{6,2},{2,0},{1,5},{5,9},... | collective-permute-start | bytes 393224 | tf_op jit(solution)/shard_map/ppermute | solution.py:87
  91.1 2.1 %collective-permute-done.23 = bf16[128,512]{1,0:T(8,128)(2,1)S(1)} collective-permute-done((bf16[128,512]{1,0:T(8,128)(2,1)S(1)}, bf16[128,512]{1,0:T(8,128)(2,1)S(1)}, u32[]{:S(2)}, u32[]{:S(2)}) %collective-permute-start.23) | collective-permute-done | bytes 131104 | tf_op jit(solution)/shard_map/ppermute | solution.py:91
  93.3 0.7 collective-permute-start.24
  94.0 1.5 %collective-permute-start.27 = (bf16[128,512]{1,0:T(8,128)(2,1)S(1)}, bf16[128,512]{1,0:T(8,128)(2,1)S(1)}, u32[]{:S(2)}, u32[]{:S(2)}) collective-permute-start(bf16[128,512]{1,0:T(8,128)(2,1)S(1)} %add_convert_fusion.3), channel_id=1, source_target_pairs={{0,4},{4,8},{8,12},{12,14},{14,10},{10,6},{6,2},{2,0},{1,5},{5,9},... | collective-permute-start | bytes 393224 | tf_op jit(solution)/shard_map/ppermute | solution.py:87
  96.1 0.7 collective-permute-start.18
  96.8 1.5 %collective-permute-start.22 = (bf16[128,512]{1,0:T(8,128)(2,1)S(1)}, bf16[128,512]{1,0:T(8,128)(2,1)S(1)}, u32[]{:S(2)}, u32[]{:S(2)}) collective-permute-start(bf16[128,512]{1,0:T(8,128)(2,1)S(1)} %add_convert_fusion.7), channel_id=1, source_target_pairs={{0,4},{4,8},{8,12},{12,14},{14,10},{10,6},{6,2},{2,0},{1,5},{5,9},... | collective-permute-start | bytes 393224 | tf_op jit(solution)/shard_map/ppermute | solution.py:87
  98.3 1.4 %collective-permute-done.24 = bf16[128,512]{1,0:T(8,128)(2,1)S(1)} collective-permute-done((bf16[128,512]{1,0:T(8,128)(2,1)S(1)}, bf16[128,512]{1,0:T(8,128)(2,1)S(1)}, u32[]{:S(2)}, u32[]{:S(2)}) %collective-permute-start.24) | collective-permute-done | bytes 131104 | tf_op jit(solution)/shard_map/ppermute | solution.py:91
  99.8 0.7 collective-permute-start.25
  100.5 1.5 %collective-permute-start.28 = (bf16[128,512]{1,0:T(8,128)(2,1)S(1)}, bf16[128,512]{1,0:T(8,128)(2,1)S(1)}, u32[]{:S(2)}, u32[]{:S(2)}) collective-permute-start(bf16[128,512]{1,0:T(8,128)(2,1)S(1)} %add_convert_fusion.2), channel_id=1, source_target_pairs={{0,4},{4,8},{8,12},{12,14},{14,10},{10,6},{6,2},{2,0},{1,5},{5,9},... | collective-permute-start | bytes 393224 | tf_op jit(solution)/shard_map/ppermute | solution.py:87
  102.5 0.7 collective-permute-start.19
  103.2 2.6 %collective-permute-done.28 = bf16[128,512]{1,0:T(8,128)(2,1)S(1)} collective-permute-done((bf16[128,512]{1,0:T(8,128)(2,1)S(1)}, bf16[128,512]{1,0:T(8,128)(2,1)S(1)}, u32[]{:S(2)}, u32[]{:S(2)}) %collective-permute-start.28) | collective-permute-done | bytes 131104 | tf_op jit(solution)/shard_map/ppermute | solution.py:87
  105.8 1.4 %collective-permute-start.29 = (bf16[128,512]{1,0:T(8,128)(2,1)S(1)}, bf16[128,512]{1,0:T(8,128)(2,1)S(1)}, u32[]{:S(2)}, u32[]{:S(2)}) collective-permute-start(bf16[128,512]{1,0:T(8,128)(2,1)S(1)} %add_convert_fusion.1), channel_id=1, source_target_pairs={{0,4},{4,8},{8,12},{12,14},{14,10},{10,6},{6,2},{2,0},{1,5},{5,9},... | collective-permute-start | bytes 393224 | tf_op jit(solution)/shard_map/ppermute | solution.py:87
  107.6 3.2 %collective-permute-done.29 = bf16[128,512]{1,0:T(8,128)(2,1)S(1)} collective-permute-done((bf16[128,512]{1,0:T(8,128)(2,1)S(1)}, bf16[128,512]{1,0:T(8,128)(2,1)S(1)}, u32[]{:S(2)}, u32[]{:S(2)}) %collective-permute-start.29) | collective-permute-done | bytes 131104 | tf_op jit(solution)/shard_map/ppermute | solution.py:87
  110.9 0.7 pad_maximum_fusion
  (66 shorter events, 5.5 us)
Async XLA Ops:
  0.0 9.5 %collective-permute-start = (bf16[128,1024]{1,0:T(8,128)(2,1)}, bf16[128,1024]{1,0:T(8,128)(2,1)S(1)}, u32[]{:S(2)}, u32[]{:S(2)}) collective-permute-start(bf16[128,1024]{1,0:T(8,128)(2,1)} %refs_8_.1), channel_id=1, source_target_pairs={{0,4},{4,8},{8,12},{12,14},{14,10},{10,6},{6,2},{2,0},{1,5},{5,9},... | collective-permute-start | bytes 786440 | tf_op jit(solution)/shard_map/ppermute | solution.py:87
  3.0 8.0 %collective-permute-start.1 = (bf16[128,1024]{1,0:T(8,128)(2,1)}, bf16[128,1024]{1,0:T(8,128)(2,1)S(1)}, u32[]{:S(2)}, u32[]{:S(2)}) collective-permute-start(bf16[128,1024]{1,0:T(8,128)(2,1)} %refs_8_.1), channel_id=1, source_target_pairs={{0,2},{4,0},{8,4},{12,8},{14,12},{10,14},{6,10},{2,6},{1,3},{5,1},... | collective-permute-start | bytes 786440 | tf_op jit(solution)/shard_map/ppermute | solution.py:91
  13.2 13.6 %collective-permute-start.3 = (bf16[144,1024]{1,0:T(8,128)(2,1)S(1)}, bf16[144,1024]{1,0:T(8,128)(2,1)S(1)}, u32[]{:S(2)}, u32[]{:S(2)}) collective-permute-start(bf16[144,1024]{1,0:T(8,128)(2,1)S(1)} %fusion.32.refs_0_), channel_id=1, source_target_pairs={{0,2},{4,0},{8,4},{12,8},{14,12},{10,14},{6,10},{2,6},{1,3},{5,1},... | collective-permute-start | bytes 884744 | tf_op jit(solution)/shard_map/ppermute | solution.py:91
  13.6 13.2 %collective-permute-start.2 = (bf16[144,1024]{1,0:T(8,128)(2,1)S(1)}, bf16[144,1024]{1,0:T(8,128)(2,1)S(1)}, u32[]{:S(2)}, u32[]{:S(2)}) collective-permute-start(bf16[144,1024]{1,0:T(8,128)(2,1)S(1)} %fusion.32.refs_0_), channel_id=1, source_target_pairs={{0,4},{4,8},{8,12},{12,14},{14,10},{10,6},{6,2},{2,0},{1,5},{5,9},... | collective-permute-start | bytes 884744 | tf_op jit(solution)/shard_map/ppermute | solution.py:87
  15.3 11.5 %collective-permute-start.4 = (bf16[128,1024]{1,0:T(8,128)(2,1)S(1)}, bf16[128,1024]{1,0:T(8,128)(2,1)S(1)}, u32[]{:S(2)}, u32[]{:S(2)}) collective-permute-start(bf16[128,1024]{1,0:T(8,128)(2,1)S(1)} %collective-permute-done.refs_9_), channel_id=1, source_target_pairs={{0,4},{4,8},{8,12},{12,14},{14,10},{10,6},{6,2},{2,0},{1,5},{5,9},... | collective-permute-start | bytes 786440 | tf_op jit(solution)/shard_map/ppermute | solution.py:87
  16.9 9.9 %collective-permute-start.5 = (bf16[128,1024]{1,0:T(8,128)(2,1)S(1)}, bf16[128,1024]{1,0:T(8,128)(2,1)S(1)}, u32[]{:S(2)}, u32[]{:S(2)}) collective-permute-start(bf16[128,1024]{1,0:T(8,128)(2,1)S(1)} %collective-permute-done.1.refs_15_), channel_id=1, source_target_pairs={{0,2},{4,0},{8,4},{12,8},{14,12},{10,14},{6,10},{2,6},{1,3},{5,1},... | collective-permute-start | bytes 786440 | tf_op jit(solution)/shard_map/ppermute | solution.py:91
  26.8 8.7 %copy-start.7 = (bf16[128,1024]{1,0:T(8,128)(2,1)}, bf16[128,1024]{1,0:T(8,128)(2,1)S(1)}, u32[]{:S(2)}) copy-start(bf16[128,1024]{1,0:T(8,128)(2,1)S(1)} %collective-permute-done.5.refs_14_) | copy-start | bytes 786436
  26.8 13.2 %collective-permute-start.6 = (bf16[144,1024]{1,0:T(8,128)(2,1)S(1)}, bf16[144,1024]{1,0:T(8,128)(2,1)S(1)}, u32[]{:S(2)}, u32[]{:S(2)}) collective-permute-start(bf16[144,1024]{1,0:T(8,128)(2,1)S(1)} %collective-permute-done.2.refs_1_), channel_id=1, source_target_pairs={{0,4},{4,8},{8,12},{12,14},{14,10},{10,6},{6,2},{2,0},{1,5},{5,9},... | collective-permute-start | bytes 884744 | tf_op jit(solution)/shard_map/ppermute | solution.py:87
  28.3 11.8 %collective-permute-start.7 = (bf16[144,1024]{1,0:T(8,128)(2,1)S(1)}, bf16[144,1024]{1,0:T(8,128)(2,1)S(1)}, u32[]{:S(2)}, u32[]{:S(2)}) collective-permute-start(bf16[144,1024]{1,0:T(8,128)(2,1)S(1)} %collective-permute-done.3.refs_7_), channel_id=1, source_target_pairs={{0,2},{4,0},{8,4},{12,8},{14,12},{10,14},{6,10},{2,6},{1,3},{5,1},... | collective-permute-start | bytes 884744 | tf_op jit(solution)/shard_map/ppermute | solution.py:91
  28.9 10.4 %collective-permute-start.8 = (bf16[128,1024]{1,0:T(8,128)(2,1)S(1)}, bf16[128,1024]{1,0:T(8,128)(2,1)S(1)}, u32[]{:S(2)}, u32[]{:S(2)}) collective-permute-start(bf16[128,1024]{1,0:T(8,128)(2,1)S(1)} %collective-permute-done.4.refs_10_), channel_id=1, source_target_pairs={{0,4},{4,8},{8,12},{12,14},{14,10},{10,6},{6,2},{2,0},{1,5},{5,9},... | collective-permute-start | bytes 786440 | tf_op jit(solution)/shard_map/ppermute | solution.py:87
  30.3 9.8 %collective-permute-start.9 = (bf16[128,1024]{1,0:T(8,128)(2,1)S(1)}, bf16[128,1024]{1,0:T(8,128)(2,1)S(1)}, u32[]{:S(2)}, u32[]{:S(2)}) collective-permute-start(bf16[128,1024]{1,0:T(8,128)(2,1)S(1)} %collective-permute-done.5.refs_14_), channel_id=1, source_target_pairs={{0,2},{4,0},{8,4},{12,8},{14,12},{10,14},{6,10},{2,6},{1,3},{5,1},... | collective-permute-start | bytes 786440 | tf_op jit(solution)/shard_map/ppermute | solution.py:91
  35.5 12.1 %copy-start = (bf16[4,1024,1024]{2,1,0:T(8,128)(2,1)}, bf16[4,1024,1024]{2,1,0:T(8,128)(2,1)S(1)}, u32[]{:S(2)}) copy-start(bf16[4,1024,1024]{2,1,0:T(8,128)(2,1)S(1)} %shard_map.92.refs_17_) | copy-start | bytes 25165828
  39.3 8.3 %copy-start.9 = (bf16[128,1024]{1,0:T(8,128)(2,1)}, bf16[128,1024]{1,0:T(8,128)(2,1)S(1)}, u32[]{:S(2)}) copy-start(bf16[128,1024]{1,0:T(8,128)(2,1)S(1)} %collective-permute-done.8.refs_11_) | copy-start | bytes 786436
  40.1 12.2 %collective-permute-start.10 = (bf16[144,1024]{1,0:T(8,128)(2,1)S(1)}, bf16[144,1024]{1,0:T(8,128)(2,1)S(1)}, u32[]{:S(2)}, u32[]{:S(2)}) collective-permute-start(bf16[144,1024]{1,0:T(8,128)(2,1)S(1)} %collective-permute-done.6.refs_2_), channel_id=1, source_target_pairs={{0,4},{4,8},{8,12},{12,14},{14,10},{10,6},{6,2},{2,0},{1,5},{5,9},... | collective-permute-start | bytes 884744 | tf_op jit(solution)/shard_map/ppermute | solution.py:87
  41.7 10.6 %collective-permute-start.11 = (bf16[144,1024]{1,0:T(8,128)(2,1)S(1)}, bf16[144,1024]{1,0:T(8,128)(2,1)S(1)}, u32[]{:S(2)}, u32[]{:S(2)}) collective-permute-start(bf16[144,1024]{1,0:T(8,128)(2,1)S(1)} %collective-permute-done.7.refs_6_), channel_id=1, source_target_pairs={{0,2},{4,0},{8,4},{12,8},{14,12},{10,14},{6,10},{2,6},{1,3},{5,1},... | collective-permute-start | bytes 884744 | tf_op jit(solution)/shard_map/ppermute | solution.py:91
  42.1 10.1 %collective-permute-start.12 = (bf16[128,1024]{1,0:T(8,128)(2,1)S(1)}, bf16[128,1024]{1,0:T(8,128)(2,1)S(1)}, u32[]{:S(2)}, u32[]{:S(2)}) collective-permute-start(bf16[128,1024]{1,0:T(8,128)(2,1)S(1)} %collective-permute-done.9.refs_13_), channel_id=1, source_target_pairs={{0,2},{4,0},{8,4},{12,8},{14,12},{10,14},{6,10},{2,6},{1,3},{5,1},... | collective-permute-start | bytes 786440 | tf_op jit(solution)/shard_map/ppermute | solution.py:91
  47.6 11.5 %copy-start.2 = (bf16[4,1024,1024]{2,1,0:T(8,128)(2,1)}, bf16[4,1024,1024]{2,1,0:T(8,128)(2,1)S(1)}, u32[]{:S(2)}) copy-start(bf16[4,1024,1024]{2,1,0:T(8,128)(2,1)S(1)} %shard_map.93.refs_0_) | copy-start | bytes 25165828
  47.6 11.6 %copy-start.6 = (bf16[128,1024]{1,0:T(8,128)(2,1)S(1)}, bf16[128,1024]{1,0:T(8,128)(2,1)}, u32[]{:S(2)}) copy-start(bf16[128,1024]{1,0:T(8,128)(2,1)} %refs_8_.1) | copy-start | bytes 786436
  47.6 11.6 %copy-start.8 = (bf16[128,1024]{1,0:T(8,128)(2,1)S(1)}, bf16[128,1024]{1,0:T(8,128)(2,1)}, u32[]{:S(2)}) copy-start(bf16[128,1024]{1,0:T(8,128)(2,1)} %copy-done.7) | copy-start | bytes 786436
  52.3 7.0 %copy-start.1 = (bf16[4,1024,1024]{2,1,0:T(8,128)(2,1)S(1)}, bf16[4,1024,1024]{2,1,0:T(8,128)(2,1)}, u32[]{:S(2)}) copy-start(bf16[4,1024,1024]{2,1,0:T(8,128)(2,1)} %copy-done) | copy-start | bytes 25165828
  52.3 7.0 %copy-start.10 = (bf16[128,1024]{1,0:T(8,128)(2,1)S(1)}, bf16[128,1024]{1,0:T(8,128)(2,1)}, u32[]{:S(2)}) copy-start(bf16[128,1024]{1,0:T(8,128)(2,1)} %copy-done.9) | copy-start | bytes 786436
  52.3 7.0 %collective-permute-start.13 = (bf16[144,1024]{1,0:T(8,128)(2,1)S(1)}, bf16[144,1024]{1,0:T(8,128)(2,1)S(1)}, u32[]{:S(2)}, u32[]{:S(2)}) collective-permute-start(bf16[144,1024]{1,0:T(8,128)(2,1)S(1)} %collective-permute-done.10.refs_3_), channel_id=1, source_target_pairs={{0,4},{4,8},{8,12},{12,14},{14,10},{10,6},{6,2},{2,0},{1,5},{5,9},... | collective-permute-start | bytes 884744 | tf_op jit(solution)/shard_map/ppermute | solution.py:87
  65.9 6.5 %copy-start.4 = (bf16[8,128,1024]{2,1,0:T(8,128)(2,1)}, bf16[8,128,1024]{2,1,0:T(8,128)(2,1)S(1)}, u32[]{:S(2)}) copy-start(bf16[8,128,1024]{2,1,0:T(8,128)(2,1)S(1)} %get-tuple-element.82.own) | copy-start | bytes 6291460
  66.0 6.5 %collective-permute-start.14 = (bf16[8,128,1024]{2,1,0:T(8,128)(2,1)S(1)}, bf16[8,128,1024]{2,1,0:T(8,128)(2,1)S(1)}, u32[]{:S(2)}, u32[]{:S(2)}) collective-permute-start(bf16[8,128,1024]{2,1,0:T(8,128)(2,1)S(1)} %get-tuple-element.82.own), channel_id=1, source_target_pairs={{0,1},{1,0},{2,3},{3,2},{4,5},{5,4},{6,7},{7,6},{8,9},{9,8},{10,11... | collective-permute-start | bytes 6291464 | tf_op jit(solution)/shard_map/ppermute | solution.py:95
  66.0 4.1 %copy-start.3 = (bf16[4,1024,1024]{2,1,0:T(8,128)(2,1)S(1)}, bf16[4,1024,1024]{2,1,0:T(8,128)(2,1)}, u32[]{:S(2)}) copy-start(bf16[4,1024,1024]{2,1,0:T(8,128)(2,1)} %copy-done.2) | copy-start | bytes 25165828
  72.5 5.9 %collective-permute-start.15 = (bf16[8,128,1024]{2,1,0:T(8,128)(2,1)S(1)}, bf16[8,128,1024]{2,1,0:T(8,128)(2,1)S(1)}, u32[]{:S(2)}, u32[]{:S(2)}) collective-permute-start(bf16[8,128,1024]{2,1,0:T(8,128)(2,1)S(1)} %shard_map.96.refs_0_), channel_id=1, source_target_pairs={{0,1},{1,0},{2,3},{3,2},{4,5},{5,4},{6,7},{7,6},{8,9},{9,8},{10,11... | collective-permute-start | bytes 6291464 | tf_op jit(solution)/shard_map/ppermute | solution.py:95
  72.6 1.6 %copy-start.5 = (bf16[8,128,1024]{2,1,0:T(8,128)(2,1)S(1)}, bf16[8,128,1024]{2,1,0:T(8,128)(2,1)}, u32[]{:S(2)}) copy-start(bf16[8,128,1024]{2,1,0:T(8,128)(2,1)} %copy-done.4) | copy-start | bytes 6291460
  81.6 7.3 %collective-permute-start.16 = (bf16[128,512]{1,0:T(8,128)(2,1)S(1)}, bf16[128,512]{1,0:T(8,128)(2,1)S(1)}, u32[]{:S(2)}, u32[]{:S(2)}) collective-permute-start(bf16[128,512]{1,0:T(8,128)(2,1)S(1)} %get-tuple-element.89), channel_id=1, source_target_pairs={{0,2},{4,0},{8,4},{12,8},{14,12},{10,14},{6,10},{2,6},{1,3},{5,1},... | collective-permute-start | bytes 393224 | tf_op jit(solution)/shard_map/ppermute | solution.py:91
  82.3 7.4 %collective-permute-start.20 = (bf16[128,512]{1,0:T(8,128)(2,1)S(1)}, bf16[128,512]{1,0:T(8,128)(2,1)S(1)}, u32[]{:S(2)}, u32[]{:S(2)}) collective-permute-start(bf16[128,512]{1,0:T(8,128)(2,1)S(1)} %get-tuple-element.93), channel_id=1, source_target_pairs={{0,4},{4,8},{8,12},{12,14},{14,10},{10,6},{6,2},{2,0},{1,5},{5,9},... | collective-permute-start | bytes 393224 | tf_op jit(solution)/shard_map/ppermute | solution.py:87
  86.8 6.4 %collective-permute-start.23 = (bf16[128,512]{1,0:T(8,128)(2,1)S(1)}, bf16[128,512]{1,0:T(8,128)(2,1)S(1)}, u32[]{:S(2)}, u32[]{:S(2)}) collective-permute-start(bf16[128,512]{1,0:T(8,128)(2,1)S(1)} %get-tuple-element.98), channel_id=1, source_target_pairs={{0,2},{4,0},{8,4},{12,8},{14,12},{10,14},{6,10},{2,6},{1,3},{5,1},... | collective-permute-start | bytes 393224 | tf_op jit(solution)/shard_map/ppermute | solution.py:91
  87.5 6.5 %collective-permute-start.26 = (bf16[128,512]{1,0:T(8,128)(2,1)S(1)}, bf16[128,512]{1,0:T(8,128)(2,1)S(1)}, u32[]{:S(2)}, u32[]{:S(2)}) collective-permute-start(bf16[128,512]{1,0:T(8,128)(2,1)S(1)} %get-tuple-element.101), channel_id=1, source_target_pairs={{0,4},{4,8},{8,12},{12,14},{14,10},{10,6},{6,2},{2,0},{1,5},{5,9},... | collective-permute-start | bytes 393224 | tf_op jit(solution)/shard_map/ppermute | solution.py:87
  89.0 7.1 %collective-permute-start.17 = (bf16[128,512]{1,0:T(8,128)(2,1)S(1)}, bf16[128,512]{1,0:T(8,128)(2,1)S(1)}, u32[]{:S(2)}, u32[]{:S(2)}) collective-permute-start(bf16[128,512]{1,0:T(8,128)(2,1)S(1)} %add_convert_fusion.11), channel_id=1, source_target_pairs={{0,2},{4,0},{8,4},{12,8},{14,12},{10,14},{6,10},{2,6},{1,3},{5,1},... | collective-permute-start | bytes 393224 | tf_op jit(solution)/shard_map/ppermute | solution.py:91
  89.7 7.1 %collective-permute-start.21 = (bf16[128,512]{1,0:T(8,128)(2,1)S(1)}, bf16[128,512]{1,0:T(8,128)(2,1)S(1)}, u32[]{:S(2)}, u32[]{:S(2)}) collective-permute-start(bf16[128,512]{1,0:T(8,128)(2,1)S(1)} %add_convert_fusion.8), channel_id=1, source_target_pairs={{0,4},{4,8},{8,12},{12,14},{14,10},{10,6},{6,2},{2,0},{1,5},{5,9},... | collective-permute-start | bytes 393224 | tf_op jit(solution)/shard_map/ppermute | solution.py:87
  93.3 6.4 %collective-permute-start.24 = (bf16[128,512]{1,0:T(8,128)(2,1)S(1)}, bf16[128,512]{1,0:T(8,128)(2,1)S(1)}, u32[]{:S(2)}, u32[]{:S(2)}) collective-permute-start(bf16[128,512]{1,0:T(8,128)(2,1)S(1)} %add_convert_fusion.5), channel_id=1, source_target_pairs={{0,2},{4,0},{8,4},{12,8},{14,12},{10,14},{6,10},{2,6},{1,3},{5,1},... | collective-permute-start | bytes 393224 | tf_op jit(solution)/shard_map/ppermute | solution.py:91
  94.0 6.4 %collective-permute-start.27 = (bf16[128,512]{1,0:T(8,128)(2,1)S(1)}, bf16[128,512]{1,0:T(8,128)(2,1)S(1)}, u32[]{:S(2)}, u32[]{:S(2)}) collective-permute-start(bf16[128,512]{1,0:T(8,128)(2,1)S(1)} %add_convert_fusion.3), channel_id=1, source_target_pairs={{0,4},{4,8},{8,12},{12,14},{14,10},{10,6},{6,2},{2,0},{1,5},{5,9},... | collective-permute-start | bytes 393224 | tf_op jit(solution)/shard_map/ppermute | solution.py:87
  96.1 6.4 %collective-permute-start.18 = (bf16[128,512]{1,0:T(8,128)(2,1)S(1)}, bf16[128,512]{1,0:T(8,128)(2,1)S(1)}, u32[]{:S(2)}, u32[]{:S(2)}) collective-permute-start(bf16[128,512]{1,0:T(8,128)(2,1)S(1)} %add_convert_fusion.10), channel_id=1, source_target_pairs={{0,2},{4,0},{8,4},{12,8},{14,12},{10,14},{6,10},{2,6},{1,3},{5,1},... | collective-permute-start | bytes 393224 | tf_op jit(solution)/shard_map/ppermute | solution.py:91
  96.8 10.4 %collective-permute-start.22 = (bf16[128,512]{1,0:T(8,128)(2,1)S(1)}, bf16[128,512]{1,0:T(8,128)(2,1)S(1)}, u32[]{:S(2)}, u32[]{:S(2)}) collective-permute-start(bf16[128,512]{1,0:T(8,128)(2,1)S(1)} %add_convert_fusion.7), channel_id=1, source_target_pairs={{0,4},{4,8},{8,12},{12,14},{14,10},{10,6},{6,2},{2,0},{1,5},{5,9},... | collective-permute-start | bytes 393224 | tf_op jit(solution)/shard_map/ppermute | solution.py:87
  99.8 7.8 %collective-permute-start.25 = (bf16[128,512]{1,0:T(8,128)(2,1)S(1)}, bf16[128,512]{1,0:T(8,128)(2,1)S(1)}, u32[]{:S(2)}, u32[]{:S(2)}) collective-permute-start(bf16[128,512]{1,0:T(8,128)(2,1)S(1)} %add_convert_fusion.4), channel_id=1, source_target_pairs={{0,2},{4,0},{8,4},{12,8},{14,12},{10,14},{6,10},{2,6},{1,3},{5,1},... | collective-permute-start | bytes 393224 | tf_op jit(solution)/shard_map/ppermute | solution.py:91
  100.5 5.3 %collective-permute-start.28 = (bf16[128,512]{1,0:T(8,128)(2,1)S(1)}, bf16[128,512]{1,0:T(8,128)(2,1)S(1)}, u32[]{:S(2)}, u32[]{:S(2)}) collective-permute-start(bf16[128,512]{1,0:T(8,128)(2,1)S(1)} %add_convert_fusion.2), channel_id=1, source_target_pairs={{0,4},{4,8},{8,12},{12,14},{14,10},{10,6},{6,2},{2,0},{1,5},{5,9},... | collective-permute-start | bytes 393224 | tf_op jit(solution)/shard_map/ppermute | solution.py:87
  102.5 5.0 %collective-permute-start.19 = (bf16[128,512]{1,0:T(8,128)(2,1)S(1)}, bf16[128,512]{1,0:T(8,128)(2,1)S(1)}, u32[]{:S(2)}, u32[]{:S(2)}) collective-permute-start(bf16[128,512]{1,0:T(8,128)(2,1)S(1)} %add_convert_fusion.9), channel_id=1, source_target_pairs={{0,2},{4,0},{8,4},{12,8},{14,12},{10,14},{6,10},{2,6},{1,3},{5,1},... | collective-permute-start | bytes 393224 | tf_op jit(solution)/shard_map/ppermute | solution.py:91
  105.8 5.0 %collective-permute-start.29 = (bf16[128,512]{1,0:T(8,128)(2,1)S(1)}, bf16[128,512]{1,0:T(8,128)(2,1)S(1)}, u32[]{:S(2)}, u32[]{:S(2)}) collective-permute-start(bf16[128,512]{1,0:T(8,128)(2,1)S(1)} %add_convert_fusion.1), channel_id=1, source_target_pairs={{0,4},{4,8},{8,12},{12,14},{14,10},{10,6},{6,2},{2,0},{1,5},{5,9},... | collective-permute-start | bytes 393224 | tf_op jit(solution)/shard_map/ppermute | solution.py:87

commit v3 on v2

--- a/solution.py
+++ b/solution.py
@@ -15,9 +15,11 @@
 BF16 = jnp.bfloat16
 RING = (0, 2, 4, 6, 7, 5, 3, 1)
 NR = 8
+CROSSING = ((1, 7, 2, 6), (3, 5), (4,))
 VMEM_LIMIT = 46 << 20
-VMEM_SMALL = 14 << 20
-FETCH_LIMITS = (40, 33, 24, 16)
+VMEM_SMALL = 10 << 20
+VMEM_FAR = 25 << 20
+FETCH_LIMITS = (34, 26, 18)
 ANY = pl.BlockSpec(memory_space=pl.ANY)
 VM = pl.BlockSpec(memory_space=pltpu.VMEM)
 
@@ -101,7 +103,7 @@
 
 def ring_gather_two(first, make_second, fetches):
     one, two = [first] * NR, [None] * NR
-    fetched = []
+    fetched, across = [], []
     far = NR // 2
     for q in range(1, far + 1):
         up, down = one[q - 1], one[(NR - q + 1) % NR]
@@ -112,18 +114,24 @@
         else:
             one[q] = from_next(down)
         if q == 1:
-            two[0], one[1], one[NR - 1] = make_second(one[1], one[NR - 1])
+            two[0], one[1], one[NR - 1] = tie(make_second(), one[1], one[NR - 1])
         up, down = two[q - 1], two[(NR - q + 1) % NR]
-        if q > 1:
+        if 1 < q < far:
             up, down, one[q], one[NR - q], *fetched = tie(up, down, one[q], one[NR - q], *fetched)
+        elif q == far:
+            up, two[NR - q + 1], one[q], across[0], *fetched = tie(up, two[NR - q + 1], one[q], across[0], *fetched)
         if q < far:
             two[q], two[NR - q] = from_prev(up), from_next(down)
             if fetches:
                 fetched.append(fetches.pop(0)())
         else:
             two[q] = from_prev(up)
-            fetched += [make() for make in fetches]
-    return one, two, fetched
+        if q == far // 2:
+            across.append(swap(jnp.concatenate([one[p] for p in CROSSING[0]]), "grp"))
+        elif q > far // 2:
+            pieces = [one[p] for p in CROSSING[q - far // 2]]
+            across.append(swap(jnp.concatenate(pieces) if len(pieces) > 1 else pieces[0], "grp"))
+    return one, two, fetched, across
 
 
 def add(left, right):
@@ -156,18 +164,27 @@
 
 def prologue_kernel(experts, slots, tile_rows, *refs):
     toks = slots * tile_rows
-    sent_in, weight_in, gate_up = refs[:NR], refs[NR : 2 * NR], refs[2 * NR : -11]
-    rows_out, mix_out, pre_out, sent, weight, packed, rows_here, missed_at, sent_sem, weight_sem = refs[-10:]
+    sent_in = refs[:NR]
+    weight_own, weight_ring = refs[NR], refs[NR + 1 : 2 * NR]
+    weight_across = refs[2 * NR : 2 * NR + len(CROSSING)]
+    gate_up = refs[2 * NR + len(CROSSING) : -8]
+    rows_out, mix_out, pre_out, sent, weight, packed, rows_here, missed_at = refs[-8:]
     near = rows_here.shape[0]
-    shard = weight_in[0].shape[0]
+    shard = weight_own.shape[0]
+    part = shard // 2
     width = packed.shape[2]
-    sent_copies = [pltpu.make_async_copy(ref, sent.at[q], sent_sem.at[q]) for q, ref in enumerate(sent_in)]
-    copies = []
-    for q, ref in enumerate(weight_in):
-        at = pl.multiple_of(ring_source(q) * shard, shard)
-        copies.append(pltpu.make_async_copy(ref, weight.at[pl.ds(at, shard)], weight_sem.at[q]))
-    for copy in sent_copies + copies:
-        copy.start()
+    grp_id = lax.axis_index("grp")
+    pieces = [(weight_own, 0, 0, shard)]
+    for q in range(1, NR):
+        pieces.append((weight_ring[q - 1], q, grp_id * part, part))
+    for batch, group in zip(weight_across, CROSSING):
+        for i, q in enumerate(group):
+            pieces.append((batch.at[pl.ds(i * part, part)], q, (1 - grp_id) * part, part))
+    for q, ref in enumerate(sent_in):
+        sent[q] = ref[...]
+    for ref, q, begin, count in pieces:
+        at = pl.multiple_of(ring_source(q) * shard + begin, part)
+        weight[pl.ds(at, count)] = ref[...]
 
     first = (lax.axis_index("wide") * experts).astype(F32)
     before = lax.broadcasted_iota(jnp.int32, (toks, toks), 0) < lax.broadcasted_iota(jnp.int32, (toks, toks), 1)
@@ -177,7 +194,6 @@
     picks = []
     missed = jnp.int32(0)
     for q in range(NR):
-        sent_copies[q].wait()
         info = sent[q, toks:].astype(F32)
         for s in range(slots):
             flag = info[TOP + s, 0] > 0.5
@@ -214,9 +230,6 @@
         def _(i=i):
             packed[i] = tile_of(i)[...]
 
-    for copy in copies:
-        copy.wait()
-
     group = 4
     for i in range(0, most, group):
 
@@ -263,8 +276,33 @@
             out[h, k : k + rows, inner:] = parted[rows:]
 
 
-def first_kernel(rows, *refs):
-    first_matmuls(rows, refs[:-1], refs[-1])
+def first_kernel(base, rows, held, gate_up, out, wbuf, spread, sem):
+    per = held.shape[0]
+    rest = wbuf.shape[0]
+    _, most, width = rows.shape
+    inner = out.shape[2] // 2
+    copies = [pltpu.make_async_copy(gate_up.at[base + h], wbuf.at[h], sem.at[h]) for h in range(rest)]
+    for copy in copies:
+        copy.start()
+    lane = 128
+    src = lax.broadcasted_iota(jnp.int32, (lane, 4 * lane), 0)
+    dst = lax.broadcasted_iota(jnp.int32, (lane, 4 * lane), 1)
+    place = ((dst == 2 * src) | (dst == 2 * src + 1 + 2 * lane)).astype(F32).astype(BF16)
+    for e in range(rest // 2):
+        mine = rows[per // 2 + e]
+        stacked = jnp.concatenate([mine[:, c : c + lane] for c in range(0, width, lane)], axis=0)
+        both = jnp.dot(stacked, place, preferred_element_type=F32).astype(BF16)
+        for c in range(width // lane):
+            at = slice(2 * lane * c, 2 * lane * (c + 1))
+            spread[e, :most, at] = both[most * c : most * (c + 1), : 2 * lane]
+            spread[e, most:, at] = both[most * c : most * (c + 1), 2 * lane :]
+    for h in range(per):
+        out[h] = jnp.dot(rows[h // 2], held[h], preferred_element_type=F32).astype(BF16)
+    for h in range(rest):
+        copies[h].wait()
+        acc = jnp.dot(spread[h // 2], wbuf[h].reshape(2 * width, inner), preferred_element_type=F32)
+        out[per + h, :, :inner] = acc[:most].astype(BF16)
+        out[per + h, :, inner:] = acc[most:].astype(BF16)
 
 
 def gated_hidden(own, other):
@@ -345,18 +383,17 @@
     shard = adapter_weight.shape[0]
     params = pltpu.CompilerParams(vmem_limit_bytes=VMEM_LIMIT)
 
-    def message(*passing):
-        hidden, *passing = tie(tile_hidden, *passing)
+    def message():
         cache_hit = jnp.any(tile_image[:, None] == cache_ids[None, :], axis=1)
         tokens_own = jnp.where(
-            cache_hit[:, None, None], cached_rows.reshape(slots, tile_rows, half_width), activate(hidden)
+            cache_hit[:, None, None], cached_rows.reshape(slots, tile_rows, half_width), activate(tile_hidden)
         ).reshape(toks, half_width)
         flags = jnp.broadcast_to(jnp.where(cache_hit, 0.0, 1.0).astype(BF16)[:, None], (slots, toks))
         info_own = jnp.concatenate([routes.T.astype(BF16), flags, jnp.zeros((16 - TOP - slots, toks), BF16)])
         gates = [jnp.pad(piece, ((0, 16 - TOP), (0, 0))) for piece in split3(route_gates.T)]
         info_own = jnp.concatenate([info_own] + gates, axis=1)
         info_own = jnp.pad(info_own, ((0, 0), (0, half_width - 4 * toks)))
-        return jnp.concatenate([tokens_own, info_own]), *passing
+        return jnp.concatenate([tokens_own, info_own])
 
     def fetch(base, count, limit):
         shape = (count, half_width, 2 * inner)
@@ -377,15 +414,18 @@
 
     near = experts // 2
     far = experts - near
-    count = halves // len(FETCH_LIMITS)
+    count = halves // 4
     fetches = [functools.partial(fetch, i * count, count, limit) for i, limit in enumerate(FETCH_LIMITS)]
-    weight_ring, sent, fetched = ring_gather_two(adapter_weight, message, fetches)
-    fetched_near, fetched_far = fetched[: len(fetched) // 2], fetched[len(fetched) // 2 :]
+    part = shard // 2
+    weight_part = jnp.where(lax.axis_index("grp") == 0, adapter_weight[:part], adapter_weight[part:])
+    weight_ring, sent, fetched, weight_across = ring_gather_two(weight_part, message, fetches)
+    weight_in = [adapter_weight, *weight_ring[1:], *weight_across]
+    *fetched_near, fetched_far = fetched
     most = NR * CAP
     pre_shape = jax.ShapeDtypeStruct((2 * near, most, 2 * inner), BF16)
     rows, mix, own_near = pl.pallas_call(
         functools.partial(prologue_kernel, experts, slots, tile_rows),
-        in_specs=[ANY] * (2 * NR) + [VM] * len(fetched_near) + [ANY],
+        in_specs=[VM] * (NR + len(weight_in)) + [VM] * len(fetched_near),
         out_specs=[VM, VM, VM],
         out_shape=[
             jax.ShapeDtypeStruct((far, most, half_width), BF16),
@@ -398,23 +438,26 @@
             pltpu.VMEM((NR * slots // 2, tile_rows, half_width), BF16),
             pltpu.VMEM((near, most, half_width), BF16),
             pltpu.SMEM((NR * slots,), jnp.int32),
-            pltpu.SemaphoreType.DMA((NR,)),
-            pltpu.SemaphoreType.DMA((NR,)),
         ],
         compiler_params=pltpu.CompilerParams(vmem_limit_bytes=VMEM_SMALL),
-    )(*sent, *weight_ring, *fetched_near, fetched_far[-1])
+    )(*sent, *weight_in, *fetched_near)
     other_near = swap(own_near, "narrow")
 
     own_far = pl.pallas_call(
-        first_kernel,
-        in_specs=[VM] * (1 + len(fetched_far)),
+        functools.partial(first_kernel, 3 * count),
+        in_specs=[VM, VM, ANY],
         out_specs=VM,
         out_shape=jax.ShapeDtypeStruct((2 * far, most, 2 * inner), BF16),
-        compiler_params=pltpu.CompilerParams(vmem_limit_bytes=VMEM_SMALL),
+        scratch_shapes=[
+            pltpu.VMEM((count, half_width, 2, inner), BF16),
+            pltpu.VMEM((count // 2, 2 * most, 2 * half_width), BF16),
+            pltpu.SemaphoreType.DMA((count,)),
+        ],
+        compiler_params=pltpu.CompilerParams(vmem_limit_bytes=VMEM_FAR),
         cost_estimate=pl.CostEstimate(
             flops=16 * most * half_width * far * inner, bytes_accessed=8 * far * half_width * inner, transcendentals=0
         ),
-    )(rows, *fetched_far)
+    )(rows, fetched_far, gate_up)
     own_far, other_near = tie(own_far, other_near)
     other_far = swap(own_far, "narrow")
 

time: 112 us -> 104 us (0.929)
  waiting for transfers between devices: 30 us -> 21.8 us
  starting transfers between devices: 30.7 us -> 35.6 us
  Pallas kernels: 38.4 us -> 35.6 us
  local copies, waits for them, and re-layouts: 5.76 us -> 3.02 us
    ppermute x14, waiting for transfers between devices: 18 us -> 9.39 us  [from_prev(): return lax.ppermute(value, 'wide', ring_pairs(1))]
    ppermute x14, starting transfers between devices: 8.12 us -> 14 us  [from_next(): return lax.ppermute(value, 'wide', ring_pairs(-1))]
    ppermute x2 -> x5, waiting for transfers between devices: 0.01 us -> 5.76 us  [swap(): return lax.ppermute(value, axis, [(0, 1), (1, 0)])]
    ppermute x14, waiting for transfers between devices: 12 us -> 6.66 us  [from_next(): return lax.ppermute(value, 'wide', ring_pairs(-1))]
    pallas_call x4 -> x3, Pallas kernels: 18.8 us -> 13.6 us  [fetch(): pl.pallas_call(functools.partial(fetch_kernel, base), in_specs=[ANY], out...]
    ppermute x14, starting transfers between devices: 22.5 us -> 17.4 us  [from_prev(): return lax.ppermute(value, 'wide', ring_pairs(1))]
    ppermute x2 -> x5, starting transfers between devices: 0.14 us -> 4.24 us  [swap(): return lax.ppermute(value, axis, [(0, 1), (1, 0)])]
    pallas_call x1, Pallas kernels: 2.35 us -> 6.18 us  [on_device_ring(): pl.pallas_call(functools.partial(first_kernel, 3 * count), in_specs=[VM,...]
  transfers between devices with their start and end apart: 30 -> 33, of which waited for: 14 -> 11; matrix products, arithmetic and copies ran while one was open for 3% -> 5% of each run, Pallas kernels for 26% -> 26%
where the time goes in v3:
time: 104 us
  starting transfers between devices  35.6 us (34%)
  Pallas kernels  35.6 us (34%)
  waiting for transfers between devices  21.8 us (21%)
  other arithmetic  7.37 us (7%)
  local copies, waits for them, and re-layouts  3.02 us (3%)
    ppermute x14, starting transfers between devices, from_prev(): return lax.ppermute(value, 'wide', ring_pairs(1))  17.4 us
    ppermute x14, starting transfers between devices, from_next(): return lax.ppermute(value, 'wide', ring_pairs(-1))  14 us
    pallas_call x3, Pallas kernels, fetch(): pl.pallas_call(functools.partial(fetch_kernel, base), in_specs=[ANY], out...  13.6 us
    ppermute x14, waiting for transfers between devices, from_prev(): return lax.ppermute(value, 'wide', ring_pairs(1))  9.39 us
    ppermute x14, waiting for transfers between devices, from_next(): return lax.ppermute(value, 'wide', ring_pairs(-1))  6.66 us
    pallas_call x2, Pallas kernels, on_device_ring(): pl.pallas_call(functools.partial(second_far_kernel, 2 * near, c, width),...  6.34 us
    pallas_call x1, Pallas kernels, on_device_ring(): pl.pallas_call(functools.partial(first_kernel, 3 * count), in_specs=[VM,...  6.18 us
    ppermute x5, waiting for transfers between devices, swap(): return lax.ppermute(value, axis, [(0, 1), (1, 0)])  5.76 us
  transfers between devices with their start and end apart: 33, of which 11 were waited for; matrix products, arithmetic and copies ran while one was open for 5% of the time, Pallas kernels for 26%

profile of v3, /device:TPU:0, one launch (start us, length us, event | category | flops | bytes accessed | tf_op | source)
XLA Modules:
  0.0 103.7 jit_solution(9462629250748894466)
XLA Ops:
  0.0 1.0 slice_select_fusion
  1.0 3.0 %collective-permute-start.1 = (bf16[64,1024]{1,0:T(8,128)(2,1)S(1)}, bf16[64,1024]{1,0:T(8,128)(2,1)S(1)}, u32[]{:S(2)}, u32[]{:S(2)}) collective-permute-start(bf16[64,1024]{1,0:T(8,128)(2,1)S(1)} %slice_select_fusion), channel_id=1, source_target_pairs={{0,2},{4,0},{8,4},{12,8},{14,12},{10,14},{6,10},{2,6},{1,3},{5,1},... | collective-permute-start | bytes 393224 | tf_op jit(solution)/shard_map/ppermute | solution.py:93
  4.1 0.7 bitcast_convert_fusion
  4.8 0.7 fusion.42
  5.5 0.9 compare_reduce_fusion
  6.4 0.7 convert_bitcast_fusion
  7.1 2.2 %fusion.33 = bf16[2,64,1024]{2,1,0:T(8,128)(2,1)S(1)} fusion(bf16[2,64,1024]{2,1,0:T(8,128)(2,1)} %bitcast.18, bf16[2,64,1024]{2,1,0:T(8,128)(2,1)} %param.9, pred[2]{0:T(512)(128)(4,1)S(1)} %compare_reduce_fusion), kind=kLoop, calls=%fused_computation.38 | loop fusion | flops 8781824 | bytes 786434 | tf_op jit(solution)/shard_map/jit(_where)/select_n | solution.py:388
  9.4 1.9 %collective-permute-start.3 = (bf16[144,1024]{1,0:T(8,128)(2,1)S(1)}, bf16[144,1024]{1,0:T(8,128)(2,1)S(1)}, u32[]{:S(2)}, u32[]{:S(2)}) collective-permute-start(bf16[144,1024]{1,0:T(8,128)(2,1)S(1)} %fusion.32.refs_0_), channel_id=1, source_target_pairs={{0,2},{4,0},{8,4},{12,8},{14,12},{10,14},{6,10},{2,6},{1,3},{5,1},... | collective-permute-start | bytes 884744 | tf_op jit(solution)/shard_map/ppermute | solution.py:93
  11.5 2.0 %collective-permute-start.4 = (bf16[64,1024]{1,0:T(8,128)(2,1)S(1)}, bf16[64,1024]{1,0:T(8,128)(2,1)S(1)}, u32[]{:S(2)}, u32[]{:S(2)}) collective-permute-start(bf16[64,1024]{1,0:T(8,128)(2,1)S(1)} %collective-permute-done.refs_9_), channel_id=1, source_target_pairs={{0,4},{4,8},{8,12},{12,14},{14,10},{10,6},{6,2},{2,0},{1,5},{5,9},... | collective-permute-start | bytes 393224 | tf_op jit(solution)/shard_map/ppermute | solution.py:89
  13.5 4.5 %shard_map.91.refs_19_ = bf16[4,1024,1024]{2,1,0:T(8,128)(2,1)S(1)} custom-call(bf16[16,1024,2,512]{3,2,1,0:T(2,128)(2,1)} %gate_up.7), custom_call_target="tpu_custom_call" | custom-call | flops 2147483648 | bytes 16777216 | tf_op jit(solution)/shard_map/pallas_call | solution.py:400
  18.1 4.0 %collective-permute-done.4.refs_10_ = bf16[64,1024]{1,0:T(8,128)(2,1)S(1)} collective-permute-done((bf16[64,1024]{1,0:T(8,128)(2,1)S(1)}, bf16[64,1024]{1,0:T(8,128)(2,1)S(1)}, u32[]{:S(2)}, u32[]{:S(2)}) %collective-permute-start.4) | collective-permute-done | bytes 131104 | tf_op jit(solution)/shard_map/ppermute | solution.py:89
  22.5 1.6 %collective-permute-start.7 = (bf16[144,1024]{1,0:T(8,128)(2,1)S(1)}, bf16[144,1024]{1,0:T(8,128)(2,1)S(1)}, u32[]{:S(2)}, u32[]{:S(2)}) collective-permute-start(bf16[144,1024]{1,0:T(8,128)(2,1)S(1)} %collective-permute-done.3.refs_7_), channel_id=1, source_target_pairs={{0,2},{4,0},{8,4},{12,8},{14,12},{10,14},{6,10},{2,6},{1,3},{5,1},... | collective-permute-start | bytes 884744 | tf_op jit(solution)/shard_map/ppermute | solution.py:93
  24.2 1.6 %collective-permute-start.13 = (bf16[256,1024]{1,0:T(8,128)(2,1)S(1)}, bf16[256,1024]{1,0:T(8,128)(2,1)S(1)}, u32[]{:S(2)}, u32[]{:S(2)}) collective-permute-start(bf16[256,1024]{1,0:T(8,128)(2,1)S(1)} %pad_maximum_fusion), channel_id=1, source_target_pairs={{0,16},{16,0},{1,17},{17,1},{2,18},{18,2},{3,19},{19,3},{4,20},{20... | collective-permute-start | bytes 1572872 | tf_op jit(solution)/shard_map/ppermute | solution.py:97
  25.8 0.5 collective-permute-start.8
  26.3 1.5 %collective-permute-start.9 = (bf16[64,1024]{1,0:T(8,128)(2,1)S(1)}, bf16[64,1024]{1,0:T(8,128)(2,1)S(1)}, u32[]{:S(2)}, u32[]{:S(2)}) collective-permute-start(bf16[64,1024]{1,0:T(8,128)(2,1)S(1)} %collective-permute-done.5.refs_14_), channel_id=1, source_target_pairs={{0,2},{4,0},{8,4},{12,8},{14,12},{10,14},{6,10},{2,6},{1,3},{5,1},... | collective-permute-start | bytes 393224 | tf_op jit(solution)/shard_map/ppermute | solution.py:93
  27.8 4.5 %shard_map.92.refs_20_ = bf16[4,1024,1024]{2,1,0:T(8,128)(2,1)S(1)} custom-call(bf16[16,1024,2,512]{3,2,1,0:T(2,128)(2,1)} %gate_up.7), custom_call_target="tpu_custom_call" | custom-call | flops 2147483648 | bytes 16777216 | tf_op jit(solution)/shard_map/pallas_call | solution.py:400
  32.4 1.4 %collective-permute-start.10 = (bf16[144,1024]{1,0:T(8,128)(2,1)S(1)}, bf16[144,1024]{1,0:T(8,128)(2,1)S(1)}, u32[]{:S(2)}, u32[]{:S(2)}) collective-permute-start(bf16[144,1024]{1,0:T(8,128)(2,1)S(1)} %collective-permute-done.6.refs_2_), channel_id=1, source_target_pairs={{0,4},{4,8},{8,12},{12,14},{14,10},{10,6},{6,2},{2,0},{1,5},{5,9},... | collective-permute-start | bytes 884744 | tf_op jit(solution)/shard_map/ppermute | solution.py:89
  33.8 0.7 collective-permute-start.11
  34.5 1.6 %collective-permute-start.12 = (bf16[64,1024]{1,0:T(8,128)(2,1)S(1)}, bf16[64,1024]{1,0:T(8,128)(2,1)S(1)}, u32[]{:S(2)}, u32[]{:S(2)}) collective-permute-start(bf16[64,1024]{1,0:T(8,128)(2,1)S(1)} %collective-permute-done.9.refs_13_), channel_id=1, source_target_pairs={{0,2},{4,0},{8,4},{12,8},{14,12},{10,14},{6,10},{2,6},{1,3},{5,1},... | collective-permute-start | bytes 393224 | tf_op jit(solution)/shard_map/ppermute | solution.py:93
  36.0 4.5 %shard_map.93.held = bf16[4,1024,1024]{2,1,0:T(8,128)(2,1)S(1)} custom-call(bf16[16,1024,2,512]{3,2,1,0:T(2,128)(2,1)} %gate_up.7), custom_call_target="tpu_custom_call" | custom-call | flops 2147483648 | bytes 16777216 | tf_op jit(solution)/shard_map/pallas_call | solution.py:400
  40.6 1.6 %collective-permute-done.12.refs_12_ = bf16[64,1024]{1,0:T(8,128)(2,1)S(1)} collective-permute-done((bf16[64,1024]{1,0:T(8,128)(2,1)S(1)}, bf16[64,1024]{1,0:T(8,128)(2,1)S(1)}, u32[]{:S(2)}, u32[]{:S(2)}) %collective-permute-start.12) | collective-permute-done | bytes 131104 | tf_op jit(solution)/shard_map/ppermute | solution.py:93
  42.2 1.6 %collective-permute-start.14 = (bf16[144,1024]{1,0:T(8,128)(2,1)S(1)}, bf16[144,1024]{1,0:T(8,128)(2,1)S(1)}, u32[]{:S(2)}, u32[]{:S(2)}) collective-permute-start(bf16[144,1024]{1,0:T(8,128)(2,1)S(1)} %collective-permute-done.10.refs_3_), channel_id=1, source_target_pairs={{0,4},{4,8},{8,12},{12,14},{14,10},{10,6},{6,2},{2,0},{1,5},{5,9},... | collective-permute-start | bytes 884744 | tf_op jit(solution)/shard_map/ppermute | solution.py:89
  43.8 1.6 %collective-permute-start.15 = (bf16[128,1024]{1,0:T(8,128)(2,1)S(1)}, bf16[128,1024]{1,0:T(8,128)(2,1)S(1)}, u32[]{:S(2)}, u32[]{:S(2)}) collective-permute-start(bf16[128,1024]{1,0:T(8,128)(2,1)S(1)} %pad_maximum_fusion.1), channel_id=1, source_target_pairs={{0,16},{16,0},{1,17},{17,1},{2,18},{18,2},{3,19},{19,3},{4,20},{20... | collective-permute-start | bytes 786440 | tf_op jit(solution)/shard_map/ppermute | solution.py:97
  45.9 4.3 %collective-permute-done.15.refs_17_ = bf16[128,1024]{1,0:T(8,128)(2,1)S(1)} collective-permute-done((bf16[128,1024]{1,0:T(8,128)(2,1)S(1)}, bf16[128,1024]{1,0:T(8,128)(2,1)S(1)}, u32[]{:S(2)}, u32[]{:S(2)}) %collective-permute-start.15) | collective-permute-done | bytes 262176 | tf_op jit(solution)/shard_map/ppermute | solution.py:97
  50.3 1.4 %collective-permute-done.16.refs_18_ = bf16[64,1024]{1,0:T(8,128)(2,1)S(1)} collective-permute-done((bf16[64,1024]{1,0:T(8,128)(2,1)S(1)}, bf16[64,1024]{1,0:T(8,128)(2,1)S(1)}, u32[]{:S(2)}, u32[]{:S(2)}) %collective-permute-start.16) | collective-permute-done | bytes 131104 | tf_op jit(solution)/shard_map/ppermute | solution.py:97
  51.7 5.2 %shard_map.94 = (bf16[4,128,1024]{2,1,0:T(8,128)(2,1)S(1)}, bf16[8,2,128,128]{3,2,1,0:T(8,128)(2,1)S(1)}, bf16[8,128,1024]{2,1,0:T(8,128)(2,1)S(1)}) custom-call(bf16[144,1024]{1,0:T(8,128)(2,1)S(1)} %fusion.32.refs_0_, bf16[144,1024]{1,0:T(8,128)(2,1)S(1)} %collective-permute-done.2.refs_1_, bf16[144,1024]{1,0:T(8,128)(2,1)S(1)} %collective-permute-done.6.refs_2_, ...), custom_call_target="tpu_custom_call" | custom-call | tf_op jit(solution)/shard_map/pallas_call | solution.py:426
  57.0 6.2 %shard_map.95.refs_0_ = bf16[8,128,1024]{2,1,0:T(8,128)(2,1)S(1)} custom-call(bf16[4,128,1024]{2,1,0:T(8,128)(2,1)S(1)} %get-tuple-element.84.rows, bf16[4,1024,1024]{2,1,0:T(8,128)(2,1)S(1)} %shard_map.93.held, bf16[16,1024,2,512]{3,2,1,0:T(2,128)(2,1)} %gate_up.7), custom_call_target="tpu_custom_call" | custom-call | flops 4294967296 | bytes 16777216 | tf_op jit(solution)/shard_map/pallas_call | solution.py:446
  63.2 1.3 %copy-done = bf16[8,128,1024]{2,1,0:T(8,128)(2,1)} copy-done((bf16[8,128,1024]{2,1,0:T(8,128)(2,1)}, bf16[8,128,1024]{2,1,0:T(8,128)(2,1)S(1)}, u32[]{:S(2)}) %copy-start) | copy-done | bytes 2097176
  65.0 1.6 %copy-done.1 = bf16[8,128,1024]{2,1,0:T(8,128)(2,1)S(1)} copy-done((bf16[8,128,1024]{2,1,0:T(8,128)(2,1)S(1)}, bf16[8,128,1024]{2,1,0:T(8,128)(2,1)}, u32[]{:S(2)}) %copy-start.1) | copy-done | bytes 2097176
  66.6 4.2 %shard_map.96.refs_2_.refs_1_ = bf16[4,128,1024]{2,1,0:T(8,128)(2,1)S(1)} custom-call(bf16[8,128,1024]{2,1,0:T(8,128)(2,1)S(1)} %get-tuple-element.86.own, bf16[8,128,1024]{2,1,0:T(8,128)(2,1)S(1)} %copy-done.1, bf16[16,512,1024]{2,1,0:T(8,128)(2,1)} %refs_3_.1), custom_call_target="tpu_custom_call" | custom-call | flops 1073741824 | bytes 8388608 | tf_op jit(solution)/shard_map/pallas_call | solution.py:464
  70.9 3.2 %shard_map.97 = (bf16[8,128,512]{2,1,0:T(8,128)(2,1)S(1)}, bf16[128,512]{1,0:T(8,128)(2,1)S(1)}, bf16[128,512]{1,0:T(8,128)(2,1)S(1)}, bf16[128,512]{1,0:T(8,128...) custom-call(bf16[8,128,1024]{2,1,0:T(8,128)(2,1)S(1)} %shard_map.95., ...), custom_call_target="tpu_custom_call" | custom-call | flops 536870912 | bytes 4194304 | tf_op jit(solution)/shard_map/pallas_call | solution.py:485
  74.1 0.5 collective-permute-start.19
  74.6 1.6 %collective-permute-start.23 = (bf16[128,512]{1,0:T(8,128)(2,1)S(1)}, bf16[128,512]{1,0:T(8,128)(2,1)S(1)}, u32[]{:S(2)}, u32[]{:S(2)}) collective-permute-start(bf16[128,512]{1,0:T(8,128)(2,1)S(1)} %get-tuple-element.97), channel_id=1, source_target_pairs={{0,4},{4,8},{8,12},{12,14},{14,10},{10,6},{6,2},{2,0},{1,5},{5,9},... | collective-permute-start | bytes 393224 | tf_op jit(solution)/shard_map/ppermute | solution.py:89
  76.1 3.2 %shard_map.98 = (bf16[128,512]{1,0:T(8,128)(2,1)S(1)}, bf16[128,512]{1,0:T(8,128)(2,1)S(1)}, bf16[128,512]{1,0:T(8,128)(2,1)S(1)}, bf16[128,512]{1,0:T(8,128)(2,...) custom-call(bf16[8,128,512]{2,1,0:T(8,128)(2,1)S(1)} %get-tuple-elem, ...), custom_call_target="tpu_custom_call" | custom-call | flops 536870912 | bytes 4194304 | tf_op jit(solution)/shard_map/pallas_call | solution.py:485
  79.8 1.6 %collective-permute-start.29 = (bf16[128,512]{1,0:T(8,128)(2,1)S(1)}, bf16[128,512]{1,0:T(8,128)(2,1)S(1)}, u32[]{:S(2)}, u32[]{:S(2)}) collective-permute-start(bf16[128,512]{1,0:T(8,128)(2,1)S(1)} %get-tuple-element.105), channel_id=1, source_target_pairs={{0,4},{4,8},{8,12},{12,14},{14,10},{10,6},{6,2},{2,0},{1,5},{5,9},... | collective-permute-start | bytes 393224 | tf_op jit(solution)/shard_map/ppermute | solution.py:89
  82.0 1.6 %collective-permute-start.24 = (bf16[128,512]{1,0:T(8,128)(2,1)S(1)}, bf16[128,512]{1,0:T(8,128)(2,1)S(1)}, u32[]{:S(2)}, u32[]{:S(2)}) collective-permute-start(bf16[128,512]{1,0:T(8,128)(2,1)S(1)} %add_convert_fusion.8), channel_id=1, source_target_pairs={{0,4},{4,8},{8,12},{12,14},{14,10},{10,6},{6,2},{2,0},{1,5},{5,9},... | collective-permute-start | bytes 393224 | tf_op jit(solution)/shard_map/ppermute | solution.py:89
  83.6 2.1 %collective-permute-done.26 = bf16[128,512]{1,0:T(8,128)(2,1)S(1)} collective-permute-done((bf16[128,512]{1,0:T(8,128)(2,1)S(1)}, bf16[128,512]{1,0:T(8,128)(2,1)S(1)}, u32[]{:S(2)}, u32[]{:S(2)}) %collective-permute-start.26) | collective-permute-done | bytes 131104 | tf_op jit(solution)/shard_map/ppermute | solution.py:93
  86.2 1.6 %collective-permute-start.30 = (bf16[128,512]{1,0:T(8,128)(2,1)S(1)}, bf16[128,512]{1,0:T(8,128)(2,1)S(1)}, u32[]{:S(2)}, u32[]{:S(2)}) collective-permute-start(bf16[128,512]{1,0:T(8,128)(2,1)S(1)} %add_convert_fusion.3), channel_id=1, source_target_pairs={{0,4},{4,8},{8,12},{12,14},{14,10},{10,6},{6,2},{2,0},{1,5},{5,9},... | collective-permute-start | bytes 393224 | tf_op jit(solution)/shard_map/ppermute | solution.py:89
  87.9 0.6 collective-permute-done.20
  89.0 1.7 %collective-permute-start.25 = (bf16[128,512]{1,0:T(8,128)(2,1)S(1)}, bf16[128,512]{1,0:T(8,128)(2,1)S(1)}, u32[]{:S(2)}, u32[]{:S(2)}) collective-permute-start(bf16[128,512]{1,0:T(8,128)(2,1)S(1)} %add_convert_fusion.7), channel_id=1, source_target_pairs={{0,4},{4,8},{8,12},{12,14},{14,10},{10,6},{6,2},{2,0},{1,5},{5,9},... | collective-permute-start | bytes 393224 | tf_op jit(solution)/shard_map/ppermute | solution.py:89
  90.7 0.8 collective-permute-done.27
  91.5 0.6 collective-permute-start.28
  92.1 1.5 %collective-permute-start.31 = (bf16[128,512]{1,0:T(8,128)(2,1)S(1)}, bf16[128,512]{1,0:T(8,128)(2,1)S(1)}, u32[]{:S(2)}, u32[]{:S(2)}) collective-permute-start(bf16[128,512]{1,0:T(8,128)(2,1)S(1)} %add_convert_fusion.2), channel_id=1, source_target_pairs={{0,4},{4,8},{8,12},{12,14},{14,10},{10,6},{6,2},{2,0},{1,5},{5,9},... | collective-permute-start | bytes 393224 | tf_op jit(solution)/shard_map/ppermute | solution.py:89
  93.6 1.2 %collective-permute-done.21 = bf16[128,512]{1,0:T(8,128)(2,1)S(1)} collective-permute-done((bf16[128,512]{1,0:T(8,128)(2,1)S(1)}, bf16[128,512]{1,0:T(8,128)(2,1)S(1)}, u32[]{:S(2)}, u32[]{:S(2)}) %collective-permute-start.21) | collective-permute-done | bytes 131104 | tf_op jit(solution)/shard_map/ppermute | solution.py:93
  95.4 2.4 %collective-permute-done.31 = bf16[128,512]{1,0:T(8,128)(2,1)S(1)} collective-permute-done((bf16[128,512]{1,0:T(8,128)(2,1)S(1)}, bf16[128,512]{1,0:T(8,128)(2,1)S(1)}, u32[]{:S(2)}, u32[]{:S(2)}) %collective-permute-start.31) | collective-permute-done | bytes 131104 | tf_op jit(solution)/shard_map/ppermute | solution.py:89
  97.8 1.6 %collective-permute-start.32 = (bf16[128,512]{1,0:T(8,128)(2,1)S(1)}, bf16[128,512]{1,0:T(8,128)(2,1)S(1)}, u32[]{:S(2)}, u32[]{:S(2)}) collective-permute-start(bf16[128,512]{1,0:T(8,128)(2,1)S(1)} %add_convert_fusion.1), channel_id=1, source_target_pairs={{0,4},{4,8},{8,12},{12,14},{14,10},{10,6},{6,2},{2,0},{1,5},{5,9},... | collective-permute-start | bytes 393224 | tf_op jit(solution)/shard_map/ppermute | solution.py:89
  99.9 2.9 %collective-permute-done.32 = bf16[128,512]{1,0:T(8,128)(2,1)S(1)} collective-permute-done((bf16[128,512]{1,0:T(8,128)(2,1)S(1)}, bf16[128,512]{1,0:T(8,128)(2,1)S(1)}, u32[]{:S(2)}, u32[]{:S(2)}) %collective-permute-start.32) | collective-permute-done | bytes 131104 | tf_op jit(solution)/shard_map/ppermute | solution.py:89
  102.9 0.7 pad_maximum_fusion.2
  (58 shorter events, 5.6 us)
Async XLA Ops:
  1.0 8.4 %collective-permute-start.1 = (bf16[64,1024]{1,0:T(8,128)(2,1)S(1)}, bf16[64,1024]{1,0:T(8,128)(2,1)S(1)}, u32[]{:S(2)}, u32[]{:S(2)}) collective-permute-start(bf16[64,1024]{1,0:T(8,128)(2,1)S(1)} %slice_select_fusion), channel_id=1, source_target_pairs={{0,2},{4,0},{8,4},{12,8},{14,12},{10,14},{6,10},{2,6},{1,3},{5,1},... | collective-permute-start | bytes 393224 | tf_op jit(solution)/shard_map/ppermute | solution.py:93
  4.0 5.4 %collective-permute-start = (bf16[64,1024]{1,0:T(8,128)(2,1)S(1)}, bf16[64,1024]{1,0:T(8,128)(2,1)S(1)}, u32[]{:S(2)}, u32[]{:S(2)}) collective-permute-start(bf16[64,1024]{1,0:T(8,128)(2,1)S(1)} %slice_select_fusion), channel_id=1, source_target_pairs={{0,4},{4,8},{8,12},{12,14},{14,10},{10,6},{6,2},{2,0},{1,5},{5,9},... | collective-permute-start | bytes 393224 | tf_op jit(solution)/shard_map/ppermute | solution.py:89
  9.4 12.7 %collective-permute-start.3 = (bf16[144,1024]{1,0:T(8,128)(2,1)S(1)}, bf16[144,1024]{1,0:T(8,128)(2,1)S(1)}, u32[]{:S(2)}, u32[]{:S(2)}) collective-permute-start(bf16[144,1024]{1,0:T(8,128)(2,1)S(1)} %fusion.32.refs_0_), channel_id=1, source_target_pairs={{0,2},{4,0},{8,4},{12,8},{14,12},{10,14},{6,10},{2,6},{1,3},{5,1},... | collective-permute-start | bytes 884744 | tf_op jit(solution)/shard_map/ppermute | solution.py:93
  11.3 10.7 %collective-permute-start.2 = (bf16[144,1024]{1,0:T(8,128)(2,1)S(1)}, bf16[144,1024]{1,0:T(8,128)(2,1)S(1)}, u32[]{:S(2)}, u32[]{:S(2)}) collective-permute-start(bf16[144,1024]{1,0:T(8,128)(2,1)S(1)} %fusion.32.refs_0_), channel_id=1, source_target_pairs={{0,4},{4,8},{8,12},{12,14},{14,10},{10,6},{6,2},{2,0},{1,5},{5,9},... | collective-permute-start | bytes 884744 | tf_op jit(solution)/shard_map/ppermute | solution.py:89
  11.5 10.6 %collective-permute-start.4 = (bf16[64,1024]{1,0:T(8,128)(2,1)S(1)}, bf16[64,1024]{1,0:T(8,128)(2,1)S(1)}, u32[]{:S(2)}, u32[]{:S(2)}) collective-permute-start(bf16[64,1024]{1,0:T(8,128)(2,1)S(1)} %collective-permute-done.refs_9_), channel_id=1, source_target_pairs={{0,4},{4,8},{8,12},{12,14},{14,10},{10,6},{6,2},{2,0},{1,5},{5,9},... | collective-permute-start | bytes 393224 | tf_op jit(solution)/shard_map/ppermute | solution.py:89
  13.4 8.6 %collective-permute-start.5 = (bf16[64,1024]{1,0:T(8,128)(2,1)S(1)}, bf16[64,1024]{1,0:T(8,128)(2,1)S(1)}, u32[]{:S(2)}, u32[]{:S(2)}) collective-permute-start(bf16[64,1024]{1,0:T(8,128)(2,1)S(1)} %collective-permute-done.1.refs_15_), channel_id=1, source_target_pairs={{0,2},{4,0},{8,4},{12,8},{14,12},{10,14},{6,10},{2,6},{1,3},{5,1},... | collective-permute-start | bytes 393224 | tf_op jit(solution)/shard_map/ppermute | solution.py:93
  22.1 10.3 %collective-permute-start.6 = (bf16[144,1024]{1,0:T(8,128)(2,1)S(1)}, bf16[144,1024]{1,0:T(8,128)(2,1)S(1)}, u32[]{:S(2)}, u32[]{:S(2)}) collective-permute-start(bf16[144,1024]{1,0:T(8,128)(2,1)S(1)} %collective-permute-done.2.refs_1_), channel_id=1, source_target_pairs={{0,4},{4,8},{8,12},{12,14},{14,10},{10,6},{6,2},{2,0},{1,5},{5,9},... | collective-permute-start | bytes 884744 | tf_op jit(solution)/shard_map/ppermute | solution.py:89
  22.5 9.8 %collective-permute-start.7 = (bf16[144,1024]{1,0:T(8,128)(2,1)S(1)}, bf16[144,1024]{1,0:T(8,128)(2,1)S(1)}, u32[]{:S(2)}, u32[]{:S(2)}) collective-permute-start(bf16[144,1024]{1,0:T(8,128)(2,1)S(1)} %collective-permute-done.3.refs_7_), channel_id=1, source_target_pairs={{0,2},{4,0},{8,4},{12,8},{14,12},{10,14},{6,10},{2,6},{1,3},{5,1},... | collective-permute-start | bytes 884744 | tf_op jit(solution)/shard_map/ppermute | solution.py:93
  24.2 18.0 %collective-permute-start.13 = (bf16[256,1024]{1,0:T(8,128)(2,1)S(1)}, bf16[256,1024]{1,0:T(8,128)(2,1)S(1)}, u32[]{:S(2)}, u32[]{:S(2)}) collective-permute-start(bf16[256,1024]{1,0:T(8,128)(2,1)S(1)} %pad_maximum_fusion), channel_id=1, source_target_pairs={{0,16},{16,0},{1,17},{17,1},{2,18},{18,2},{3,19},{19,3},{4,20},{20... | collective-permute-start | bytes 1572872 | tf_op jit(solution)/shard_map/ppermute | solution.py:97
  25.8 6.6 %collective-permute-start.8 = (bf16[64,1024]{1,0:T(8,128)(2,1)S(1)}, bf16[64,1024]{1,0:T(8,128)(2,1)S(1)}, u32[]{:S(2)}, u32[]{:S(2)}) collective-permute-start(bf16[64,1024]{1,0:T(8,128)(2,1)S(1)} %collective-permute-done.4.refs_10_), channel_id=1, source_target_pairs={{0,4},{4,8},{8,12},{12,14},{14,10},{10,6},{6,2},{2,0},{1,5},{5,9},... | collective-permute-start | bytes 393224 | tf_op jit(solution)/shard_map/ppermute | solution.py:89
  26.3 6.1 %collective-permute-start.9 = (bf16[64,1024]{1,0:T(8,128)(2,1)S(1)}, bf16[64,1024]{1,0:T(8,128)(2,1)S(1)}, u32[]{:S(2)}, u32[]{:S(2)}) collective-permute-start(bf16[64,1024]{1,0:T(8,128)(2,1)S(1)} %collective-permute-done.5.refs_14_), channel_id=1, source_target_pairs={{0,2},{4,0},{8,4},{12,8},{14,12},{10,14},{6,10},{2,6},{1,3},{5,1},... | collective-permute-start | bytes 393224 | tf_op jit(solution)/shard_map/ppermute | solution.py:93
  32.3 19.3 %copy-start.2 = (bf16[128,1024]{1,0:T(8,128)(2,1)S(1)}, bf16[128,1024]{1,0:T(8,128)(2,1)}, u32[]{:S(2)}) copy-start(bf16[128,1024]{1,0:T(8,128)(2,1)} %refs_8_.1) | copy-start | bytes 786436
  32.4 9.8 %collective-permute-start.10 = (bf16[144,1024]{1,0:T(8,128)(2,1)S(1)}, bf16[144,1024]{1,0:T(8,128)(2,1)S(1)}, u32[]{:S(2)}, u32[]{:S(2)}) collective-permute-start(bf16[144,1024]{1,0:T(8,128)(2,1)S(1)} %collective-permute-done.6.refs_2_), channel_id=1, source_target_pairs={{0,4},{4,8},{8,12},{12,14},{14,10},{10,6},{6,2},{2,0},{1,5},{5,9},... | collective-permute-start | bytes 884744 | tf_op jit(solution)/shard_map/ppermute | solution.py:89
  33.8 8.4 %collective-permute-start.11 = (bf16[144,1024]{1,0:T(8,128)(2,1)S(1)}, bf16[144,1024]{1,0:T(8,128)(2,1)S(1)}, u32[]{:S(2)}, u32[]{:S(2)}) collective-permute-start(bf16[144,1024]{1,0:T(8,128)(2,1)S(1)} %collective-permute-done.7.refs_6_), channel_id=1, source_target_pairs={{0,2},{4,0},{8,4},{12,8},{14,12},{10,14},{6,10},{2,6},{1,3},{5,1},... | collective-permute-start | bytes 884744 | tf_op jit(solution)/shard_map/ppermute | solution.py:93
  34.5 7.7 %collective-permute-start.12 = (bf16[64,1024]{1,0:T(8,128)(2,1)S(1)}, bf16[64,1024]{1,0:T(8,128)(2,1)S(1)}, u32[]{:S(2)}, u32[]{:S(2)}) collective-permute-start(bf16[64,1024]{1,0:T(8,128)(2,1)S(1)} %collective-permute-done.9.refs_13_), channel_id=1, source_target_pairs={{0,2},{4,0},{8,4},{12,8},{14,12},{10,14},{6,10},{2,6},{1,3},{5,1},... | collective-permute-start | bytes 393224 | tf_op jit(solution)/shard_map/ppermute | solution.py:93
  42.2 9.5 %collective-permute-start.14 = (bf16[144,1024]{1,0:T(8,128)(2,1)S(1)}, bf16[144,1024]{1,0:T(8,128)(2,1)S(1)}, u32[]{:S(2)}, u32[]{:S(2)}) collective-permute-start(bf16[144,1024]{1,0:T(8,128)(2,1)S(1)} %collective-permute-done.10.refs_3_), channel_id=1, source_target_pairs={{0,4},{4,8},{8,12},{12,14},{14,10},{10,6},{6,2},{2,0},{1,5},{5,9},... | collective-permute-start | bytes 884744 | tf_op jit(solution)/shard_map/ppermute | solution.py:89
  43.8 6.4 %collective-permute-start.15 = (bf16[128,1024]{1,0:T(8,128)(2,1)S(1)}, bf16[128,1024]{1,0:T(8,128)(2,1)S(1)}, u32[]{:S(2)}, u32[]{:S(2)}) collective-permute-start(bf16[128,1024]{1,0:T(8,128)(2,1)S(1)} %pad_maximum_fusion.1), channel_id=1, source_target_pairs={{0,16},{16,0},{1,17},{17,1},{2,18},{18,2},{3,19},{19,3},{4,20},{20... | collective-permute-start | bytes 786440 | tf_op jit(solution)/shard_map/ppermute | solution.py:97
  45.4 6.3 %collective-permute-start.16 = (bf16[64,1024]{1,0:T(8,128)(2,1)S(1)}, bf16[64,1024]{1,0:T(8,128)(2,1)S(1)}, u32[]{:S(2)}, u32[]{:S(2)}) collective-permute-start(bf16[64,1024]{1,0:T(8,128)(2,1)S(1)} %collective-permute-done.12.refs_12_), channel_id=1, source_target_pairs={{0,16},{16,0},{1,17},{17,1},{2,18},{18,2},{3,19},{19,3},{4,20},{20... | collective-permute-start | bytes 393224 | tf_op jit(solution)/shard_map/ppermute | solution.py:97
  56.9 6.3 %collective-permute-start.17 = (bf16[8,128,1024]{2,1,0:T(8,128)(2,1)S(1)}, bf16[8,128,1024]{2,1,0:T(8,128)(2,1)S(1)}, u32[]{:S(2)}, u32[]{:S(2)}) collective-permute-start(bf16[8,128,1024]{2,1,0:T(8,128)(2,1)S(1)} %get-tuple-element.86.own), channel_id=1, source_target_pairs={{0,1},{1,0},{2,3},{3,2},{4,5},{5,4},{6,7},{7,6},{8,9},{9,8},{10,11... | collective-permute-start | bytes 6291464 | tf_op jit(solution)/shard_map/ppermute | solution.py:97
  63.2 1.4 %copy-start = (bf16[8,128,1024]{2,1,0:T(8,128)(2,1)}, bf16[8,128,1024]{2,1,0:T(8,128)(2,1)S(1)}, u32[]{:S(2)}) copy-start(bf16[8,128,1024]{2,1,0:T(8,128)(2,1)S(1)} %collective-permute-done.17.other) | copy-start | bytes 6291460
  64.5 6.3 %collective-permute-start.18 = (bf16[8,128,1024]{2,1,0:T(8,128)(2,1)S(1)}, bf16[8,128,1024]{2,1,0:T(8,128)(2,1)S(1)}, u32[]{:S(2)}, u32[]{:S(2)}) collective-permute-start(bf16[8,128,1024]{2,1,0:T(8,128)(2,1)S(1)} %shard_map.95.refs_0_), channel_id=1, source_target_pairs={{0,1},{1,0},{2,3},{3,2},{4,5},{5,4},{6,7},{7,6},{8,9},{9,8},{10,11... | collective-permute-start | bytes 6291464 | tf_op jit(solution)/shard_map/ppermute | solution.py:97
  65.0 1.6 %copy-start.1 = (bf16[8,128,1024]{2,1,0:T(8,128)(2,1)S(1)}, bf16[8,128,1024]{2,1,0:T(8,128)(2,1)}, u32[]{:S(2)}) copy-start(bf16[8,128,1024]{2,1,0:T(8,128)(2,1)} %copy-done) | copy-start | bytes 6291460
  74.1 7.3 %collective-permute-start.19 = (bf16[128,512]{1,0:T(8,128)(2,1)S(1)}, bf16[128,512]{1,0:T(8,128)(2,1)S(1)}, u32[]{:S(2)}, u32[]{:S(2)}) collective-permute-start(bf16[128,512]{1,0:T(8,128)(2,1)S(1)} %get-tuple-element.93), channel_id=1, source_target_pairs={{0,2},{4,0},{8,4},{12,8},{14,12},{10,14},{6,10},{2,6},{1,3},{5,1},... | collective-permute-start | bytes 393224 | tf_op jit(solution)/shard_map/ppermute | solution.py:93
  74.6 7.4 %collective-permute-start.23 = (bf16[128,512]{1,0:T(8,128)(2,1)S(1)}, bf16[128,512]{1,0:T(8,128)(2,1)S(1)}, u32[]{:S(2)}, u32[]{:S(2)}) collective-permute-start(bf16[128,512]{1,0:T(8,128)(2,1)S(1)} %get-tuple-element.97), channel_id=1, source_target_pairs={{0,4},{4,8},{8,12},{12,14},{14,10},{10,6},{6,2},{2,0},{1,5},{5,9},... | collective-permute-start | bytes 393224 | tf_op jit(solution)/shard_map/ppermute | solution.py:89
  79.3 6.3 %collective-permute-start.26 = (bf16[128,512]{1,0:T(8,128)(2,1)S(1)}, bf16[128,512]{1,0:T(8,128)(2,1)S(1)}, u32[]{:S(2)}, u32[]{:S(2)}) collective-permute-start(bf16[128,512]{1,0:T(8,128)(2,1)S(1)} %get-tuple-element.102), channel_id=1, source_target_pairs={{0,2},{4,0},{8,4},{12,8},{14,12},{10,14},{6,10},{2,6},{1,3},{5,1},... | collective-permute-start | bytes 393224 | tf_op jit(solution)/shard_map/ppermute | solution.py:93
  79.8 6.4 %collective-permute-start.29 = (bf16[128,512]{1,0:T(8,128)(2,1)S(1)}, bf16[128,512]{1,0:T(8,128)(2,1)S(1)}, u32[]{:S(2)}, u32[]{:S(2)}) collective-permute-start(bf16[128,512]{1,0:T(8,128)(2,1)S(1)} %get-tuple-element.105), channel_id=1, source_target_pairs={{0,4},{4,8},{8,12},{12,14},{14,10},{10,6},{6,2},{2,0},{1,5},{5,9},... | collective-permute-start | bytes 393224 | tf_op jit(solution)/shard_map/ppermute | solution.py:89
  81.4 7.0 %collective-permute-start.20 = (bf16[128,512]{1,0:T(8,128)(2,1)S(1)}, bf16[128,512]{1,0:T(8,128)(2,1)S(1)}, u32[]{:S(2)}, u32[]{:S(2)}) collective-permute-start(bf16[128,512]{1,0:T(8,128)(2,1)S(1)} %add_convert_fusion.11), channel_id=1, source_target_pairs={{0,2},{4,0},{8,4},{12,8},{14,12},{10,14},{6,10},{2,6},{1,3},{5,1},... | collective-permute-start | bytes 393224 | tf_op jit(solution)/shard_map/ppermute | solution.py:93
  82.0 7.0 %collective-permute-start.24 = (bf16[128,512]{1,0:T(8,128)(2,1)S(1)}, bf16[128,512]{1,0:T(8,128)(2,1)S(1)}, u32[]{:S(2)}, u32[]{:S(2)}) collective-permute-start(bf16[128,512]{1,0:T(8,128)(2,1)S(1)} %add_convert_fusion.8), channel_id=1, source_target_pairs={{0,4},{4,8},{8,12},{12,14},{14,10},{10,6},{6,2},{2,0},{1,5},{5,9},... | collective-permute-start | bytes 393224 | tf_op jit(solution)/shard_map/ppermute | solution.py:89
  85.7 5.7 %collective-permute-start.27 = (bf16[128,512]{1,0:T(8,128)(2,1)S(1)}, bf16[128,512]{1,0:T(8,128)(2,1)S(1)}, u32[]{:S(2)}, u32[]{:S(2)}) collective-permute-start(bf16[128,512]{1,0:T(8,128)(2,1)S(1)} %add_convert_fusion.5), channel_id=1, source_target_pairs={{0,2},{4,0},{8,4},{12,8},{14,12},{10,14},{6,10},{2,6},{1,3},{5,1},... | collective-permute-start | bytes 393224 | tf_op jit(solution)/shard_map/ppermute | solution.py:93
  86.2 5.9 %collective-permute-start.30 = (bf16[128,512]{1,0:T(8,128)(2,1)S(1)}, bf16[128,512]{1,0:T(8,128)(2,1)S(1)}, u32[]{:S(2)}, u32[]{:S(2)}) collective-permute-start(bf16[128,512]{1,0:T(8,128)(2,1)S(1)} %add_convert_fusion.3), channel_id=1, source_target_pairs={{0,4},{4,8},{8,12},{12,14},{14,10},{10,6},{6,2},{2,0},{1,5},{5,9},... | collective-permute-start | bytes 393224 | tf_op jit(solution)/shard_map/ppermute | solution.py:89
  88.5 6.3 %collective-permute-start.21 = (bf16[128,512]{1,0:T(8,128)(2,1)S(1)}, bf16[128,512]{1,0:T(8,128)(2,1)S(1)}, u32[]{:S(2)}, u32[]{:S(2)}) collective-permute-start(bf16[128,512]{1,0:T(8,128)(2,1)S(1)} %add_convert_fusion.10), channel_id=1, source_target_pairs={{0,2},{4,0},{8,4},{12,8},{14,12},{10,14},{6,10},{2,6},{1,3},{5,1},... | collective-permute-start | bytes 393224 | tf_op jit(solution)/shard_map/ppermute | solution.py:93
  89.0 10.4 %collective-permute-start.25 = (bf16[128,512]{1,0:T(8,128)(2,1)S(1)}, bf16[128,512]{1,0:T(8,128)(2,1)S(1)}, u32[]{:S(2)}, u32[]{:S(2)}) collective-permute-start(bf16[128,512]{1,0:T(8,128)(2,1)S(1)} %add_convert_fusion.7), channel_id=1, source_target_pairs={{0,4},{4,8},{8,12},{12,14},{14,10},{10,6},{6,2},{2,0},{1,5},{5,9},... | collective-permute-start | bytes 393224 | tf_op jit(solution)/shard_map/ppermute | solution.py:89
  91.5 8.5 %collective-permute-start.28 = (bf16[128,512]{1,0:T(8,128)(2,1)S(1)}, bf16[128,512]{1,0:T(8,128)(2,1)S(1)}, u32[]{:S(2)}, u32[]{:S(2)}) collective-permute-start(bf16[128,512]{1,0:T(8,128)(2,1)S(1)} %add_convert_fusion.4), channel_id=1, source_target_pairs={{0,2},{4,0},{8,4},{12,8},{14,12},{10,14},{6,10},{2,6},{1,3},{5,1},... | collective-permute-start | bytes 393224 | tf_op jit(solution)/shard_map/ppermute | solution.py:93
  92.1 5.7 %collective-permute-start.31 = (bf16[128,512]{1,0:T(8,128)(2,1)S(1)}, bf16[128,512]{1,0:T(8,128)(2,1)S(1)}, u32[]{:S(2)}, u32[]{:S(2)}) collective-permute-start(bf16[128,512]{1,0:T(8,128)(2,1)S(1)} %add_convert_fusion.2), channel_id=1, source_target_pairs={{0,4},{4,8},{8,12},{12,14},{14,10},{10,6},{6,2},{2,0},{1,5},{5,9},... | collective-permute-start | bytes 393224 | tf_op jit(solution)/shard_map/ppermute | solution.py:89
  94.9 5.0 %collective-permute-start.22 = (bf16[128,512]{1,0:T(8,128)(2,1)S(1)}, bf16[128,512]{1,0:T(8,128)(2,1)S(1)}, u32[]{:S(2)}, u32[]{:S(2)}) collective-permute-start(bf16[128,512]{1,0:T(8,128)(2,1)S(1)} %add_convert_fusion.9), channel_id=1, source_target_pairs={{0,2},{4,0},{8,4},{12,8},{14,12},{10,14},{6,10},{2,6},{1,3},{5,1},... | collective-permute-start | bytes 393224 | tf_op jit(solution)/shard_map/ppermute | solution.py:93
  97.8 5.0 %collective-permute-start.32 = (bf16[128,512]{1,0:T(8,128)(2,1)S(1)}, bf16[128,512]{1,0:T(8,128)(2,1)S(1)}, u32[]{:S(2)}, u32[]{:S(2)}) collective-permute-start(bf16[128,512]{1,0:T(8,128)(2,1)S(1)} %add_convert_fusion.1), channel_id=1, source_target_pairs={{0,4},{4,8},{8,12},{12,14},{14,10},{10,6},{6,2},{2,0},{1,5},{5,9},... | collective-permute-start | bytes 393224 | tf_op jit(solution)/shard_map/ppermute | solution.py:89

commit v4 on v3

--- a/solution.py
+++ b/solution.py
@@ -16,7 +16,7 @@
 RING = (0, 2, 4, 6, 7, 5, 3, 1)
 NR = 8
 CROSSING = ((1, 7, 2, 6), (3, 5), (4,))
-VMEM_LIMIT = 46 << 20
+VMEM_LIMIT = 43 << 20
 VMEM_SMALL = 10 << 20
 VMEM_FAR = 25 << 20
 FETCH_LIMITS = (34, 26, 18)
@@ -119,7 +119,7 @@
         if 1 < q < far:
             up, down, one[q], one[NR - q], *fetched = tie(up, down, one[q], one[NR - q], *fetched)
         elif q == far:
-            up, two[NR - q + 1], one[q], across[0], *fetched = tie(up, two[NR - q + 1], one[q], across[0], *fetched)
+            up, two[NR - q + 1], one[q], across[0], across[1], *fetched = tie(up, two[NR - q + 1], one[q], *across, *fetched)
         if q < far:
             two[q], two[NR - q] = from_prev(up), from_next(down)
             if fetches:

time: 104 us -> 100 us (0.962)
  local copies, waits for them, and re-layouts: 3.02 us -> 0.08 us
  waiting for transfers between devices: 21.8 us -> 20.3 us
    ppermute x14, starting transfers between devices: 17.4 us -> 7.04 us  [from_prev(): return lax.ppermute(value, 'wide', ring_pairs(1))]
    ppermute x14, starting transfers between devices: 14 us -> 24.3 us  [from_next(): return lax.ppermute(value, 'wide', ring_pairs(-1))]
    unnamed x6 -> x2, local copies, waits for them, and re-layouts: 2.94 us -> 0.01 us
    ppermute x14, waiting for transfers between devices: 9.39 us -> 11.8 us  [from_prev(): return lax.ppermute(value, 'wide', ring_pairs(1))]
    ppermute x14, waiting for transfers between devices: 6.66 us -> 4.69 us  [from_next(): return lax.ppermute(value, 'wide', ring_pairs(-1))]
    ppermute x5, waiting for transfers between devices: 5.76 us -> 3.84 us  [swap(): return lax.ppermute(value, axis, [(0, 1), (1, 0)])]
  transfers between devices with their start and end apart: 33 -> 33, of which waited for: 11 -> 12; matrix products, arithmetic and copies ran while one was open for 5% -> 6% of each run, Pallas kernels for 26% -> 27%
where the time goes in v4:
time: 100 us
  starting transfers between devices  36.5 us (36%)
  Pallas kernels  35.6 us (36%)
  waiting for transfers between devices  20.3 us (20%)
  other arithmetic  7.37 us (7%)
    ppermute x14, starting transfers between devices, from_next(): return lax.ppermute(value, 'wide', ring_pairs(-1))  24.3 us
    pallas_call x3, Pallas kernels, fetch(): pl.pallas_call(functools.partial(fetch_kernel, base), in_specs=[ANY], out...  13.6 us
    ppermute x14, waiting for transfers between devices, from_prev(): return lax.ppermute(value, 'wide', ring_pairs(1))  11.8 us
    ppermute x14, starting transfers between devices, from_prev(): return lax.ppermute(value, 'wide', ring_pairs(1))  7.04 us
    pallas_call x2, Pallas kernels, on_device_ring(): pl.pallas_call(functools.partial(second_far_kernel, 2 * near, c, width),...  6.33 us
    pallas_call x1, Pallas kernels, on_device_ring(): pl.pallas_call(functools.partial(first_kernel, 3 * count), in_specs=[VM,...  6.18 us
    pallas_call x1, Pallas kernels, on_device_ring(): pl.pallas_call(functools.partial(prologue_kernel, experts, slots, tile_ro...  5.25 us
    ppermute x5, starting transfers between devices, swap(): return lax.ppermute(value, axis, [(0, 1), (1, 0)])  5.17 us
  transfers between devices with their start and end apart: 33, of which 12 were waited for; matrix products, arithmetic and copies ran while one was open for 6% of the time, Pallas kernels for 27%

profile of v4, /device:TPU:0, one launch (start us, length us, event | category | flops | bytes accessed | tf_op | source)
XLA Modules:
  0.0 100.1 jit_solution(12059132623093605022)
XLA Ops:
  0.0 1.0 slice_select_fusion
  1.0 3.0 %collective-permute-start.1 = (bf16[64,1024]{1,0:T(8,128)(2,1)S(1)}, bf16[64,1024]{1,0:T(8,128)(2,1)S(1)}, u32[]{:S(2)}, u32[]{:S(2)}) collective-permute-start(bf16[64,1024]{1,0:T(8,128)(2,1)S(1)} %slice_select_fusion), channel_id=1, source_target_pairs={{0,2},{4,0},{8,4},{12,8},{14,12},{10,14},{6,10},{2,6},{1,3},{5,1},... | collective-permute-start | bytes 393224 | tf_op jit(solution)/shard_map/ppermute | solution.py:93
  4.1 0.7 bitcast_convert_fusion
  4.8 0.7 fusion.42
  5.5 0.9 compare_reduce_fusion
  6.4 0.7 convert_bitcast_fusion
  7.1 2.2 %fusion.33 = bf16[2,64,1024]{2,1,0:T(8,128)(2,1)S(1)} fusion(bf16[2,64,1024]{2,1,0:T(8,128)(2,1)} %bitcast.18, bf16[2,64,1024]{2,1,0:T(8,128)(2,1)} %param.9, pred[2]{0:T(512)(128)(4,1)S(1)} %compare_reduce_fusion), kind=kLoop, calls=%fused_computation.38 | loop fusion | flops 8781824 | bytes 786434 | tf_op jit(solution)/shard_map/jit(_where)/select_n | solution.py:388
  9.4 1.9 %collective-permute-start.3 = (bf16[144,1024]{1,0:T(8,128)(2,1)S(1)}, bf16[144,1024]{1,0:T(8,128)(2,1)S(1)}, u32[]{:S(2)}, u32[]{:S(2)}) collective-permute-start(bf16[144,1024]{1,0:T(8,128)(2,1)S(1)} %fusion.32.refs_0_), channel_id=1, source_target_pairs={{0,2},{4,0},{8,4},{12,8},{14,12},{10,14},{6,10},{2,6},{1,3},{5,1},... | collective-permute-start | bytes 884744 | tf_op jit(solution)/shard_map/ppermute | solution.py:93
  11.5 2.0 %collective-permute-start.4 = (bf16[64,1024]{1,0:T(8,128)(2,1)S(1)}, bf16[64,1024]{1,0:T(8,128)(2,1)S(1)}, u32[]{:S(2)}, u32[]{:S(2)}) collective-permute-start(bf16[64,1024]{1,0:T(8,128)(2,1)S(1)} %collective-permute-done.refs_9_), channel_id=1, source_target_pairs={{0,4},{4,8},{8,12},{12,14},{14,10},{10,6},{6,2},{2,0},{1,5},{5,9},... | collective-permute-start | bytes 393224 | tf_op jit(solution)/shard_map/ppermute | solution.py:89
  13.5 4.5 %shard_map.91.refs_19_ = bf16[4,1024,1024]{2,1,0:T(8,128)(2,1)S(1)} custom-call(bf16[16,1024,2,512]{3,2,1,0:T(2,128)(2,1)} %gate_up.7), custom_call_target="tpu_custom_call" | custom-call | flops 2147483648 | bytes 16777216 | tf_op jit(solution)/shard_map/pallas_call | solution.py:400
  18.1 4.0 %collective-permute-done.4.refs_10_ = bf16[64,1024]{1,0:T(8,128)(2,1)S(1)} collective-permute-done((bf16[64,1024]{1,0:T(8,128)(2,1)S(1)}, bf16[64,1024]{1,0:T(8,128)(2,1)S(1)}, u32[]{:S(2)}, u32[]{:S(2)}) %collective-permute-start.4) | collective-permute-done | bytes 131104 | tf_op jit(solution)/shard_map/ppermute | solution.py:89
  22.1 0.5 collective-permute-start.8
  22.5 1.6 %collective-permute-start.9 = (bf16[64,1024]{1,0:T(8,128)(2,1)S(1)}, bf16[64,1024]{1,0:T(8,128)(2,1)S(1)}, u32[]{:S(2)}, u32[]{:S(2)}) collective-permute-start(bf16[64,1024]{1,0:T(8,128)(2,1)S(1)} %collective-permute-done.5.refs_14_), channel_id=1, source_target_pairs={{0,2},{4,0},{8,4},{12,8},{14,12},{10,14},{6,10},{2,6},{1,3},{5,1},... | collective-permute-start | bytes 393224 | tf_op jit(solution)/shard_map/ppermute | solution.py:93
  24.1 0.4 collective-permute-start.6
  24.6 1.6 %collective-permute-start.7 = (bf16[144,1024]{1,0:T(8,128)(2,1)S(1)}, bf16[144,1024]{1,0:T(8,128)(2,1)S(1)}, u32[]{:S(2)}, u32[]{:S(2)}) collective-permute-start(bf16[144,1024]{1,0:T(8,128)(2,1)S(1)} %collective-permute-done.3.refs_7_), channel_id=1, source_target_pairs={{0,2},{4,0},{8,4},{12,8},{14,12},{10,14},{6,10},{2,6},{1,3},{5,1},... | collective-permute-start | bytes 884744 | tf_op jit(solution)/shard_map/ppermute | solution.py:93
  26.2 1.6 %collective-permute-start.13 = (bf16[256,1024]{1,0:T(8,128)(2,1)S(1)}, bf16[256,1024]{1,0:T(8,128)(2,1)S(1)}, u32[]{:S(2)}, u32[]{:S(2)}) collective-permute-start(bf16[256,1024]{1,0:T(8,128)(2,1)S(1)} %pad_maximum_fusion), channel_id=1, source_target_pairs={{0,16},{16,0},{1,17},{17,1},{2,18},{18,2},{3,19},{19,3},{4,20},{20... | collective-permute-start | bytes 1572872 | tf_op jit(solution)/shard_map/ppermute | solution.py:97
  27.8 4.5 %shard_map.92.refs_20_ = bf16[4,1024,1024]{2,1,0:T(8,128)(2,1)S(1)} custom-call(bf16[16,1024,2,512]{3,2,1,0:T(2,128)(2,1)} %gate_up.7), custom_call_target="tpu_custom_call" | custom-call | flops 2147483648 | bytes 16777216 | tf_op jit(solution)/shard_map/pallas_call | solution.py:400
  32.4 1.5 %collective-permute-start.10 = (bf16[144,1024]{1,0:T(8,128)(2,1)S(1)}, bf16[144,1024]{1,0:T(8,128)(2,1)S(1)}, u32[]{:S(2)}, u32[]{:S(2)}) collective-permute-start(bf16[144,1024]{1,0:T(8,128)(2,1)S(1)} %collective-permute-done.6.refs_2_), channel_id=1, source_target_pairs={{0,4},{4,8},{8,12},{12,14},{14,10},{10,6},{6,2},{2,0},{1,5},{5,9},... | collective-permute-start | bytes 884744 | tf_op jit(solution)/shard_map/ppermute | solution.py:89
  33.9 0.6 collective-permute-start.11
  34.5 1.4 %collective-permute-start.14 = (bf16[128,1024]{1,0:T(8,128)(2,1)S(1)}, bf16[128,1024]{1,0:T(8,128)(2,1)S(1)}, u32[]{:S(2)}, u32[]{:S(2)}) collective-permute-start(bf16[128,1024]{1,0:T(8,128)(2,1)S(1)} %pad_maximum_fusion.1), channel_id=1, source_target_pairs={{0,16},{16,0},{1,17},{17,1},{2,18},{18,2},{3,19},{19,3},{4,20},{20... | collective-permute-start | bytes 786440 | tf_op jit(solution)/shard_map/ppermute | solution.py:97
  35.9 1.5 %collective-permute-start.12 = (bf16[64,1024]{1,0:T(8,128)(2,1)S(1)}, bf16[64,1024]{1,0:T(8,128)(2,1)S(1)}, u32[]{:S(2)}, u32[]{:S(2)}) collective-permute-start(bf16[64,1024]{1,0:T(8,128)(2,1)S(1)} %collective-permute-done.9.refs_13_), channel_id=1, source_target_pairs={{0,2},{4,0},{8,4},{12,8},{14,12},{10,14},{6,10},{2,6},{1,3},{5,1},... | collective-permute-start | bytes 393224 | tf_op jit(solution)/shard_map/ppermute | solution.py:93
  37.4 4.5 %shard_map.93.held = bf16[4,1024,1024]{2,1,0:T(8,128)(2,1)S(1)} custom-call(bf16[16,1024,2,512]{3,2,1,0:T(2,128)(2,1)} %gate_up.7), custom_call_target="tpu_custom_call" | custom-call | flops 2147483648 | bytes 16777216 | tf_op jit(solution)/shard_map/pallas_call | solution.py:400
  42.3 0.4 collective-permute-done.14.refs_17_
  42.7 1.3 %collective-permute-start.15 = (bf16[144,1024]{1,0:T(8,128)(2,1)S(1)}, bf16[144,1024]{1,0:T(8,128)(2,1)S(1)}, u32[]{:S(2)}, u32[]{:S(2)}) collective-permute-start(bf16[144,1024]{1,0:T(8,128)(2,1)S(1)} %collective-permute-done.10.refs_3_), channel_id=1, source_target_pairs={{0,4},{4,8},{8,12},{12,14},{14,10},{10,6},{6,2},{2,0},{1,5},{5,9},... | collective-permute-start | bytes 884744 | tf_op jit(solution)/shard_map/ppermute | solution.py:89
  43.9 1.5 %collective-permute-start.16 = (bf16[64,1024]{1,0:T(8,128)(2,1)S(1)}, bf16[64,1024]{1,0:T(8,128)(2,1)S(1)}, u32[]{:S(2)}, u32[]{:S(2)}) collective-permute-start(bf16[64,1024]{1,0:T(8,128)(2,1)S(1)} %collective-permute-done.12.refs_12_), channel_id=1, source_target_pairs={{0,16},{16,0},{1,17},{17,1},{2,18},{18,2},{3,19},{19,3},{4,20},{20... | collective-permute-start | bytes 393224 | tf_op jit(solution)/shard_map/ppermute | solution.py:97
  45.5 3.4 %collective-permute-done.16.refs_18_ = bf16[64,1024]{1,0:T(8,128)(2,1)S(1)} collective-permute-done((bf16[64,1024]{1,0:T(8,128)(2,1)S(1)}, bf16[64,1024]{1,0:T(8,128)(2,1)S(1)}, u32[]{:S(2)}, u32[]{:S(2)}) %collective-permute-start.16) | collective-permute-done | bytes 131104 | tf_op jit(solution)/shard_map/ppermute | solution.py:97
  48.9 0.5 collective-permute-done.15.refs_4_
  49.4 5.2 %shard_map.94 = (bf16[4,128,1024]{2,1,0:T(8,128)(2,1)S(1)}, bf16[8,2,128,128]{3,2,1,0:T(8,128)(2,1)S(1)}, bf16[8,128,1024]{2,1,0:T(8,128)(2,1)S(1)}) custom-call(bf16[144,1024]{1,0:T(8,128)(2,1)S(1)} %fusion.32.refs_0_, bf16[144,1024]{1,0:T(8,128)(2,1)S(1)} %collective-permute-done.2.refs_1_, bf16[144,1024]{1,0:T(8,128)(2,1)S(1)} %collective-permute-done.6.refs_2_, ...), custom_call_target="tpu_custom_call" | custom-call | tf_op jit(solution)/shard_map/pallas_call | solution.py:426
  54.7 6.2 %shard_map.95.refs_0_ = bf16[8,128,1024]{2,1,0:T(8,128)(2,1)S(1)} custom-call(bf16[4,128,1024]{2,1,0:T(8,128)(2,1)S(1)} %get-tuple-element.86.rows, bf16[4,1024,1024]{2,1,0:T(8,128)(2,1)S(1)} %shard_map.93.held, bf16[16,1024,2,512]{3,2,1,0:T(2,128)(2,1)} %gate_up.7), custom_call_target="tpu_custom_call" | custom-call | flops 4294967296 | bytes 16777216 | tf_op jit(solution)/shard_map/pallas_call | solution.py:446
  60.9 0.6 collective-permute-start.18
  61.5 4.2 %shard_map.96.refs_2_.refs_1_ = bf16[4,128,1024]{2,1,0:T(8,128)(2,1)S(1)} custom-call(bf16[8,128,1024]{2,1,0:T(8,128)(2,1)S(1)} %get-tuple-element.88.own, bf16[8,128,1024]{2,1,0:T(8,128)(2,1)S(1)} %collective-permute-done.17.other, bf16[16,512,1024]{2,1,0:T(8,128)(2,1)} %refs_3_.1), custom_call_target="tpu_custom_call" | custom-call | flops 1073741824 | bytes 8388608 | tf_op jit(solution)/shard_map/pallas_call | solution.py:464
  65.8 3.2 %shard_map.97 = (bf16[8,128,512]{2,1,0:T(8,128)(2,1)S(1)}, bf16[128,512]{1,0:T(8,128)(2,1)S(1)}, bf16[128,512]{1,0:T(8,128)(2,1)S(1)}, bf16[128,512]{1,0:T(8,128...) custom-call(bf16[8,128,1024]{2,1,0:T(8,128)(2,1)S(1)} %shard_map.95., ...), custom_call_target="tpu_custom_call" | custom-call | flops 536870912 | bytes 4194304 | tf_op jit(solution)/shard_map/pallas_call | solution.py:485
  68.9 1.9 %collective-permute-start.19 = (bf16[128,512]{1,0:T(8,128)(2,1)S(1)}, bf16[128,512]{1,0:T(8,128)(2,1)S(1)}, u32[]{:S(2)}, u32[]{:S(2)}) collective-permute-start(bf16[128,512]{1,0:T(8,128)(2,1)S(1)} %get-tuple-element.95), channel_id=1, source_target_pairs={{0,2},{4,0},{8,4},{12,8},{14,12},{10,14},{6,10},{2,6},{1,3},{5,1},... | collective-permute-start | bytes 393224 | tf_op jit(solution)/shard_map/ppermute | solution.py:93
  71.0 3.2 %shard_map.98 = (bf16[128,512]{1,0:T(8,128)(2,1)S(1)}, bf16[128,512]{1,0:T(8,128)(2,1)S(1)}, bf16[128,512]{1,0:T(8,128)(2,1)S(1)}, bf16[128,512]{1,0:T(8,128)(2,...) custom-call(bf16[8,128,512]{2,1,0:T(8,128)(2,1)S(1)} %get-tuple-elem, ...), custom_call_target="tpu_custom_call" | custom-call | flops 536870912 | bytes 4194304 | tf_op jit(solution)/shard_map/pallas_call | solution.py:485
  74.2 1.9 %collective-permute-start.26 = (bf16[128,512]{1,0:T(8,128)(2,1)S(1)}, bf16[128,512]{1,0:T(8,128)(2,1)S(1)}, u32[]{:S(2)}, u32[]{:S(2)}) collective-permute-start(bf16[128,512]{1,0:T(8,128)(2,1)S(1)} %get-tuple-element.104), channel_id=1, source_target_pairs={{0,2},{4,0},{8,4},{12,8},{14,12},{10,14},{6,10},{2,6},{1,3},{5,1},... | collective-permute-start | bytes 393224 | tf_op jit(solution)/shard_map/ppermute | solution.py:93
  76.3 1.9 %collective-permute-start.20 = (bf16[128,512]{1,0:T(8,128)(2,1)S(1)}, bf16[128,512]{1,0:T(8,128)(2,1)S(1)}, u32[]{:S(2)}, u32[]{:S(2)}) collective-permute-start(bf16[128,512]{1,0:T(8,128)(2,1)S(1)} %add_convert_fusion.11), channel_id=1, source_target_pairs={{0,2},{4,0},{8,4},{12,8},{14,12},{10,14},{6,10},{2,6},{1,3},{5,1},... | collective-permute-start | bytes 393224 | tf_op jit(solution)/shard_map/ppermute | solution.py:93
  78.5 1.8 %collective-permute-done.26 = bf16[128,512]{1,0:T(8,128)(2,1)S(1)} collective-permute-done((bf16[128,512]{1,0:T(8,128)(2,1)S(1)}, bf16[128,512]{1,0:T(8,128)(2,1)S(1)}, u32[]{:S(2)}, u32[]{:S(2)}) %collective-permute-start.26) | collective-permute-done | bytes 131104 | tf_op jit(solution)/shard_map/ppermute | solution.py:93
  80.3 2.2 %collective-permute-start.27 = (bf16[128,512]{1,0:T(8,128)(2,1)S(1)}, bf16[128,512]{1,0:T(8,128)(2,1)S(1)}, u32[]{:S(2)}, u32[]{:S(2)}) collective-permute-start(bf16[128,512]{1,0:T(8,128)(2,1)S(1)} %add_convert_fusion.5), channel_id=1, source_target_pairs={{0,2},{4,0},{8,4},{12,8},{14,12},{10,14},{6,10},{2,6},{1,3},{5,1},... | collective-permute-start | bytes 393224 | tf_op jit(solution)/shard_map/ppermute | solution.py:93
  82.6 0.4 collective-permute-done.20
  83.1 2.2 %collective-permute-start.21 = (bf16[128,512]{1,0:T(8,128)(2,1)S(1)}, bf16[128,512]{1,0:T(8,128)(2,1)S(1)}, u32[]{:S(2)}, u32[]{:S(2)}) collective-permute-start(bf16[128,512]{1,0:T(8,128)(2,1)S(1)} %add_convert_fusion.10), channel_id=1, source_target_pairs={{0,2},{4,0},{8,4},{12,8},{14,12},{10,14},{6,10},{2,6},{1,3},{5,1},... | collective-permute-start | bytes 393224 | tf_op jit(solution)/shard_map/ppermute | solution.py:93
  85.4 1.3 %collective-permute-done.27 = bf16[128,512]{1,0:T(8,128)(2,1)S(1)} collective-permute-done((bf16[128,512]{1,0:T(8,128)(2,1)S(1)}, bf16[128,512]{1,0:T(8,128)(2,1)S(1)}, u32[]{:S(2)}, u32[]{:S(2)}) %collective-permute-start.27) | collective-permute-done | bytes 131104 | tf_op jit(solution)/shard_map/ppermute | solution.py:93
  86.8 1.8 %collective-permute-start.28 = (bf16[128,512]{1,0:T(8,128)(2,1)S(1)}, bf16[128,512]{1,0:T(8,128)(2,1)S(1)}, u32[]{:S(2)}, u32[]{:S(2)}) collective-permute-start(bf16[128,512]{1,0:T(8,128)(2,1)S(1)} %add_convert_fusion.4), channel_id=1, source_target_pairs={{0,2},{4,0},{8,4},{12,8},{14,12},{10,14},{6,10},{2,6},{1,3},{5,1},... | collective-permute-start | bytes 393224 | tf_op jit(solution)/shard_map/ppermute | solution.py:93
  88.6 0.4 collective-permute-start.31
  88.9 0.5 collective-permute-done.21
  89.5 2.1 %collective-permute-start.22 = (bf16[128,512]{1,0:T(8,128)(2,1)S(1)}, bf16[128,512]{1,0:T(8,128)(2,1)S(1)}, u32[]{:S(2)}, u32[]{:S(2)}) collective-permute-start(bf16[128,512]{1,0:T(8,128)(2,1)S(1)} %add_convert_fusion.9), channel_id=1, source_target_pairs={{0,2},{4,0},{8,4},{12,8},{14,12},{10,14},{6,10},{2,6},{1,3},{5,1},... | collective-permute-start | bytes 393224 | tf_op jit(solution)/shard_map/ppermute | solution.py:93
  91.7 2.6 %collective-permute-done.31 = bf16[128,512]{1,0:T(8,128)(2,1)S(1)} collective-permute-done((bf16[128,512]{1,0:T(8,128)(2,1)S(1)}, bf16[128,512]{1,0:T(8,128)(2,1)S(1)}, u32[]{:S(2)}, u32[]{:S(2)}) %collective-permute-start.31) | collective-permute-done | bytes 131104 | tf_op jit(solution)/shard_map/ppermute | solution.py:89
  94.6 4.7 %collective-permute-done.32 = bf16[128,512]{1,0:T(8,128)(2,1)S(1)} collective-permute-done((bf16[128,512]{1,0:T(8,128)(2,1)S(1)}, bf16[128,512]{1,0:T(8,128)(2,1)S(1)}, u32[]{:S(2)}, u32[]{:S(2)}) %collective-permute-start.32) | collective-permute-done | bytes 131104 | tf_op jit(solution)/shard_map/ppermute | solution.py:89
  99.3 0.7 pad_maximum_fusion.2
  (54 shorter events, 2.5 us)
Async XLA Ops:
  1.0 8.4 %collective-permute-start.1 = (bf16[64,1024]{1,0:T(8,128)(2,1)S(1)}, bf16[64,1024]{1,0:T(8,128)(2,1)S(1)}, u32[]{:S(2)}, u32[]{:S(2)}) collective-permute-start(bf16[64,1024]{1,0:T(8,128)(2,1)S(1)} %slice_select_fusion), channel_id=1, source_target_pairs={{0,2},{4,0},{8,4},{12,8},{14,12},{10,14},{6,10},{2,6},{1,3},{5,1},... | collective-permute-start | bytes 393224 | tf_op jit(solution)/shard_map/ppermute | solution.py:93
  4.0 5.4 %collective-permute-start = (bf16[64,1024]{1,0:T(8,128)(2,1)S(1)}, bf16[64,1024]{1,0:T(8,128)(2,1)S(1)}, u32[]{:S(2)}, u32[]{:S(2)}) collective-permute-start(bf16[64,1024]{1,0:T(8,128)(2,1)S(1)} %slice_select_fusion), channel_id=1, source_target_pairs={{0,4},{4,8},{8,12},{12,14},{14,10},{10,6},{6,2},{2,0},{1,5},{5,9},... | collective-permute-start | bytes 393224 | tf_op jit(solution)/shard_map/ppermute | solution.py:89
  9.4 12.7 %collective-permute-start.3 = (bf16[144,1024]{1,0:T(8,128)(2,1)S(1)}, bf16[144,1024]{1,0:T(8,128)(2,1)S(1)}, u32[]{:S(2)}, u32[]{:S(2)}) collective-permute-start(bf16[144,1024]{1,0:T(8,128)(2,1)S(1)} %fusion.32.refs_0_), channel_id=1, source_target_pairs={{0,2},{4,0},{8,4},{12,8},{14,12},{10,14},{6,10},{2,6},{1,3},{5,1},... | collective-permute-start | bytes 884744 | tf_op jit(solution)/shard_map/ppermute | solution.py:93
  11.3 10.7 %collective-permute-start.2 = (bf16[144,1024]{1,0:T(8,128)(2,1)S(1)}, bf16[144,1024]{1,0:T(8,128)(2,1)S(1)}, u32[]{:S(2)}, u32[]{:S(2)}) collective-permute-start(bf16[144,1024]{1,0:T(8,128)(2,1)S(1)} %fusion.32.refs_0_), channel_id=1, source_target_pairs={{0,4},{4,8},{8,12},{12,14},{14,10},{10,6},{6,2},{2,0},{1,5},{5,9},... | collective-permute-start | bytes 884744 | tf_op jit(solution)/shard_map/ppermute | solution.py:89
  11.5 10.6 %collective-permute-start.4 = (bf16[64,1024]{1,0:T(8,128)(2,1)S(1)}, bf16[64,1024]{1,0:T(8,128)(2,1)S(1)}, u32[]{:S(2)}, u32[]{:S(2)}) collective-permute-start(bf16[64,1024]{1,0:T(8,128)(2,1)S(1)} %collective-permute-done.refs_9_), channel_id=1, source_target_pairs={{0,4},{4,8},{8,12},{12,14},{14,10},{10,6},{6,2},{2,0},{1,5},{5,9},... | collective-permute-start | bytes 393224 | tf_op jit(solution)/shard_map/ppermute | solution.py:89
  13.4 8.6 %collective-permute-start.5 = (bf16[64,1024]{1,0:T(8,128)(2,1)S(1)}, bf16[64,1024]{1,0:T(8,128)(2,1)S(1)}, u32[]{:S(2)}, u32[]{:S(2)}) collective-permute-start(bf16[64,1024]{1,0:T(8,128)(2,1)S(1)} %collective-permute-done.1.refs_15_), channel_id=1, source_target_pairs={{0,2},{4,0},{8,4},{12,8},{14,12},{10,14},{6,10},{2,6},{1,3},{5,1},... | collective-permute-start | bytes 393224 | tf_op jit(solution)/shard_map/ppermute | solution.py:93
  22.1 10.3 %collective-permute-start.8 = (bf16[64,1024]{1,0:T(8,128)(2,1)S(1)}, bf16[64,1024]{1,0:T(8,128)(2,1)S(1)}, u32[]{:S(2)}, u32[]{:S(2)}) collective-permute-start(bf16[64,1024]{1,0:T(8,128)(2,1)S(1)} %collective-permute-done.4.refs_10_), channel_id=1, source_target_pairs={{0,4},{4,8},{8,12},{12,14},{14,10},{10,6},{6,2},{2,0},{1,5},{5,9},... | collective-permute-start | bytes 393224 | tf_op jit(solution)/shard_map/ppermute | solution.py:89
  22.5 9.8 %collective-permute-start.9 = (bf16[64,1024]{1,0:T(8,128)(2,1)S(1)}, bf16[64,1024]{1,0:T(8,128)(2,1)S(1)}, u32[]{:S(2)}, u32[]{:S(2)}) collective-permute-start(bf16[64,1024]{1,0:T(8,128)(2,1)S(1)} %collective-permute-done.5.refs_14_), channel_id=1, source_target_pairs={{0,2},{4,0},{8,4},{12,8},{14,12},{10,14},{6,10},{2,6},{1,3},{5,1},... | collective-permute-start | bytes 393224 | tf_op jit(solution)/shard_map/ppermute | solution.py:93
  24.1 8.2 %collective-permute-start.6 = (bf16[144,1024]{1,0:T(8,128)(2,1)S(1)}, bf16[144,1024]{1,0:T(8,128)(2,1)S(1)}, u32[]{:S(2)}, u32[]{:S(2)}) collective-permute-start(bf16[144,1024]{1,0:T(8,128)(2,1)S(1)} %collective-permute-done.2.refs_1_), channel_id=1, source_target_pairs={{0,4},{4,8},{8,12},{12,14},{14,10},{10,6},{6,2},{2,0},{1,5},{5,9},... | collective-permute-start | bytes 884744 | tf_op jit(solution)/shard_map/ppermute | solution.py:89
  24.6 7.8 %collective-permute-start.7 = (bf16[144,1024]{1,0:T(8,128)(2,1)S(1)}, bf16[144,1024]{1,0:T(8,128)(2,1)S(1)}, u32[]{:S(2)}, u32[]{:S(2)}) collective-permute-start(bf16[144,1024]{1,0:T(8,128)(2,1)S(1)} %collective-permute-done.3.refs_7_), channel_id=1, source_target_pairs={{0,2},{4,0},{8,4},{12,8},{14,12},{10,14},{6,10},{2,6},{1,3},{5,1},... | collective-permute-start | bytes 884744 | tf_op jit(solution)/shard_map/ppermute | solution.py:93
  26.2 16.1 %collective-permute-start.13 = (bf16[256,1024]{1,0:T(8,128)(2,1)S(1)}, bf16[256,1024]{1,0:T(8,128)(2,1)S(1)}, u32[]{:S(2)}, u32[]{:S(2)}) collective-permute-start(bf16[256,1024]{1,0:T(8,128)(2,1)S(1)} %pad_maximum_fusion), channel_id=1, source_target_pairs={{0,16},{16,0},{1,17},{17,1},{2,18},{18,2},{3,19},{19,3},{4,20},{20... | collective-permute-start | bytes 1572872 | tf_op jit(solution)/shard_map/ppermute | solution.py:97
  32.4 10.3 %collective-permute-start.10 = (bf16[144,1024]{1,0:T(8,128)(2,1)S(1)}, bf16[144,1024]{1,0:T(8,128)(2,1)S(1)}, u32[]{:S(2)}, u32[]{:S(2)}) collective-permute-start(bf16[144,1024]{1,0:T(8,128)(2,1)S(1)} %collective-permute-done.6.refs_2_), channel_id=1, source_target_pairs={{0,4},{4,8},{8,12},{12,14},{14,10},{10,6},{6,2},{2,0},{1,5},{5,9},... | collective-permute-start | bytes 884744 | tf_op jit(solution)/shard_map/ppermute | solution.py:89
  33.9 8.8 %collective-permute-start.11 = (bf16[144,1024]{1,0:T(8,128)(2,1)S(1)}, bf16[144,1024]{1,0:T(8,128)(2,1)S(1)}, u32[]{:S(2)}, u32[]{:S(2)}) collective-permute-start(bf16[144,1024]{1,0:T(8,128)(2,1)S(1)} %collective-permute-done.7.refs_6_), channel_id=1, source_target_pairs={{0,2},{4,0},{8,4},{12,8},{14,12},{10,14},{6,10},{2,6},{1,3},{5,1},... | collective-permute-start | bytes 884744 | tf_op jit(solution)/shard_map/ppermute | solution.py:93
  34.5 14.9 %copy-start = (bf16[128,1024]{1,0:T(8,128)(2,1)S(1)}, bf16[128,1024]{1,0:T(8,128)(2,1)}, u32[]{:S(2)}) copy-start(bf16[128,1024]{1,0:T(8,128)(2,1)} %refs_8_.1) | copy-start | bytes 786436
  34.5 8.2 %collective-permute-start.14 = (bf16[128,1024]{1,0:T(8,128)(2,1)S(1)}, bf16[128,1024]{1,0:T(8,128)(2,1)S(1)}, u32[]{:S(2)}, u32[]{:S(2)}) collective-permute-start(bf16[128,1024]{1,0:T(8,128)(2,1)S(1)} %pad_maximum_fusion.1), channel_id=1, source_target_pairs={{0,16},{16,0},{1,17},{17,1},{2,18},{18,2},{3,19},{19,3},{4,20},{20... | collective-permute-start | bytes 786440 | tf_op jit(solution)/shard_map/ppermute | solution.py:97
  35.9 6.4 %collective-permute-start.12 = (bf16[64,1024]{1,0:T(8,128)(2,1)S(1)}, bf16[64,1024]{1,0:T(8,128)(2,1)S(1)}, u32[]{:S(2)}, u32[]{:S(2)}) collective-permute-start(bf16[64,1024]{1,0:T(8,128)(2,1)S(1)} %collective-permute-done.9.refs_13_), channel_id=1, source_target_pairs={{0,2},{4,0},{8,4},{12,8},{14,12},{10,14},{6,10},{2,6},{1,3},{5,1},... | collective-permute-start | bytes 393224 | tf_op jit(solution)/shard_map/ppermute | solution.py:93
  42.7 6.7 %collective-permute-start.15 = (bf16[144,1024]{1,0:T(8,128)(2,1)S(1)}, bf16[144,1024]{1,0:T(8,128)(2,1)S(1)}, u32[]{:S(2)}, u32[]{:S(2)}) collective-permute-start(bf16[144,1024]{1,0:T(8,128)(2,1)S(1)} %collective-permute-done.10.refs_3_), channel_id=1, source_target_pairs={{0,4},{4,8},{8,12},{12,14},{14,10},{10,6},{6,2},{2,0},{1,5},{5,9},... | collective-permute-start | bytes 884744 | tf_op jit(solution)/shard_map/ppermute | solution.py:89
  43.9 5.0 %collective-permute-start.16 = (bf16[64,1024]{1,0:T(8,128)(2,1)S(1)}, bf16[64,1024]{1,0:T(8,128)(2,1)S(1)}, u32[]{:S(2)}, u32[]{:S(2)}) collective-permute-start(bf16[64,1024]{1,0:T(8,128)(2,1)S(1)} %collective-permute-done.12.refs_12_), channel_id=1, source_target_pairs={{0,16},{16,0},{1,17},{17,1},{2,18},{18,2},{3,19},{19,3},{4,20},{20... | collective-permute-start | bytes 393224 | tf_op jit(solution)/shard_map/ppermute | solution.py:97
  54.7 6.3 %collective-permute-start.17 = (bf16[8,128,1024]{2,1,0:T(8,128)(2,1)S(1)}, bf16[8,128,1024]{2,1,0:T(8,128)(2,1)S(1)}, u32[]{:S(2)}, u32[]{:S(2)}) collective-permute-start(bf16[8,128,1024]{2,1,0:T(8,128)(2,1)S(1)} %get-tuple-element.88.own), channel_id=1, source_target_pairs={{0,1},{1,0},{2,3},{3,2},{4,5},{5,4},{6,7},{7,6},{8,9},{9,8},{10,11... | collective-permute-start | bytes 6291464 | tf_op jit(solution)/shard_map/ppermute | solution.py:97
  60.9 4.8 %collective-permute-start.18 = (bf16[8,128,1024]{2,1,0:T(8,128)(2,1)S(1)}, bf16[8,128,1024]{2,1,0:T(8,128)(2,1)S(1)}, u32[]{:S(2)}, u32[]{:S(2)}) collective-permute-start(bf16[8,128,1024]{2,1,0:T(8,128)(2,1)S(1)} %shard_map.95.refs_0_), channel_id=1, source_target_pairs={{0,1},{1,0},{2,3},{3,2},{4,5},{5,4},{6,7},{7,6},{8,9},{9,8},{10,11... | collective-permute-start | bytes 6291464 | tf_op jit(solution)/shard_map/ppermute | solution.py:97
  68.9 7.3 %collective-permute-start.19 = (bf16[128,512]{1,0:T(8,128)(2,1)S(1)}, bf16[128,512]{1,0:T(8,128)(2,1)S(1)}, u32[]{:S(2)}, u32[]{:S(2)}) collective-permute-start(bf16[128,512]{1,0:T(8,128)(2,1)S(1)} %get-tuple-element.95), channel_id=1, source_target_pairs={{0,2},{4,0},{8,4},{12,8},{14,12},{10,14},{6,10},{2,6},{1,3},{5,1},... | collective-permute-start | bytes 393224 | tf_op jit(solution)/shard_map/ppermute | solution.py:93
  70.8 7.4 %collective-permute-start.23 = (bf16[128,512]{1,0:T(8,128)(2,1)S(1)}, bf16[128,512]{1,0:T(8,128)(2,1)S(1)}, u32[]{:S(2)}, u32[]{:S(2)}) collective-permute-start(bf16[128,512]{1,0:T(8,128)(2,1)S(1)} %get-tuple-element.99), channel_id=1, source_target_pairs={{0,4},{4,8},{8,12},{12,14},{14,10},{10,6},{6,2},{2,0},{1,5},{5,9},... | collective-permute-start | bytes 393224 | tf_op jit(solution)/shard_map/ppermute | solution.py:89
  74.2 6.1 %collective-permute-start.26 = (bf16[128,512]{1,0:T(8,128)(2,1)S(1)}, bf16[128,512]{1,0:T(8,128)(2,1)S(1)}, u32[]{:S(2)}, u32[]{:S(2)}) collective-permute-start(bf16[128,512]{1,0:T(8,128)(2,1)S(1)} %get-tuple-element.104), channel_id=1, source_target_pairs={{0,2},{4,0},{8,4},{12,8},{14,12},{10,14},{6,10},{2,6},{1,3},{5,1},... | collective-permute-start | bytes 393224 | tf_op jit(solution)/shard_map/ppermute | solution.py:93
  76.1 6.5 %collective-permute-start.29 = (bf16[128,512]{1,0:T(8,128)(2,1)S(1)}, bf16[128,512]{1,0:T(8,128)(2,1)S(1)}, u32[]{:S(2)}, u32[]{:S(2)}) collective-permute-start(bf16[128,512]{1,0:T(8,128)(2,1)S(1)} %get-tuple-element.107), channel_id=1, source_target_pairs={{0,4},{4,8},{8,12},{12,14},{14,10},{10,6},{6,2},{2,0},{1,5},{5,9},... | collective-permute-start | bytes 393224 | tf_op jit(solution)/shard_map/ppermute | solution.py:89
  76.3 6.8 %collective-permute-start.20 = (bf16[128,512]{1,0:T(8,128)(2,1)S(1)}, bf16[128,512]{1,0:T(8,128)(2,1)S(1)}, u32[]{:S(2)}, u32[]{:S(2)}) collective-permute-start(bf16[128,512]{1,0:T(8,128)(2,1)S(1)} %add_convert_fusion.11), channel_id=1, source_target_pairs={{0,2},{4,0},{8,4},{12,8},{14,12},{10,14},{6,10},{2,6},{1,3},{5,1},... | collective-permute-start | bytes 393224 | tf_op jit(solution)/shard_map/ppermute | solution.py:93
  78.2 7.1 %collective-permute-start.24 = (bf16[128,512]{1,0:T(8,128)(2,1)S(1)}, bf16[128,512]{1,0:T(8,128)(2,1)S(1)}, u32[]{:S(2)}, u32[]{:S(2)}) collective-permute-start(bf16[128,512]{1,0:T(8,128)(2,1)S(1)} %add_convert_fusion.8), channel_id=1, source_target_pairs={{0,4},{4,8},{8,12},{12,14},{14,10},{10,6},{6,2},{2,0},{1,5},{5,9},... | collective-permute-start | bytes 393224 | tf_op jit(solution)/shard_map/ppermute | solution.py:89
  80.3 6.4 %collective-permute-start.27 = (bf16[128,512]{1,0:T(8,128)(2,1)S(1)}, bf16[128,512]{1,0:T(8,128)(2,1)S(1)}, u32[]{:S(2)}, u32[]{:S(2)}) collective-permute-start(bf16[128,512]{1,0:T(8,128)(2,1)S(1)} %add_convert_fusion.5), channel_id=1, source_target_pairs={{0,2},{4,0},{8,4},{12,8},{14,12},{10,14},{6,10},{2,6},{1,3},{5,1},... | collective-permute-start | bytes 393224 | tf_op jit(solution)/shard_map/ppermute | solution.py:93
  82.6 6.0 %collective-permute-start.30 = (bf16[128,512]{1,0:T(8,128)(2,1)S(1)}, bf16[128,512]{1,0:T(8,128)(2,1)S(1)}, u32[]{:S(2)}, u32[]{:S(2)}) collective-permute-start(bf16[128,512]{1,0:T(8,128)(2,1)S(1)} %add_convert_fusion.3), channel_id=1, source_target_pairs={{0,4},{4,8},{8,12},{12,14},{14,10},{10,6},{6,2},{2,0},{1,5},{5,9},... | collective-permute-start | bytes 393224 | tf_op jit(solution)/shard_map/ppermute | solution.py:89
  83.1 6.4 %collective-permute-start.21 = (bf16[128,512]{1,0:T(8,128)(2,1)S(1)}, bf16[128,512]{1,0:T(8,128)(2,1)S(1)}, u32[]{:S(2)}, u32[]{:S(2)}) collective-permute-start(bf16[128,512]{1,0:T(8,128)(2,1)S(1)} %add_convert_fusion.10), channel_id=1, source_target_pairs={{0,2},{4,0},{8,4},{12,8},{14,12},{10,14},{6,10},{2,6},{1,3},{5,1},... | collective-permute-start | bytes 393224 | tf_op jit(solution)/shard_map/ppermute | solution.py:93
  85.4 9.0 %collective-permute-start.25 = (bf16[128,512]{1,0:T(8,128)(2,1)S(1)}, bf16[128,512]{1,0:T(8,128)(2,1)S(1)}, u32[]{:S(2)}, u32[]{:S(2)}) collective-permute-start(bf16[128,512]{1,0:T(8,128)(2,1)S(1)} %add_convert_fusion.7), channel_id=1, source_target_pairs={{0,4},{4,8},{8,12},{12,14},{14,10},{10,6},{6,2},{2,0},{1,5},{5,9},... | collective-permute-start | bytes 393224 | tf_op jit(solution)/shard_map/ppermute | solution.py:89
  86.8 7.8 %collective-permute-start.28 = (bf16[128,512]{1,0:T(8,128)(2,1)S(1)}, bf16[128,512]{1,0:T(8,128)(2,1)S(1)}, u32[]{:S(2)}, u32[]{:S(2)}) collective-permute-start(bf16[128,512]{1,0:T(8,128)(2,1)S(1)} %add_convert_fusion.4), channel_id=1, source_target_pairs={{0,2},{4,0},{8,4},{12,8},{14,12},{10,14},{6,10},{2,6},{1,3},{5,1},... | collective-permute-start | bytes 393224 | tf_op jit(solution)/shard_map/ppermute | solution.py:93
  88.6 5.6 %collective-permute-start.31 = (bf16[128,512]{1,0:T(8,128)(2,1)S(1)}, bf16[128,512]{1,0:T(8,128)(2,1)S(1)}, u32[]{:S(2)}, u32[]{:S(2)}) collective-permute-start(bf16[128,512]{1,0:T(8,128)(2,1)S(1)} %add_convert_fusion.2), channel_id=1, source_target_pairs={{0,4},{4,8},{8,12},{12,14},{14,10},{10,6},{6,2},{2,0},{1,5},{5,9},... | collective-permute-start | bytes 393224 | tf_op jit(solution)/shard_map/ppermute | solution.py:89
  89.5 5.0 %collective-permute-start.22 = (bf16[128,512]{1,0:T(8,128)(2,1)S(1)}, bf16[128,512]{1,0:T(8,128)(2,1)S(1)}, u32[]{:S(2)}, u32[]{:S(2)}) collective-permute-start(bf16[128,512]{1,0:T(8,128)(2,1)S(1)} %add_convert_fusion.9), channel_id=1, source_target_pairs={{0,2},{4,0},{8,4},{12,8},{14,12},{10,14},{6,10},{2,6},{1,3},{5,1},... | collective-permute-start | bytes 393224 | tf_op jit(solution)/shard_map/ppermute | solution.py:93
  94.3 5.0 %collective-permute-start.32 = (bf16[128,512]{1,0:T(8,128)(2,1)S(1)}, bf16[128,512]{1,0:T(8,128)(2,1)S(1)}, u32[]{:S(2)}, u32[]{:S(2)}) collective-permute-start(bf16[128,512]{1,0:T(8,128)(2,1)S(1)} %add_convert_fusion.1), channel_id=1, source_target_pairs={{0,4},{4,8},{8,12},{12,14},{14,10},{10,6},{6,2},{2,0},{1,5},{5,9},... | collective-permute-start | bytes 393224 | tf_op jit(solution)/shard_map/ppermute | solution.py:89

commit v5 on v4

--- a/solution.py
+++ b/solution.py
@@ -114,7 +114,7 @@
         else:
             one[q] = from_next(down)
         if q == 1:
-            two[0], one[1], one[NR - 1] = tie(make_second(), one[1], one[NR - 1])
+            two[0] = make_second()
         up, down = two[q - 1], two[(NR - q + 1) % NR]
         if 1 < q < far:
             up, down, one[q], one[NR - q], *fetched = tie(up, down, one[q], one[NR - q], *fetched)

time: 100 us -> 100 us (level)
    ppermute x14, waiting for transfers between devices: 4.69 us -> 7.66 us  [from_next(): return lax.ppermute(value, 'wide', ring_pairs(-1))]
    ppermute x14, waiting for transfers between devices: 11.8 us -> 8.87 us  [from_prev(): return lax.ppermute(value, 'wide', ring_pairs(1))]
    ppermute x14, starting transfers between devices: 7.04 us -> 5.55 us  [from_prev(): return lax.ppermute(value, 'wide', ring_pairs(1))]
    ppermute x14, starting transfers between devices: 24.3 us -> 25.7 us  [from_next(): return lax.ppermute(value, 'wide', ring_pairs(-1))]
  transfers between devices with their start and end apart: 33 -> 33, of which waited for: 12 -> 14; matrix products, arithmetic and copies ran while one was open for 6% -> 6% of each run, Pallas kernels for 27% -> 27%
where the time goes in v5:
time: 100 us
  starting transfers between devices  36.6 us (37%)
  Pallas kernels  35.6 us (36%)
  waiting for transfers between devices  20.1 us (20%)
  other arithmetic  7.37 us (7%)
    ppermute x14, starting transfers between devices, from_next(): return lax.ppermute(value, 'wide', ring_pairs(-1))  25.7 us
    pallas_call x3, Pallas kernels, fetch(): pl.pallas_call(functools.partial(fetch_kernel, base), in_specs=[ANY], out...  13.6 us
    ppermute x14, waiting for transfers between devices, from_prev(): return lax.ppermute(value, 'wide', ring_pairs(1))  8.87 us
    ppermute x14, waiting for transfers between devices, from_next(): return lax.ppermute(value, 'wide', ring_pairs(-1))  7.66 us
    pallas_call x2, Pallas kernels, on_device_ring(): pl.pallas_call(functools.partial(second_far_kernel, 2 * near, c, width),...  6.33 us
    pallas_call x1, Pallas kernels, on_device_ring(): pl.pallas_call(functools.partial(first_kernel, 3 * count), in_specs=[VM,...  6.18 us
    ppermute x14, starting transfers between devices, from_prev(): return lax.ppermute(value, 'wide', ring_pairs(1))  5.55 us
    ppermute x5, starting transfers between devices, swap(): return lax.ppermute(value, axis, [(0, 1), (1, 0)])  5.28 us
  transfers between devices with their start and end apart: 33, of which 14 were waited for; matrix products, arithmetic and copies ran while one was open for 6% of the time, Pallas kernels for 27%

profile of v5, /device:TPU:0, one launch (start us, length us, event | category | flops | bytes accessed | tf_op | source)
XLA Modules:
  0.0 100.0 jit_solution(16141556847737737182)
XLA Ops:
  0.0 1.0 slice_select_fusion
  1.0 3.0 %collective-permute-start.4 = (bf16[64,1024]{1,0:T(8,128)(2,1)S(1)}, bf16[64,1024]{1,0:T(8,128)(2,1)S(1)}, u32[]{:S(2)}, u32[]{:S(2)}) collective-permute-start(bf16[64,1024]{1,0:T(8,128)(2,1)S(1)} %slice_select_fusion), channel_id=1, source_target_pairs={{0,2},{4,0},{8,4},{12,8},{14,12},{10,14},{6,10},{2,6},{1,3},{5,1},... | collective-permute-start | bytes 393224 | tf_op jit(solution)/shard_map/ppermute | solution.py:93
  4.1 0.7 bitcast_convert_fusion
  4.8 0.7 fusion.42
  5.5 0.9 compare_reduce_fusion
  6.4 0.7 convert_bitcast_fusion
  7.1 2.2 %fusion.33 = bf16[2,64,1024]{2,1,0:T(8,128)(2,1)S(1)} fusion(bf16[2,64,1024]{2,1,0:T(8,128)(2,1)} %bitcast.18, bf16[2,64,1024]{2,1,0:T(8,128)(2,1)} %param.9, pred[2]{0:T(512)(128)(4,1)S(1)} %compare_reduce_fusion), kind=kLoop, calls=%fused_computation.38 | loop fusion | flops 8781824 | bytes 786434 | tf_op jit(solution)/shard_map/jit(_where)/select_n | solution.py:388
  9.4 1.9 %collective-permute-start.1 = (bf16[144,1024]{1,0:T(8,128)(2,1)S(1)}, bf16[144,1024]{1,0:T(8,128)(2,1)S(1)}, u32[]{:S(2)}, u32[]{:S(2)}) collective-permute-start(bf16[144,1024]{1,0:T(8,128)(2,1)S(1)} %fusion.32.refs_0_), channel_id=1, source_target_pairs={{0,2},{4,0},{8,4},{12,8},{14,12},{10,14},{6,10},{2,6},{1,3},{5,1},... | collective-permute-start | bytes 884744 | tf_op jit(solution)/shard_map/ppermute | solution.py:93
  11.5 1.9 %collective-permute-start.5 = (bf16[64,1024]{1,0:T(8,128)(2,1)S(1)}, bf16[64,1024]{1,0:T(8,128)(2,1)S(1)}, u32[]{:S(2)}, u32[]{:S(2)}) collective-permute-start(bf16[64,1024]{1,0:T(8,128)(2,1)S(1)} %collective-permute-done.4.refs_15_), channel_id=1, source_target_pairs={{0,2},{4,0},{8,4},{12,8},{14,12},{10,14},{6,10},{2,6},{1,3},{5,1},... | collective-permute-start | bytes 393224 | tf_op jit(solution)/shard_map/ppermute | solution.py:93
  13.5 4.5 %shard_map.91.refs_19_ = bf16[4,1024,1024]{2,1,0:T(8,128)(2,1)S(1)} custom-call(bf16[16,1024,2,512]{3,2,1,0:T(2,128)(2,1)} %gate_up.7), custom_call_target="tpu_custom_call" | custom-call | flops 2147483648 | bytes 16777216 | tf_op jit(solution)/shard_map/pallas_call | solution.py:400
  18.0 2.7 %collective-permute-done.5.refs_14_ = bf16[64,1024]{1,0:T(8,128)(2,1)S(1)} collective-permute-done((bf16[64,1024]{1,0:T(8,128)(2,1)S(1)}, bf16[64,1024]{1,0:T(8,128)(2,1)S(1)}, u32[]{:S(2)}, u32[]{:S(2)}) %collective-permute-start.5) | collective-permute-done | bytes 131104 | tf_op jit(solution)/shard_map/ppermute | solution.py:93
  20.7 1.3 %collective-permute-done.3.refs_10_ = bf16[64,1024]{1,0:T(8,128)(2,1)S(1)} collective-permute-done((bf16[64,1024]{1,0:T(8,128)(2,1)S(1)}, bf16[64,1024]{1,0:T(8,128)(2,1)S(1)}, u32[]{:S(2)}, u32[]{:S(2)}) %collective-permute-start.3) | collective-permute-done | bytes 131104 | tf_op jit(solution)/shard_map/ppermute | solution.py:89
  22.0 0.4 collective-permute-start.8
  22.5 1.6 %collective-permute-start.9 = (bf16[64,1024]{1,0:T(8,128)(2,1)S(1)}, bf16[64,1024]{1,0:T(8,128)(2,1)S(1)}, u32[]{:S(2)}, u32[]{:S(2)}) collective-permute-start(bf16[64,1024]{1,0:T(8,128)(2,1)S(1)} %collective-permute-done.5.refs_14_), channel_id=1, source_target_pairs={{0,2},{4,0},{8,4},{12,8},{14,12},{10,14},{6,10},{2,6},{1,3},{5,1},... | collective-permute-start | bytes 393224 | tf_op jit(solution)/shard_map/ppermute | solution.py:93
  24.1 0.4 collective-permute-start.6
  24.5 1.6 %collective-permute-start.7 = (bf16[144,1024]{1,0:T(8,128)(2,1)S(1)}, bf16[144,1024]{1,0:T(8,128)(2,1)S(1)}, u32[]{:S(2)}, u32[]{:S(2)}) collective-permute-start(bf16[144,1024]{1,0:T(8,128)(2,1)S(1)} %collective-permute-done.1.refs_7_), channel_id=1, source_target_pairs={{0,2},{4,0},{8,4},{12,8},{14,12},{10,14},{6,10},{2,6},{1,3},{5,1},... | collective-permute-start | bytes 884744 | tf_op jit(solution)/shard_map/ppermute | solution.py:93
  26.1 1.6 %collective-permute-start.13 = (bf16[256,1024]{1,0:T(8,128)(2,1)S(1)}, bf16[256,1024]{1,0:T(8,128)(2,1)S(1)}, u32[]{:S(2)}, u32[]{:S(2)}) collective-permute-start(bf16[256,1024]{1,0:T(8,128)(2,1)S(1)} %pad_maximum_fusion), channel_id=1, source_target_pairs={{0,16},{16,0},{1,17},{17,1},{2,18},{18,2},{3,19},{19,3},{4,20},{20... | collective-permute-start | bytes 1572872 | tf_op jit(solution)/shard_map/ppermute | solution.py:97
  27.7 4.5 %shard_map.92.refs_20_ = bf16[4,1024,1024]{2,1,0:T(8,128)(2,1)S(1)} custom-call(bf16[16,1024,2,512]{3,2,1,0:T(2,128)(2,1)} %gate_up.7), custom_call_target="tpu_custom_call" | custom-call | flops 2147483648 | bytes 16777216 | tf_op jit(solution)/shard_map/pallas_call | solution.py:400
  32.3 1.6 %collective-permute-start.10 = (bf16[144,1024]{1,0:T(8,128)(2,1)S(1)}, bf16[144,1024]{1,0:T(8,128)(2,1)S(1)}, u32[]{:S(2)}, u32[]{:S(2)}) collective-permute-start(bf16[144,1024]{1,0:T(8,128)(2,1)S(1)} %collective-permute-done.6.refs_2_), channel_id=1, source_target_pairs={{0,4},{4,8},{8,12},{12,14},{14,10},{10,6},{6,2},{2,0},{1,5},{5,9},... | collective-permute-start | bytes 884744 | tf_op jit(solution)/shard_map/ppermute | solution.py:89
  33.9 0.5 collective-permute-start.11
  34.4 1.5 %collective-permute-start.14 = (bf16[128,1024]{1,0:T(8,128)(2,1)S(1)}, bf16[128,1024]{1,0:T(8,128)(2,1)S(1)}, u32[]{:S(2)}, u32[]{:S(2)}) collective-permute-start(bf16[128,1024]{1,0:T(8,128)(2,1)S(1)} %pad_maximum_fusion.1), channel_id=1, source_target_pairs={{0,16},{16,0},{1,17},{17,1},{2,18},{18,2},{3,19},{19,3},{4,20},{20... | collective-permute-start | bytes 786440 | tf_op jit(solution)/shard_map/ppermute | solution.py:97
  36.0 1.3 %collective-permute-start.12 = (bf16[64,1024]{1,0:T(8,128)(2,1)S(1)}, bf16[64,1024]{1,0:T(8,128)(2,1)S(1)}, u32[]{:S(2)}, u32[]{:S(2)}) collective-permute-start(bf16[64,1024]{1,0:T(8,128)(2,1)S(1)} %collective-permute-done.9.refs_13_), channel_id=1, source_target_pairs={{0,2},{4,0},{8,4},{12,8},{14,12},{10,14},{6,10},{2,6},{1,3},{5,1},... | collective-permute-start | bytes 393224 | tf_op jit(solution)/shard_map/ppermute | solution.py:93
  37.3 4.5 %shard_map.93.held = bf16[4,1024,1024]{2,1,0:T(8,128)(2,1)S(1)} custom-call(bf16[16,1024,2,512]{3,2,1,0:T(2,128)(2,1)} %gate_up.7), custom_call_target="tpu_custom_call" | custom-call | flops 2147483648 | bytes 16777216 | tf_op jit(solution)/shard_map/pallas_call | solution.py:400
  41.8 0.6 collective-permute-done.12.refs_12_
  42.6 1.5 %collective-permute-start.15 = (bf16[144,1024]{1,0:T(8,128)(2,1)S(1)}, bf16[144,1024]{1,0:T(8,128)(2,1)S(1)}, u32[]{:S(2)}, u32[]{:S(2)}) collective-permute-start(bf16[144,1024]{1,0:T(8,128)(2,1)S(1)} %collective-permute-done.10.refs_3_), channel_id=1, source_target_pairs={{0,4},{4,8},{8,12},{12,14},{14,10},{10,6},{6,2},{2,0},{1,5},{5,9},... | collective-permute-start | bytes 884744 | tf_op jit(solution)/shard_map/ppermute | solution.py:89
  44.1 1.5 %collective-permute-start.16 = (bf16[64,1024]{1,0:T(8,128)(2,1)S(1)}, bf16[64,1024]{1,0:T(8,128)(2,1)S(1)}, u32[]{:S(2)}, u32[]{:S(2)}) collective-permute-start(bf16[64,1024]{1,0:T(8,128)(2,1)S(1)} %collective-permute-done.12.refs_12_), channel_id=1, source_target_pairs={{0,16},{16,0},{1,17},{17,1},{2,18},{18,2},{3,19},{19,3},{4,20},{20... | collective-permute-start | bytes 393224 | tf_op jit(solution)/shard_map/ppermute | solution.py:97
  45.6 3.4 %collective-permute-done.16.refs_18_ = bf16[64,1024]{1,0:T(8,128)(2,1)S(1)} collective-permute-done((bf16[64,1024]{1,0:T(8,128)(2,1)S(1)}, bf16[64,1024]{1,0:T(8,128)(2,1)S(1)}, u32[]{:S(2)}, u32[]{:S(2)}) %collective-permute-start.16) | collective-permute-done | bytes 131104 | tf_op jit(solution)/shard_map/ppermute | solution.py:97
  49.3 5.2 %shard_map.94 = (bf16[4,128,1024]{2,1,0:T(8,128)(2,1)S(1)}, bf16[8,2,128,128]{3,2,1,0:T(8,128)(2,1)S(1)}, bf16[8,128,1024]{2,1,0:T(8,128)(2,1)S(1)}) custom-call(bf16[144,1024]{1,0:T(8,128)(2,1)S(1)} %fusion.32.refs_0_, bf16[144,1024]{1,0:T(8,128)(2,1)S(1)} %collective-permute-done.refs_1_, bf16[144,1024]{1,0:T(8,128)(2,1)S(1)} %collective-permute-done.6.refs_2_, ...), custom_call_target="tpu_custom_call" | custom-call | tf_op jit(solution)/shard_map/pallas_call | solution.py:426
  54.7 6.2 %shard_map.95.refs_0_ = bf16[8,128,1024]{2,1,0:T(8,128)(2,1)S(1)} custom-call(bf16[4,128,1024]{2,1,0:T(8,128)(2,1)S(1)} %get-tuple-element.80.rows, bf16[4,1024,1024]{2,1,0:T(8,128)(2,1)S(1)} %shard_map.93.held, bf16[16,1024,2,512]{3,2,1,0:T(2,128)(2,1)} %gate_up.7), custom_call_target="tpu_custom_call" | custom-call | flops 4294967296 | bytes 16777216 | tf_op jit(solution)/shard_map/pallas_call | solution.py:446
  60.9 0.6 collective-permute-start.18
  61.4 4.2 %shard_map.96.refs_2_.refs_1_ = bf16[4,128,1024]{2,1,0:T(8,128)(2,1)S(1)} custom-call(bf16[8,128,1024]{2,1,0:T(8,128)(2,1)S(1)} %get-tuple-element.82.own, bf16[8,128,1024]{2,1,0:T(8,128)(2,1)S(1)} %collective-permute-done.17.other, bf16[16,512,1024]{2,1,0:T(8,128)(2,1)} %refs_3_.1), custom_call_target="tpu_custom_call" | custom-call | flops 1073741824 | bytes 8388608 | tf_op jit(solution)/shard_map/pallas_call | solution.py:464
  65.7 3.2 %shard_map.97 = (bf16[8,128,512]{2,1,0:T(8,128)(2,1)S(1)}, bf16[128,512]{1,0:T(8,128)(2,1)S(1)}, bf16[128,512]{1,0:T(8,128)(2,1)S(1)}, bf16[128,512]{1,0:T(8,128...) custom-call(bf16[8,128,1024]{2,1,0:T(8,128)(2,1)S(1)} %shard_map.95., ...), custom_call_target="tpu_custom_call" | custom-call | flops 536870912 | bytes 4194304 | tf_op jit(solution)/shard_map/pallas_call | solution.py:485
  68.9 1.9 %collective-permute-start.19 = (bf16[128,512]{1,0:T(8,128)(2,1)S(1)}, bf16[128,512]{1,0:T(8,128)(2,1)S(1)}, u32[]{:S(2)}, u32[]{:S(2)}) collective-permute-start(bf16[128,512]{1,0:T(8,128)(2,1)S(1)} %get-tuple-element.89), channel_id=1, source_target_pairs={{0,2},{4,0},{8,4},{12,8},{14,12},{10,14},{6,10},{2,6},{1,3},{5,1},... | collective-permute-start | bytes 393224 | tf_op jit(solution)/shard_map/ppermute | solution.py:93
  70.9 3.2 %shard_map.98 = (bf16[128,512]{1,0:T(8,128)(2,1)S(1)}, bf16[128,512]{1,0:T(8,128)(2,1)S(1)}, bf16[128,512]{1,0:T(8,128)(2,1)S(1)}, bf16[128,512]{1,0:T(8,128)(2,...) custom-call(bf16[8,128,512]{2,1,0:T(8,128)(2,1)S(1)} %get-tuple-elem, ...), custom_call_target="tpu_custom_call" | custom-call | flops 536870912 | bytes 4194304 | tf_op jit(solution)/shard_map/pallas_call | solution.py:485
  74.1 1.9 %collective-permute-start.26 = (bf16[128,512]{1,0:T(8,128)(2,1)S(1)}, bf16[128,512]{1,0:T(8,128)(2,1)S(1)}, u32[]{:S(2)}, u32[]{:S(2)}) collective-permute-start(bf16[128,512]{1,0:T(8,128)(2,1)S(1)} %get-tuple-element.98), channel_id=1, source_target_pairs={{0,2},{4,0},{8,4},{12,8},{14,12},{10,14},{6,10},{2,6},{1,3},{5,1},... | collective-permute-start | bytes 393224 | tf_op jit(solution)/shard_map/ppermute | solution.py:93
  76.2 1.9 %collective-permute-start.20 = (bf16[128,512]{1,0:T(8,128)(2,1)S(1)}, bf16[128,512]{1,0:T(8,128)(2,1)S(1)}, u32[]{:S(2)}, u32[]{:S(2)}) collective-permute-start(bf16[128,512]{1,0:T(8,128)(2,1)S(1)} %add_convert_fusion.11), channel_id=1, source_target_pairs={{0,2},{4,0},{8,4},{12,8},{14,12},{10,14},{6,10},{2,6},{1,3},{5,1},... | collective-permute-start | bytes 393224 | tf_op jit(solution)/shard_map/ppermute | solution.py:93
  78.4 1.8 %collective-permute-done.26 = bf16[128,512]{1,0:T(8,128)(2,1)S(1)} collective-permute-done((bf16[128,512]{1,0:T(8,128)(2,1)S(1)}, bf16[128,512]{1,0:T(8,128)(2,1)S(1)}, u32[]{:S(2)}, u32[]{:S(2)}) %collective-permute-start.26) | collective-permute-done | bytes 131104 | tf_op jit(solution)/shard_map/ppermute | solution.py:93
  80.2 2.2 %collective-permute-start.27 = (bf16[128,512]{1,0:T(8,128)(2,1)S(1)}, bf16[128,512]{1,0:T(8,128)(2,1)S(1)}, u32[]{:S(2)}, u32[]{:S(2)}) collective-permute-start(bf16[128,512]{1,0:T(8,128)(2,1)S(1)} %add_convert_fusion.5), channel_id=1, source_target_pairs={{0,2},{4,0},{8,4},{12,8},{14,12},{10,14},{6,10},{2,6},{1,3},{5,1},... | collective-permute-start | bytes 393224 | tf_op jit(solution)/shard_map/ppermute | solution.py:93
  82.6 0.5 collective-permute-done.20
  83.0 2.2 %collective-permute-start.21 = (bf16[128,512]{1,0:T(8,128)(2,1)S(1)}, bf16[128,512]{1,0:T(8,128)(2,1)S(1)}, u32[]{:S(2)}, u32[]{:S(2)}) collective-permute-start(bf16[128,512]{1,0:T(8,128)(2,1)S(1)} %add_convert_fusion.10), channel_id=1, source_target_pairs={{0,2},{4,0},{8,4},{12,8},{14,12},{10,14},{6,10},{2,6},{1,3},{5,1},... | collective-permute-start | bytes 393224 | tf_op jit(solution)/shard_map/ppermute | solution.py:93
  85.4 1.3 %collective-permute-done.27 = bf16[128,512]{1,0:T(8,128)(2,1)S(1)} collective-permute-done((bf16[128,512]{1,0:T(8,128)(2,1)S(1)}, bf16[128,512]{1,0:T(8,128)(2,1)S(1)}, u32[]{:S(2)}, u32[]{:S(2)}) %collective-permute-start.27) | collective-permute-done | bytes 131104 | tf_op jit(solution)/shard_map/ppermute | solution.py:93
  86.7 1.8 %collective-permute-start.28 = (bf16[128,512]{1,0:T(8,128)(2,1)S(1)}, bf16[128,512]{1,0:T(8,128)(2,1)S(1)}, u32[]{:S(2)}, u32[]{:S(2)}) collective-permute-start(bf16[128,512]{1,0:T(8,128)(2,1)S(1)} %add_convert_fusion.4), channel_id=1, source_target_pairs={{0,2},{4,0},{8,4},{12,8},{14,12},{10,14},{6,10},{2,6},{1,3},{5,1},... | collective-permute-start | bytes 393224 | tf_op jit(solution)/shard_map/ppermute | solution.py:93
  88.5 0.4 collective-permute-start.31
  88.9 0.5 collective-permute-done.21
  89.4 2.1 %collective-permute-start.22 = (bf16[128,512]{1,0:T(8,128)(2,1)S(1)}, bf16[128,512]{1,0:T(8,128)(2,1)S(1)}, u32[]{:S(2)}, u32[]{:S(2)}) collective-permute-start(bf16[128,512]{1,0:T(8,128)(2,1)S(1)} %add_convert_fusion.9), channel_id=1, source_target_pairs={{0,2},{4,0},{8,4},{12,8},{14,12},{10,14},{6,10},{2,6},{1,3},{5,1},... | collective-permute-start | bytes 393224 | tf_op jit(solution)/shard_map/ppermute | solution.py:93
  91.6 2.6 %collective-permute-done.31 = bf16[128,512]{1,0:T(8,128)(2,1)S(1)} collective-permute-done((bf16[128,512]{1,0:T(8,128)(2,1)S(1)}, bf16[128,512]{1,0:T(8,128)(2,1)S(1)}, u32[]{:S(2)}, u32[]{:S(2)}) %collective-permute-start.31) | collective-permute-done | bytes 131104 | tf_op jit(solution)/shard_map/ppermute | solution.py:89
  94.5 4.7 %collective-permute-done.32 = bf16[128,512]{1,0:T(8,128)(2,1)S(1)} collective-permute-done((bf16[128,512]{1,0:T(8,128)(2,1)S(1)}, bf16[128,512]{1,0:T(8,128)(2,1)S(1)}, u32[]{:S(2)}, u32[]{:S(2)}) %collective-permute-start.32) | collective-permute-done | bytes 131104 | tf_op jit(solution)/shard_map/ppermute | solution.py:89
  99.3 0.7 pad_maximum_fusion.2
  (54 shorter events, 2.7 us)
Async XLA Ops:
  1.0 10.5 %collective-permute-start.4 = (bf16[64,1024]{1,0:T(8,128)(2,1)S(1)}, bf16[64,1024]{1,0:T(8,128)(2,1)S(1)}, u32[]{:S(2)}, u32[]{:S(2)}) collective-permute-start(bf16[64,1024]{1,0:T(8,128)(2,1)S(1)} %slice_select_fusion), channel_id=1, source_target_pairs={{0,2},{4,0},{8,4},{12,8},{14,12},{10,14},{6,10},{2,6},{1,3},{5,1},... | collective-permute-start | bytes 393224 | tf_op jit(solution)/shard_map/ppermute | solution.py:93
  4.0 9.4 %collective-permute-start.2 = (bf16[64,1024]{1,0:T(8,128)(2,1)S(1)}, bf16[64,1024]{1,0:T(8,128)(2,1)S(1)}, u32[]{:S(2)}, u32[]{:S(2)}) collective-permute-start(bf16[64,1024]{1,0:T(8,128)(2,1)S(1)} %slice_select_fusion), channel_id=1, source_target_pairs={{0,4},{4,8},{8,12},{12,14},{14,10},{10,6},{6,2},{2,0},{1,5},{5,9},... | collective-permute-start | bytes 393224 | tf_op jit(solution)/shard_map/ppermute | solution.py:89
  9.4 12.6 %collective-permute-start.1 = (bf16[144,1024]{1,0:T(8,128)(2,1)S(1)}, bf16[144,1024]{1,0:T(8,128)(2,1)S(1)}, u32[]{:S(2)}, u32[]{:S(2)}) collective-permute-start(bf16[144,1024]{1,0:T(8,128)(2,1)S(1)} %fusion.32.refs_0_), channel_id=1, source_target_pairs={{0,2},{4,0},{8,4},{12,8},{14,12},{10,14},{6,10},{2,6},{1,3},{5,1},... | collective-permute-start | bytes 884744 | tf_op jit(solution)/shard_map/ppermute | solution.py:93
  11.3 10.7 %collective-permute-start = (bf16[144,1024]{1,0:T(8,128)(2,1)S(1)}, bf16[144,1024]{1,0:T(8,128)(2,1)S(1)}, u32[]{:S(2)}, u32[]{:S(2)}) collective-permute-start(bf16[144,1024]{1,0:T(8,128)(2,1)S(1)} %fusion.32.refs_0_), channel_id=1, source_target_pairs={{0,4},{4,8},{8,12},{12,14},{14,10},{10,6},{6,2},{2,0},{1,5},{5,9},... | collective-permute-start | bytes 884744 | tf_op jit(solution)/shard_map/ppermute | solution.py:89
  11.5 9.2 %collective-permute-start.5 = (bf16[64,1024]{1,0:T(8,128)(2,1)S(1)}, bf16[64,1024]{1,0:T(8,128)(2,1)S(1)}, u32[]{:S(2)}, u32[]{:S(2)}) collective-permute-start(bf16[64,1024]{1,0:T(8,128)(2,1)S(1)} %collective-permute-done.4.refs_15_), channel_id=1, source_target_pairs={{0,2},{4,0},{8,4},{12,8},{14,12},{10,14},{6,10},{2,6},{1,3},{5,1},... | collective-permute-start | bytes 393224 | tf_op jit(solution)/shard_map/ppermute | solution.py:93
  13.3 8.7 %collective-permute-start.3 = (bf16[64,1024]{1,0:T(8,128)(2,1)S(1)}, bf16[64,1024]{1,0:T(8,128)(2,1)S(1)}, u32[]{:S(2)}, u32[]{:S(2)}) collective-permute-start(bf16[64,1024]{1,0:T(8,128)(2,1)S(1)} %collective-permute-done.2.refs_9_), channel_id=1, source_target_pairs={{0,4},{4,8},{8,12},{12,14},{14,10},{10,6},{6,2},{2,0},{1,5},{5,9},... | collective-permute-start | bytes 393224 | tf_op jit(solution)/shard_map/ppermute | solution.py:89
  22.0 10.2 %collective-permute-start.8 = (bf16[64,1024]{1,0:T(8,128)(2,1)S(1)}, bf16[64,1024]{1,0:T(8,128)(2,1)S(1)}, u32[]{:S(2)}, u32[]{:S(2)}) collective-permute-start(bf16[64,1024]{1,0:T(8,128)(2,1)S(1)} %collective-permute-done.3.refs_10_), channel_id=1, source_target_pairs={{0,4},{4,8},{8,12},{12,14},{14,10},{10,6},{6,2},{2,0},{1,5},{5,9},... | collective-permute-start | bytes 393224 | tf_op jit(solution)/shard_map/ppermute | solution.py:89
  22.5 9.8 %collective-permute-start.9 = (bf16[64,1024]{1,0:T(8,128)(2,1)S(1)}, bf16[64,1024]{1,0:T(8,128)(2,1)S(1)}, u32[]{:S(2)}, u32[]{:S(2)}) collective-permute-start(bf16[64,1024]{1,0:T(8,128)(2,1)S(1)} %collective-permute-done.5.refs_14_), channel_id=1, source_target_pairs={{0,2},{4,0},{8,4},{12,8},{14,12},{10,14},{6,10},{2,6},{1,3},{5,1},... | collective-permute-start | bytes 393224 | tf_op jit(solution)/shard_map/ppermute | solution.py:93
  24.1 8.2 %collective-permute-start.6 = (bf16[144,1024]{1,0:T(8,128)(2,1)S(1)}, bf16[144,1024]{1,0:T(8,128)(2,1)S(1)}, u32[]{:S(2)}, u32[]{:S(2)}) collective-permute-start(bf16[144,1024]{1,0:T(8,128)(2,1)S(1)} %collective-permute-done.refs_1_), channel_id=1, source_target_pairs={{0,4},{4,8},{8,12},{12,14},{14,10},{10,6},{6,2},{2,0},{1,5},{5,9},... | collective-permute-start | bytes 884744 | tf_op jit(solution)/shard_map/ppermute | solution.py:89
  24.5 7.8 %collective-permute-start.7 = (bf16[144,1024]{1,0:T(8,128)(2,1)S(1)}, bf16[144,1024]{1,0:T(8,128)(2,1)S(1)}, u32[]{:S(2)}, u32[]{:S(2)}) collective-permute-start(bf16[144,1024]{1,0:T(8,128)(2,1)S(1)} %collective-permute-done.1.refs_7_), channel_id=1, source_target_pairs={{0,2},{4,0},{8,4},{12,8},{14,12},{10,14},{6,10},{2,6},{1,3},{5,1},... | collective-permute-start | bytes 884744 | tf_op jit(solution)/shard_map/ppermute | solution.py:93
  26.1 16.3 %collective-permute-start.13 = (bf16[256,1024]{1,0:T(8,128)(2,1)S(1)}, bf16[256,1024]{1,0:T(8,128)(2,1)S(1)}, u32[]{:S(2)}, u32[]{:S(2)}) collective-permute-start(bf16[256,1024]{1,0:T(8,128)(2,1)S(1)} %pad_maximum_fusion), channel_id=1, source_target_pairs={{0,16},{16,0},{1,17},{17,1},{2,18},{18,2},{3,19},{19,3},{4,20},{20... | collective-permute-start | bytes 1572872 | tf_op jit(solution)/shard_map/ppermute | solution.py:97
  32.3 10.3 %collective-permute-start.10 = (bf16[144,1024]{1,0:T(8,128)(2,1)S(1)}, bf16[144,1024]{1,0:T(8,128)(2,1)S(1)}, u32[]{:S(2)}, u32[]{:S(2)}) collective-permute-start(bf16[144,1024]{1,0:T(8,128)(2,1)S(1)} %collective-permute-done.6.refs_2_), channel_id=1, source_target_pairs={{0,4},{4,8},{8,12},{12,14},{14,10},{10,6},{6,2},{2,0},{1,5},{5,9},... | collective-permute-start | bytes 884744 | tf_op jit(solution)/shard_map/ppermute | solution.py:89
  33.9 8.7 %collective-permute-start.11 = (bf16[144,1024]{1,0:T(8,128)(2,1)S(1)}, bf16[144,1024]{1,0:T(8,128)(2,1)S(1)}, u32[]{:S(2)}, u32[]{:S(2)}) collective-permute-start(bf16[144,1024]{1,0:T(8,128)(2,1)S(1)} %collective-permute-done.7.refs_6_), channel_id=1, source_target_pairs={{0,2},{4,0},{8,4},{12,8},{14,12},{10,14},{6,10},{2,6},{1,3},{5,1},... | collective-permute-start | bytes 884744 | tf_op jit(solution)/shard_map/ppermute | solution.py:93
  34.4 14.9 %copy-start = (bf16[128,1024]{1,0:T(8,128)(2,1)S(1)}, bf16[128,1024]{1,0:T(8,128)(2,1)}, u32[]{:S(2)}) copy-start(bf16[128,1024]{1,0:T(8,128)(2,1)} %refs_8_.1) | copy-start | bytes 786436
  34.4 8.2 %collective-permute-start.14 = (bf16[128,1024]{1,0:T(8,128)(2,1)S(1)}, bf16[128,1024]{1,0:T(8,128)(2,1)S(1)}, u32[]{:S(2)}, u32[]{:S(2)}) collective-permute-start(bf16[128,1024]{1,0:T(8,128)(2,1)S(1)} %pad_maximum_fusion.1), channel_id=1, source_target_pairs={{0,16},{16,0},{1,17},{17,1},{2,18},{18,2},{3,19},{19,3},{4,20},{20... | collective-permute-start | bytes 786440 | tf_op jit(solution)/shard_map/ppermute | solution.py:97
  36.0 6.5 %collective-permute-start.12 = (bf16[64,1024]{1,0:T(8,128)(2,1)S(1)}, bf16[64,1024]{1,0:T(8,128)(2,1)S(1)}, u32[]{:S(2)}, u32[]{:S(2)}) collective-permute-start(bf16[64,1024]{1,0:T(8,128)(2,1)S(1)} %collective-permute-done.9.refs_13_), channel_id=1, source_target_pairs={{0,2},{4,0},{8,4},{12,8},{14,12},{10,14},{6,10},{2,6},{1,3},{5,1},... | collective-permute-start | bytes 393224 | tf_op jit(solution)/shard_map/ppermute | solution.py:93
  42.6 6.7 %collective-permute-start.15 = (bf16[144,1024]{1,0:T(8,128)(2,1)S(1)}, bf16[144,1024]{1,0:T(8,128)(2,1)S(1)}, u32[]{:S(2)}, u32[]{:S(2)}) collective-permute-start(bf16[144,1024]{1,0:T(8,128)(2,1)S(1)} %collective-permute-done.10.refs_3_), channel_id=1, source_target_pairs={{0,4},{4,8},{8,12},{12,14},{14,10},{10,6},{6,2},{2,0},{1,5},{5,9},... | collective-permute-start | bytes 884744 | tf_op jit(solution)/shard_map/ppermute | solution.py:89
  44.1 5.0 %collective-permute-start.16 = (bf16[64,1024]{1,0:T(8,128)(2,1)S(1)}, bf16[64,1024]{1,0:T(8,128)(2,1)S(1)}, u32[]{:S(2)}, u32[]{:S(2)}) collective-permute-start(bf16[64,1024]{1,0:T(8,128)(2,1)S(1)} %collective-permute-done.12.refs_12_), channel_id=1, source_target_pairs={{0,16},{16,0},{1,17},{17,1},{2,18},{18,2},{3,19},{19,3},{4,20},{20... | collective-permute-start | bytes 393224 | tf_op jit(solution)/shard_map/ppermute | solution.py:97
  54.6 6.3 %collective-permute-start.17 = (bf16[8,128,1024]{2,1,0:T(8,128)(2,1)S(1)}, bf16[8,128,1024]{2,1,0:T(8,128)(2,1)S(1)}, u32[]{:S(2)}, u32[]{:S(2)}) collective-permute-start(bf16[8,128,1024]{2,1,0:T(8,128)(2,1)S(1)} %get-tuple-element.82.own), channel_id=1, source_target_pairs={{0,1},{1,0},{2,3},{3,2},{4,5},{5,4},{6,7},{7,6},{8,9},{9,8},{10,11... | collective-permute-start | bytes 6291464 | tf_op jit(solution)/shard_map/ppermute | solution.py:97
  60.9 4.8 %collective-permute-start.18 = (bf16[8,128,1024]{2,1,0:T(8,128)(2,1)S(1)}, bf16[8,128,1024]{2,1,0:T(8,128)(2,1)S(1)}, u32[]{:S(2)}, u32[]{:S(2)}) collective-permute-start(bf16[8,128,1024]{2,1,0:T(8,128)(2,1)S(1)} %shard_map.95.refs_0_), channel_id=1, source_target_pairs={{0,1},{1,0},{2,3},{3,2},{4,5},{5,4},{6,7},{7,6},{8,9},{9,8},{10,11... | collective-permute-start | bytes 6291464 | tf_op jit(solution)/shard_map/ppermute | solution.py:97
  68.9 7.3 %collective-permute-start.19 = (bf16[128,512]{1,0:T(8,128)(2,1)S(1)}, bf16[128,512]{1,0:T(8,128)(2,1)S(1)}, u32[]{:S(2)}, u32[]{:S(2)}) collective-permute-start(bf16[128,512]{1,0:T(8,128)(2,1)S(1)} %get-tuple-element.89), channel_id=1, source_target_pairs={{0,2},{4,0},{8,4},{12,8},{14,12},{10,14},{6,10},{2,6},{1,3},{5,1},... | collective-permute-start | bytes 393224 | tf_op jit(solution)/shard_map/ppermute | solution.py:93
  70.7 7.4 %collective-permute-start.23 = (bf16[128,512]{1,0:T(8,128)(2,1)S(1)}, bf16[128,512]{1,0:T(8,128)(2,1)S(1)}, u32[]{:S(2)}, u32[]{:S(2)}) collective-permute-start(bf16[128,512]{1,0:T(8,128)(2,1)S(1)} %get-tuple-element.93), channel_id=1, source_target_pairs={{0,4},{4,8},{8,12},{12,14},{14,10},{10,6},{6,2},{2,0},{1,5},{5,9},... | collective-permute-start | bytes 393224 | tf_op jit(solution)/shard_map/ppermute | solution.py:89
  74.1 6.1 %collective-permute-start.26 = (bf16[128,512]{1,0:T(8,128)(2,1)S(1)}, bf16[128,512]{1,0:T(8,128)(2,1)S(1)}, u32[]{:S(2)}, u32[]{:S(2)}) collective-permute-start(bf16[128,512]{1,0:T(8,128)(2,1)S(1)} %get-tuple-element.98), channel_id=1, source_target_pairs={{0,2},{4,0},{8,4},{12,8},{14,12},{10,14},{6,10},{2,6},{1,3},{5,1},... | collective-permute-start | bytes 393224 | tf_op jit(solution)/shard_map/ppermute | solution.py:93
  76.0 6.5 %collective-permute-start.29 = (bf16[128,512]{1,0:T(8,128)(2,1)S(1)}, bf16[128,512]{1,0:T(8,128)(2,1)S(1)}, u32[]{:S(2)}, u32[]{:S(2)}) collective-permute-start(bf16[128,512]{1,0:T(8,128)(2,1)S(1)} %get-tuple-element.101), channel_id=1, source_target_pairs={{0,4},{4,8},{8,12},{12,14},{14,10},{10,6},{6,2},{2,0},{1,5},{5,9},... | collective-permute-start | bytes 393224 | tf_op jit(solution)/shard_map/ppermute | solution.py:89
  76.2 6.8 %collective-permute-start.20 = (bf16[128,512]{1,0:T(8,128)(2,1)S(1)}, bf16[128,512]{1,0:T(8,128)(2,1)S(1)}, u32[]{:S(2)}, u32[]{:S(2)}) collective-permute-start(bf16[128,512]{1,0:T(8,128)(2,1)S(1)} %add_convert_fusion.11), channel_id=1, source_target_pairs={{0,2},{4,0},{8,4},{12,8},{14,12},{10,14},{6,10},{2,6},{1,3},{5,1},... | collective-permute-start | bytes 393224 | tf_op jit(solution)/shard_map/ppermute | solution.py:93
  78.2 7.1 %collective-permute-start.24 = (bf16[128,512]{1,0:T(8,128)(2,1)S(1)}, bf16[128,512]{1,0:T(8,128)(2,1)S(1)}, u32[]{:S(2)}, u32[]{:S(2)}) collective-permute-start(bf16[128,512]{1,0:T(8,128)(2,1)S(1)} %add_convert_fusion.8), channel_id=1, source_target_pairs={{0,4},{4,8},{8,12},{12,14},{14,10},{10,6},{6,2},{2,0},{1,5},{5,9},... | collective-permute-start | bytes 393224 | tf_op jit(solution)/shard_map/ppermute | solution.py:89
  80.2 6.4 %collective-permute-start.27 = (bf16[128,512]{1,0:T(8,128)(2,1)S(1)}, bf16[128,512]{1,0:T(8,128)(2,1)S(1)}, u32[]{:S(2)}, u32[]{:S(2)}) collective-permute-start(bf16[128,512]{1,0:T(8,128)(2,1)S(1)} %add_convert_fusion.5), channel_id=1, source_target_pairs={{0,2},{4,0},{8,4},{12,8},{14,12},{10,14},{6,10},{2,6},{1,3},{5,1},... | collective-permute-start | bytes 393224 | tf_op jit(solution)/shard_map/ppermute | solution.py:93
  82.5 6.0 %collective-permute-start.30 = (bf16[128,512]{1,0:T(8,128)(2,1)S(1)}, bf16[128,512]{1,0:T(8,128)(2,1)S(1)}, u32[]{:S(2)}, u32[]{:S(2)}) collective-permute-start(bf16[128,512]{1,0:T(8,128)(2,1)S(1)} %add_convert_fusion.3), channel_id=1, source_target_pairs={{0,4},{4,8},{8,12},{12,14},{14,10},{10,6},{6,2},{2,0},{1,5},{5,9},... | collective-permute-start | bytes 393224 | tf_op jit(solution)/shard_map/ppermute | solution.py:89
  83.0 6.4 %collective-permute-start.21 = (bf16[128,512]{1,0:T(8,128)(2,1)S(1)}, bf16[128,512]{1,0:T(8,128)(2,1)S(1)}, u32[]{:S(2)}, u32[]{:S(2)}) collective-permute-start(bf16[128,512]{1,0:T(8,128)(2,1)S(1)} %add_convert_fusion.10), channel_id=1, source_target_pairs={{0,2},{4,0},{8,4},{12,8},{14,12},{10,14},{6,10},{2,6},{1,3},{5,1},... | collective-permute-start | bytes 393224 | tf_op jit(solution)/shard_map/ppermute | solution.py:93
  85.3 9.0 %collective-permute-start.25 = (bf16[128,512]{1,0:T(8,128)(2,1)S(1)}, bf16[128,512]{1,0:T(8,128)(2,1)S(1)}, u32[]{:S(2)}, u32[]{:S(2)}) collective-permute-start(bf16[128,512]{1,0:T(8,128)(2,1)S(1)} %add_convert_fusion.7), channel_id=1, source_target_pairs={{0,4},{4,8},{8,12},{12,14},{14,10},{10,6},{6,2},{2,0},{1,5},{5,9},... | collective-permute-start | bytes 393224 | tf_op jit(solution)/shard_map/ppermute | solution.py:89
  86.7 7.8 %collective-permute-start.28 = (bf16[128,512]{1,0:T(8,128)(2,1)S(1)}, bf16[128,512]{1,0:T(8,128)(2,1)S(1)}, u32[]{:S(2)}, u32[]{:S(2)}) collective-permute-start(bf16[128,512]{1,0:T(8,128)(2,1)S(1)} %add_convert_fusion.4), channel_id=1, source_target_pairs={{0,2},{4,0},{8,4},{12,8},{14,12},{10,14},{6,10},{2,6},{1,3},{5,1},... | collective-permute-start | bytes 393224 | tf_op jit(solution)/shard_map/ppermute | solution.py:93
  88.5 5.7 %collective-permute-start.31 = (bf16[128,512]{1,0:T(8,128)(2,1)S(1)}, bf16[128,512]{1,0:T(8,128)(2,1)S(1)}, u32[]{:S(2)}, u32[]{:S(2)}) collective-permute-start(bf16[128,512]{1,0:T(8,128)(2,1)S(1)} %add_convert_fusion.2), channel_id=1, source_target_pairs={{0,4},{4,8},{8,12},{12,14},{14,10},{10,6},{6,2},{2,0},{1,5},{5,9},... | collective-permute-start | bytes 393224 | tf_op jit(solution)/shard_map/ppermute | solution.py:89
  89.4 5.0 %collective-permute-start.22 = (bf16[128,512]{1,0:T(8,128)(2,1)S(1)}, bf16[128,512]{1,0:T(8,128)(2,1)S(1)}, u32[]{:S(2)}, u32[]{:S(2)}) collective-permute-start(bf16[128,512]{1,0:T(8,128)(2,1)S(1)} %add_convert_fusion.9), channel_id=1, source_target_pairs={{0,2},{4,0},{8,4},{12,8},{14,12},{10,14},{6,10},{2,6},{1,3},{5,1},... | collective-permute-start | bytes 393224 | tf_op jit(solution)/shard_map/ppermute | solution.py:93
  94.2 5.0 %collective-permute-start.32 = (bf16[128,512]{1,0:T(8,128)(2,1)S(1)}, bf16[128,512]{1,0:T(8,128)(2,1)S(1)}, u32[]{:S(2)}, u32[]{:S(2)}) collective-permute-start(bf16[128,512]{1,0:T(8,128)(2,1)S(1)} %add_convert_fusion.1), channel_id=1, source_target_pairs={{0,4},{4,8},{8,12},{12,14},{14,10},{10,6},{6,2},{2,0},{1,5},{5,9},... | collective-permute-start | bytes 393224 | tf_op jit(solution)/shard_map/ppermute | solution.py:89
